TPU v7x, 256 devices: a whole 4x4x8 slice. The times are simulated.
256 devices in a mesh: dp: 32 (over x, y, core), tensor: 8 (over z).
Axes of the slice: x: 4, y: 4, z: 8, core: 2. Of those that a mesh axis runs over, the one named last changes fastest.
Arguments:
- grad_out: bfloat16 [32768, 4608], P(('dp', 'tensor')), may hold values from -6 to 6
- attn_out: bfloat16 [32768, 2048], P('dp', 'tensor'), may hold values from -0.119628906 to 0.119628906
- out_weight: bfloat16 [2048, 4608], P('tensor'), may hold values from -0.09375 to 0.09375
- error_prev: bfloat16 [32, 2048, 4608], P('dp', 'tensor'), may hold values from -3 to 3
- q_prev: float32 [4608, 64], replicated, may hold values from -0.09375 to 0.09375
Outputs:
- grad_attn: bfloat16 [32768, 2048], P('dp', 'tensor')
- p_factor: float32 [2048, 64], P('tensor')
- q_factor: float32 [4608, 64], replicated
- error_new: bfloat16 [32, 2048, 4608], P('dp', 'tensor')
All inputs are finite; a program needn't handle non-finite values.
Results may differ from a plain program's by a relative error of at most 0.014.
Values may be sent and summed in bfloat16 or wider, within the bound.
No kernel may reach another device: no remote copies, remote signals or barrier semaphores. Data moves between devices by JAX's collectives and lax.ppermute only.
A program may use at most 128 MiB of HBM per device.

v0:
```python
import jax
import jax.numpy as jnp
from jax import lax
from jax.sharding import PartitionSpec as P


def on_device(grad_out, attn_out, out_weight, error_prev, q_prev):
    row_block = lax.all_gather(grad_out, "tensor", axis=0, tiled=True)
    weight_sum = lax.dot_general(
        attn_out, row_block, (((0,), (0,)), ((), ())), preferred_element_type=jnp.float32
    )
    fresh = lax.dot_general(
        row_block, out_weight, (((1,), (1,)), ((), ())), preferred_element_type=jnp.float32
    )
    grad_rows = fresh
    weight_sum, grad_rows = (weight_sum, grad_rows)
    merged = weight_sum + error_prev[0].astype(jnp.float32)
    p_local = jnp.dot(merged, q_prev, precision=lax.Precision.HIGHEST)
    p_summed = lax.psum(p_local, "dp")
    gram_part = jnp.dot(p_summed.T, p_summed, precision=lax.Precision.HIGHEST)
    gram_matrix = lax.psum(gram_part, "tensor")
    lower_factor = jnp.linalg.cholesky(gram_matrix)
    p_factor = jax.scipy.linalg.solve_triangular(lower_factor, p_summed.T, lower=True).T
    q_term = lax.dot_general(
        merged, p_factor, (((0,), (0,)), ((), ())), precision=lax.Precision.HIGHEST
    )
    q_total = lax.psum(q_term, ("dp", "tensor"))
    q_factor = q_total / lax.axis_size("dp")
    approx = jnp.dot(p_factor, q_factor.T, precision=lax.Precision.HIGHEST)
    error_new = (merged - approx).astype(jnp.bfloat16)[None]
    return (grad_rows.astype(jnp.bfloat16), p_factor, q_factor, error_new)


def solution(mesh):
    in_specs = (
        P(("dp", "tensor"), None),
        P("dp", "tensor"),
        P("tensor", None),
        P("dp", "tensor", None),
        P(),
    )
    out_specs = (P("dp", "tensor"), P("tensor", None), P(), P("dp", "tensor", None))
    return jax.shard_map(
        on_device, mesh=mesh, in_specs=in_specs, out_specs=out_specs, check_vma=False
    )
```

profile of v0, /device:TPU:1, one launch (start us, length us, event | category | flops | bytes accessed | tf_op | source)
XLA Modules:
  0.0 555.3 jit_solution(9946124947982423570)
XLA Ops:
  7.2 0.0 all-gather.2.cloned.1.call-start
  7.2 0.7 all-gather.2.cloned.1.call-update
  7.9 0.0 all-reduce.3.cloned.1.call-start
  8.0 109.6 %all-gather.2.cloned.1.call-done = bf16[1024,4608]{1,0:T(8,128)(2,1)} async-done(((bf16[128,4608]{1,0:T(8,128)(2,1)}), bf16[1024,4608]{1,0:T(8,128)(2,1)}) %all-gather.2.cloned.1.call-update) | async-done | bytes 9437200 | tf_op jit(solution)/shard_map/all_gather | solution.py:8
  117.6 7.3 %convolution_add_fusion = f32[256,4608]{1,0:T(8,128)S(1)} fusion(bf16[1024,256]{1,0:T(8,128)(2,1)} %param.6, bf16[1024,4608]{1,0:T(8,128)(2,1)} %all-gather.2.cloned.1.call-done, bf16[1,256,4608]{2,1,0:T(8,128)(2,1)} %param.8), kind=kOutput, calls=%fused_computation.1 | convolution fusion | flops 2418278400 | bytes 17039360 | tf_op jit(solution)/shard_map/dot_general | solution.py:9
  125.0 2.2 copy-done.1
  127.2 5.0 fusion.6
  132.2 0.0 all-reduce.3.cloned.1.call-update
  132.2 0.0 all-reduce.5.cloned.1.call-start
  132.3 104.7 %all-reduce.3.cloned.1.call-done = f32[256,64]{0,1:T(8,128)} async-done(((f32[256,64]{0,1:T(8,128)}), f32[256,64]{0,1:T(8,128)}) %all-reduce.3.cloned.1.call-update) | async-done | bytes 65552 | tf_op jit(solution)/shard_map/psum | solution.py:19
  237.0 1.1 fusion.7
  238.1 23.4 %psum.22 = f32[64,64]{0,1:T(8,128)S(1)} all-reduce(f32[64,64]{0,1:T(8,128)S(1)} %fusion.7), channel_id=1, replica_groups=mesh['dp'=32,'tensor'=8] {'tensor'}, use_global_device_ids=true, to_apply=%region_1.0 | all-reduce | flops 4096 | bytes 32768 | tf_op jit(solution)/shard_map/psum | solution.py:21
  261.6 0.1 copy.10
  261.7 5.8 %cholesky.16 = f32[64,64]{1,0:T(8,128)S(1)} custom-call(f32[64,64]{1,0:T(8,128)S(1)} %fusion.5), custom_call_target="Cholesky" | custom-call | tf_op jit(solution)/shard_map/jit(cholesky)/cholesky | solution.py:22
  267.5 0.6 compare_reduce_fusion
  268.2 0.7 fusion.2
  268.8 4.9 custom-call.7
  273.7 1.1 fusion.3
  274.9 6.5 %fusion.8 = f32[4608,64]{0,1:T(8,128)} fusion(f32[256,4608]{1,0:T(8,128)} %copy-done.1, f32[64,256]{1,0:T(8,128)S(1)} %fusion.3), kind=kOutput, calls=%fused_computation.18 | convolution fusion | flops 905969664 | bytes 5963776 | tf_op jit(solution)/shard_map/dot_general | solution.py:24
  281.4 0.0 all-reduce.5.cloned.1.call-update
  281.4 7.1 %convolution_convert_fusion = bf16[1024,256]{1,0:T(8,128)(2,1)} fusion(bf16[1024,4608]{1,0:T(8,128)(2,1)} %all-gather.2.cloned.1.call-done, bf16[256,4608]{1,0:T(8,128)(2,1)S(1)} %copy-done), kind=kOutput, calls=%fused_computation.4 | convolution fusion | flops 2416181248 | bytes 12320768 | tf_op jit(solution)/shard_map/dot_general | solution.py:12
  288.5 251.6 %all-reduce.5.cloned.1.call-done = f32[4608,64]{0,1:T(8,128)} async-done(((f32[4608,64]{0,1:T(8,128)}), f32[4608,64]{0,1:T(8,128)}) %all-reduce.5.cloned.1.call-update) | async-done | bytes 1179664 | tf_op jit(solution)/shard_map/psum | solution.py:27
  540.1 1.4 broadcast_multiply_fusion
  541.5 7.2 %fusion.1 = bf16[1,256,4608]{2,1,0:T(8,128)(2,1)} fusion(f32[256,4608]{1,0:T(8,128)} %copy-done.1, f32[64,256]{1,0:T(8,128)S(1)} %fusion.3, f32[4608,64]{0,1:T(8,128)S(1)} %broadcast_multiply_fusion), kind=kOutput, calls=%fused_computation.3 | convolution fusion | flops 908328960 | bytes 8323072 | tf_op jit(solution)/shard_map/dot_general | solution.py:29
  (11 shorter events, 0.1 us)
Async XLA Ops:
  7.2 274.2 %copy-start = (bf16[256,4608]{1,0:T(8,128)(2,1)S(1)}, bf16[256,4608]{1,0:T(8,128)(2,1)}, u32[]{:S(2)}) copy-start(bf16[256,4608]{1,0:T(8,128)(2,1)} %param.7) | copy-start | bytes 7077892
  7.2 110.4 %all-gather.2.cloned.1.call-start = ((), (), s32[]{:S(2)}) async-start(), calls=%async_computation | async-start | bytes 10616832 | tf_op jit(solution)/shard_map/all_gather | solution.py:8
  7.9 119.3 %copy-start.3 = (f32[4608,64]{0,1:T(8,128)S(1)}, f32[4608,64]{0,1:T(8,128)}, u32[]{:S(2)}) copy-start(f32[4608,64]{0,1:T(8,128)} %param.9) | copy-start | bytes 3538948
  7.9 229.1 %all-reduce.3.cloned.1.call-start = ((), (), s32[]{:S(2)}) async-start(), calls=%async_computation.1 | async-start | bytes 131072 | tf_op jit(solution)/shard_map/psum | solution.py:19
  124.9 2.2 copy-start.1
  132.2 407.9 %all-reduce.5.cloned.1.call-start = ((), (), s32[]{:S(2)}) async-start(), calls=%async_computation.2 | async-start | bytes 2359296 | tf_op jit(solution)/shard_map/psum | solution.py:27
  274.9 266.6 %copy-start.4 = (f32[64,256]{1,0:T(8,128)}, f32[64,256]{1,0:T(8,128)S(1)}, u32[]{:S(2)}) copy-start(f32[64,256]{1,0:T(8,128)S(1)} %fusion.3) | copy-start | bytes 196612
  541.5 7.2 %copy-start.2 = (f32[4608,64]{0,1:T(8,128)}, f32[4608,64]{0,1:T(8,128)S(1)}, u32[]{:S(2)}) copy-start(f32[4608,64]{0,1:T(8,128)S(1)} %broadcast_multiply_fusion) | copy-start | bytes 3538948
Sparse Core Ops, SparseCore 0:
  9.8 107.7 all-gather.1
  132.4 104.5 all-reduce.2
  281.5 258.5 all-reduce.4
where the time goes:
time: 558 us; the launch traced here: 555 us
  waiting for transfers between devices  467 us (84%)
  matrix products  35.4 us (6%)
  blocking collectives  23.4 us (4%)
  between operations  13.9 us (2%)
  other arithmetic  13.4 us (2%)
    psum x1, waiting for transfers between devices, on_device(): q_total = lax.psum(q_term, ('dp', 'tensor'))  252 us
    all_gather x1, waiting for transfers between devices, on_device(): row_block = lax.all_gather(grad_out, 'tensor', axis=0, tiled=True)  110 us
    psum x1, waiting for transfers between devices, on_device(): p_summed = lax.psum(p_local, 'dp')  105 us
    psum x1, blocking collectives, on_device(): gram_matrix = lax.psum(gram_part, 'tensor')  23.4 us
  transfers between devices with their start and end apart: 3, of which 3 were waited for; matrix products, arithmetic and copies ran while one was open for 1% of the time, Pallas kernels for 0%

commit v1 on v0

v1 whole, which is shorter than its diff:
```python
import functools

import jax
import jax.numpy as jnp
from jax import lax
from jax.experimental import pallas as pl
from jax.experimental.pallas import tpu as pltpu
from jax.sharding import Mesh
from jax.sharding import PartitionSpec as P

D, K, NZ, NXY = 4608, 64, 8, 16
TILE = 1152
HI = lax.Precision.HIGHEST


def split3(v, axis):
    hi = lax.reduce_precision(v, 8, 7)
    rest = v - hi
    mid = lax.reduce_precision(rest, 8, 7)
    low = rest - mid
    return jnp.concatenate([hi, mid, low], axis=axis).astype(jnp.bfloat16)


def fold3(v):
    n = v.shape[0] // 3
    return v[:n] + v[n : 2 * n] + v[2 * n :]


def dot(a, b, ca, cb):
    return lax.dot_general(a, b, (((ca,), (cb,)), ((), ())), preferred_element_type=jnp.float32)


def shift(v, axis, size, by):
    return lax.ppermute(v, axis, [(i, (i + by) % size) for i in range(size)])


def everyone(v, axis, n):
    return lax.all_to_all(jnp.broadcast_to(v[None], (n,) + v.shape), axis, 0, 0)


def after(v, *others):
    return lax.optimization_barrier((v,) + others)[0]


def final_kernel(z_ref, *refs):
    blocks = refs[:15]
    a_ref, e_ref, w_ref, pf_ref, qraw_ref, linv_ref = refs[15:21]
    err_ref, grad_ref, q_ref, acc_ref = refs[21:]
    step = pl.program_id(0)
    rows = jnp.concatenate([b[...] for b in blocks], axis=0)
    qf = jnp.dot(linv_ref[...], qraw_ref[...], precision=HI, preferred_element_type=jnp.float32)
    qf = qf * (1.0 / 32)
    q_ref[...] = qf.T
    pf = pf_ref[...]
    pf_hi = pf.astype(jnp.bfloat16)
    pf_lo = (pf - pf_hi.astype(jnp.float32)).astype(jnp.bfloat16)
    q_hi = qf.astype(jnp.bfloat16)
    q_lo = (qf - q_hi.astype(jnp.float32)).astype(jnp.bfloat16)
    low = dot(
        jnp.concatenate([pf_hi, pf_hi, pf_lo], axis=0),
        jnp.concatenate([q_hi, q_lo, q_hi], axis=0), 0, 0,
    )
    fresh = jnp.dot(a_ref[...], rows, preferred_element_type=jnp.float32)
    err_ref[0] = (fresh + e_ref[0].astype(jnp.float32) - low).astype(jnp.bfloat16)
    part = dot(rows, w_ref[...], 1, 1)

    @pl.when(step == 0)
    def _():
        acc_ref[...] = part

    @pl.when(step > 0)
    def _():
        acc_ref[...] += part

    @pl.when(step == pl.num_programs(0) - 1)
    def _():
        z = z_ref[0]
        for j in range(NZ):
            src = lax.rem(z + (NZ - j), NZ)
            grad_ref[pl.ds(pl.multiple_of(src * 128, 128), 128), :] = acc_ref[
                j * 128 : (j + 1) * 128, :
            ].astype(jnp.bfloat16)


def final(z, blocks, a_rel_t, error_prev, out_weight, pf_t, q_raw, linv):
    col = lambda rows: pl.BlockSpec((rows, TILE), lambda i: (0, i))
    whole = lambda shape: pl.BlockSpec(shape, lambda i: (0,) * len(shape))
    err_spec = pl.BlockSpec((1, 256, TILE), lambda i: (0, 0, i))
    return pl.pallas_call(
        final_kernel,
        grid=(D // TILE,),
        in_specs=[pl.BlockSpec(memory_space=pltpu.SMEM)]
        + [col(b.shape[0]) for b in blocks]
        + [whole((256, 1024)), err_spec, col(256), whole((K, 256)), col(K), whole((K, K))],
        out_specs=[err_spec, whole((1024, 256)), pl.BlockSpec((TILE, K), lambda i: (i, 0))],
        out_shape=[
            jax.ShapeDtypeStruct((1, 256, D), jnp.bfloat16),
            jax.ShapeDtypeStruct((1024, 256), jnp.bfloat16),
            jax.ShapeDtypeStruct((D, K), jnp.float32),
        ],
        scratch_shapes=[pltpu.VMEM((1024, 256), jnp.float32)],
        compiler_params=pltpu.CompilerParams(vmem_limit_bytes=40 * 1024 * 1024),
        cost_estimate=pl.CostEstimate(
            flops=4 * 256 * 1024 * D, bytes_accessed=18 * 1024 * 1024, transcendentals=0
        ),
    )(z, *blocks, a_rel_t, error_prev, out_weight, pf_t, q_raw, linv)


def on_device(grad_out, attn_out, out_weight, error_prev, q_prev):
    z = lax.axis_index("z")
    core = lax.axis_index("core")
    up = lambda v: shift(v, "z", NZ, 1)
    down = lambda v: shift(v, "z", NZ, NZ - 1)
    swap = lambda v: shift(v, "core", 2, 1)

    def halves(v):
        n = v.shape[0] // 2
        first = core == 0
        return jnp.where(first, v[:n], v[n:]), jnp.where(first, v[n:], v[:n])

    def rejoin(mine):
        other = swap(mine)
        first = core == 0
        return jnp.concatenate(
            [jnp.where(first, mine, other), jnp.where(first, other, mine)], axis=0
        )

    ga, gb = grad_out[:64], grad_out[64:]
    u1a, d1a = up(ga), down(ga)
    u1b, d1b = up(gb), down(gb)

    q3 = split3(q_prev, 1)
    y_t = fold3(dot(q3, grad_out, 0, 1))
    y_all = everyone(y_t, "z", NZ)
    eq_t = fold3(dot(q3, error_prev[0], 0, 1))
    y_all = after(y_all, u1a, d1a)
    u2a, d2a = up(u1a), down(d1a)
    y_cat = y_all.transpose(1, 0, 2).reshape(K, 1024)
    p_t = fold3(dot(split3(y_cat, 0), attn_out, 1, 0)) + eq_t
    mine, other = halves(p_t)
    mine = jnp.sum(everyone(mine + swap(other), ("x", "y"), NXY), axis=0)
    mine = after(mine, u1b, d1b)
    u2b, d2b = up(u1b), down(d1b)
    p_t = rejoin(mine)

    p3 = split3(p_t, 0)
    terms = fold3(dot(p3, attn_out, 1, 1)).reshape(K, NZ, 128).transpose(1, 0, 2)
    gram = lax.dot_general(p_t, p_t, (((1,), (1,)), ((), ())), precision=HI)
    packed = jnp.concatenate([gram[:32], gram[32:]], axis=1)
    sent = jnp.concatenate([terms, jnp.broadcast_to(packed[None], (NZ, 32, 128))], axis=1)
    got = jnp.sum(lax.all_to_all(sent, "z", 0, 0), axis=0)
    got = after(got, u2a, d2a)
    u3a, d3a = up(u2a), down(d2a)
    gram = jnp.concatenate([got[K:, :K], got[K:, K:]], axis=0)
    q_t = fold3(dot(p3, error_prev[0], 1, 0)) + fold3(dot(split3(got[:K], 0), grad_out, 1, 0))

    q_t = after(q_t, u2b, d2b)
    u3b, d3b = up(u2b), down(d2b)
    mine, other = halves(q_t)
    mine = (mine + swap(other)).reshape(NXY, 2, D)
    mine = jnp.sum(lax.all_to_all(mine, ("x", "y"), 0, 0), axis=0)
    mine = after(mine, u3a, d3a)
    ufar = up(u3a)
    mine = jnp.sum(everyone(mine, "z", NZ), axis=0)
    mine = after(mine, u3b, d3b)
    dfar = down(d3b)
    mine = everyone(mine, ("x", "y"), NXY).reshape(32, D)
    q_raw = rejoin(mine)

    lower = jnp.linalg.cholesky(gram)
    linv = jax.scipy.linalg.solve_triangular(lower, jnp.eye(K, dtype=jnp.float32), lower=True)
    pf_t = jnp.dot(linv, p_t, precision=HI)

    order = (z - jnp.arange(NZ)) % NZ
    a_rel_t = attn_out.reshape(NZ, 128, 256)[order].reshape(1024, 256).T
    blocks = [grad_out, u1a, u1b, u2a, u2b, u3a, u3b, ufar, dfar, d3a, d3b, d2a, d2b, d1a, d1b]
    error_new, grad_attn, q_factor = final(
        z.astype(jnp.int32).reshape(1), blocks, a_rel_t, error_prev, out_weight, pf_t, q_raw, linv
    )
    return grad_attn, pf_t.T, q_factor, error_new


def solution(mesh):
    fine = Mesh(mesh.devices.reshape(4, 4, 2, 8), ("x", "y", "core", "z"))
    dp = ("x", "y", "core")
    in_specs = (P(dp + ("z",), None), P(dp, "z"), P("z", None), P(dp, "z", None), P())
    out_specs = (P(dp, "z"), P("z", None), P(), P(dp, "z", None))
    return jax.shard_map(
        on_device, mesh=fine, in_specs=in_specs, out_specs=out_specs, check_vma=False
    )
```

time: 558 us -> 192 us (0.34)
  waiting for transfers between devices: 467 us -> 42.9 us
  starting transfers between devices: 0.12 us -> 55.7 us
  matrix products: 35.4 us -> 9.66 us
  local copies, waits for them, and re-layouts: 2.33 us -> 25.2 us
  other arithmetic: 13.4 us -> 26.8 us
  between operations: 13.9 us -> 1.03 us
  Pallas kernels: 0 us -> 11.8 us
  blocking collectives: 23.4 us -> 17 us
    psum x2 -> x0, waiting for transfers between devices: 356 us -> none  [the longest x1 252 us: on_device(): q_total = lax.psum(q_term, ('dp', 'tensor'))]
    all_gather x1 -> x0, waiting for transfers between devices: 110 us -> none  [on_device(): row_block = lax.all_gather(grad_out, 'tensor', axis=0, tiled=True)]
    ppermute x0 -> x18, starting transfers between devices: none -> 33.6 us  [shift(): return lax.ppermute(v, axis, [(i, (i + by) % size) for i in range(size)])]
    dot_general x6 -> x8, matrix products: 34.3 us -> 9.43 us  [the longest x6 9.03 us: dot(): lax.dot_general(a, b, (((ca,), (cb,)), ((), ())), preferred_element_type=...]
    all_to_all x0 -> x5, waiting for transfers between devices: none -> 24.9 us  [the longest x3 9.71 us: everyone(): return lax.all_to_all(jnp.broadcast_to(v[None], (n,) + v.shape), axis, 0, 0)]
    psum x1 -> x0, blocking collectives: 23.4 us -> none  [on_device(): gram_matrix = lax.psum(gram_part, 'tensor')]
    all_to_all x0 -> x5, starting transfers between devices: none -> 22.1 us  [the longest x3 13.8 us: everyone(): return lax.all_to_all(jnp.broadcast_to(v[None], (n,) + v.shape), axis, 0, 0)]
    ppermute x0 -> x18, waiting for transfers between devices: none -> 18.1 us  [shift(): return lax.ppermute(v, axis, [(i, (i + by) % size) for i in range(size)])]
  transfers between devices with their start and end apart: 3 -> 23, of which waited for: 3 -> 8; matrix products, arithmetic and copies ran while one was open for 1% -> 26% of each run, Pallas kernels for 0% -> 0%
where the time goes in v1:
time: 192 us; the launch traced here: 190 us
  starting transfers between devices  55.7 us (29%)
  waiting for transfers between devices  42.9 us (22%)
  other arithmetic  26.8 us (14%)
  local copies, waits for them, and re-layouts  25.2 us (13%)
  blocking collectives  17 us (9%)
  Pallas kernels  11.8 us (6%)
  matrix products  9.66 us (5%)
    ppermute x18, starting transfers between devices, shift(): return lax.ppermute(v, axis, [(i, (i + by) % size) for i in range(size)])  33.6 us
    ppermute x18, waiting for transfers between devices, shift(): return lax.ppermute(v, axis, [(i, (i + by) % size) for i in range(size)])  18.1 us
    all_to_all x1, blocking collectives, everyone(): return lax.all_to_all(jnp.broadcast_to(v[None], (n,) + v.shape), axis, 0, 0)  17 us
    all_to_all x3, starting transfers between devices, everyone(): return lax.all_to_all(jnp.broadcast_to(v[None], (n,) + v.shape), axis, 0, 0)  13.8 us
    pallas_call x1, Pallas kernels, final(): pl.pallas_call(final_kernel, grid=(D // TILE,), in_specs=[pl.BlockSpec(me...  11.8 us
    all_to_all x3, waiting for transfers between devices, everyone(): return lax.all_to_all(jnp.broadcast_to(v[None], (n,) + v.shape), axis, 0, 0)  9.71 us
    all_to_all x1, waiting for transfers between devices, on_device(): mine = jnp.sum(lax.all_to_all(mine, ('x', 'y'), 0, 0), axis=0)  9.42 us
    dot_general x6, matrix products, dot(): lax.dot_general(a, b, (((ca,), (cb,)), ((), ())), preferred_element_type=...  9.03 us
  transfers between devices with their start and end apart: 23, of which 8 were waited for; matrix products, arithmetic and copies ran while one was open for 26% of the time, Pallas kernels for 0%

profile of v1, /device:TPU:1, one launch (start us, length us, event | category | flops | bytes accessed | tf_op | source)
XLA Modules:
  0.0 190.2 jit_solution(18188927955992670236)
XLA Ops:
  3.1 2.5 %collective-permute-start = (bf16[64,4608]{1,0:T(8,128)(2,1)}, bf16[64,4608]{1,0:T(8,128)(2,1)S(1)}, u32[]{:S(2)}, u32[]{:S(2)}) collective-permute-start(bf16[64,4608]{1,0:T(8,128)(2,1)} %get-tuple-element.48), channel_id=1, source_target_pairs={{0,1},{1,2},{2,3},{3,4},{4,5},{5,6},{6,7},{7,0},{8,9},{9,10},{10,1... | collective-permute-start | bytes 1769480 | tf_op jit(solution)/shard_map/ppermute | solution.py:34
  5.6 3.9 %collective-permute-start.11 = (bf16[64,4608]{1,0:T(8,128)(2,1)}, bf16[64,4608]{1,0:T(8,128)(2,1)S(1)}, u32[]{:S(2)}, u32[]{:S(2)}) collective-permute-start(bf16[64,4608]{1,0:T(8,128)(2,1)} %get-tuple-element.48), channel_id=1, source_target_pairs={{0,7},{1,0},{2,1},{3,2},{4,3},{5,4},{6,5},{7,6},{8,15},{9,8},{10,9... | collective-permute-start | bytes 1769480 | tf_op jit(solution)/shard_map/ppermute | solution.py:34
  11.7 5.3 %all-to-all-start = ((f32[8,64,128]{2,1,0:T(8,128)}), f32[8,64,128]{2,1,0:T(8,128)S(1)}, u32[]{:S(2)}, u32[]{:S(2)}) async-start(f32[8,64,128]{2,1,0:T(8,128)} %broadcast_in_dim.11), calls=%async_computation | async-start | bytes 524288 | tf_op jit(solution)/shard_map/all_to_all | solution.py:38
  17.0 3.1 %fusion.2 = f32[192,256]{1,0:T(8,128)S(1)} fusion(bf16[1,256,4608]{2,1,0:T(8,128)(2,1)} %refs_16_.1, bf16[4608,64]{0,1:T(8,128)(2,1)} %copy-done.11, bf16[4608,64]{0,1:T(8,128)(2,1)} %copy-done.12, bf16[4608,64]{0,1:T(8,128)(2,1)} %copy-done.10), kind=kOutput, calls=%fused_computation.3 | convolution fusion | flops 458293248 | bytes 4325376 | tf_op jit(solution)/shard_map/dot_general | solution.py:30
  20.1 7.5 %all-to-all-done = f32[8,64,128]{2,1,0:T(8,128)S(1)} async-done(((f32[8,64,128]{2,1,0:T(8,128)}), f32[8,64,128]{2,1,0:T(8,128)S(1)}, u32[]{:S(2)}, u32[]{:S(2)}) %all-to-all-start) | async-done | bytes 262176 | tf_op jit(solution)/shard_map/all_to_all | solution.py:38
  28.0 2.6 %collective-permute-start.14 = (f32[32,256]{1,0:T(8,128)S(1)}, f32[32,256]{1,0:T(8,128)S(1)}, u32[]{:S(2)}, u32[]{:S(2)}) collective-permute-start(f32[32,256]{1,0:T(8,128)S(1)} %slice_select_fusion.1), channel_id=1, source_target_pairs={{0,8},{8,0},{1,9},{9,1},{2,10},{10,2},{3,11},{11,3},{4,12},{12,4},... | collective-permute-start | bytes 98312 | tf_op jit(solution)/shard_map/ppermute | solution.py:34
  30.6 3.8 %collective-permute-start.1 = (bf16[64,4608]{1,0:T(8,128)(2,1)}, bf16[64,4608]{1,0:T(8,128)(2,1)S(1)}, u32[]{:S(2)}, u32[]{:S(2)}) collective-permute-start(bf16[64,4608]{1,0:T(8,128)(2,1)} %get-tuple-element.47), channel_id=1, source_target_pairs={{0,1},{1,2},{2,3},{3,4},{4,5},{5,6},{6,7},{7,0},{8,9},{9,10},{10,1... | collective-permute-start | bytes 1769480 | tf_op jit(solution)/shard_map/ppermute | solution.py:34
  34.5 17.0 %all_to_all.30 = f32[16,32,256]{2,1,0:T(8,128)} all-to-all(f32[16,32,256]{2,1,0:T(8,128)S(1)} %broadcast_in_dim.12), channel_id=1, replica_groups=mesh['x'=4,'y'=4,'core'=2,'z'=8] {'x','y'}, dimensions={0} | all-to-all | bytes 1048576 | tf_op jit(solution)/shard_map/all_to_all | solution.py:38
  58.4 4.1 %all-to-all-start.2 = ((f32[8,96,128]{2,1,0:T(8,128)}), f32[8,96,128]{2,1,0:T(8,128)}, u32[]{:S(2)}, u32[]{:S(2)}) async-start(f32[8,96,128]{2,1,0:T(8,128)} %pad_maximum_fusion.4), calls=%async_computation.2 | async-start | bytes 786432 | tf_op jit(solution)/shard_map/all_to_all | solution.py:151
  62.5 2.6 %collective-permute-start.12 = (bf16[64,4608]{1,0:T(8,128)(2,1)S(1)}, bf16[64,4608]{1,0:T(8,128)(2,1)}, u32[]{:S(2)}, u32[]{:S(2)}) collective-permute-start(bf16[64,4608]{1,0:T(8,128)(2,1)S(1)} %collective-permute-done.11.refs_13_), channel_id=1, source_target_pairs={{0,7},{1,0},{2,1},{3,2},{4,3},{5,4},{6,5},{7,6},{8,15},{9,8},{10,9... | collective-permute-start | bytes 1769480 | tf_op jit(solution)/shard_map/ppermute | solution.py:34
  67.8 4.1 %fusion = f32[192,4608]{1,0:T(8,128)} fusion(bf16[1,256,4608]{2,1,0:T(8,128)(2,1)} %refs_16_.1, bf16[64,256]{1,0:T(8,128)(2,1)} %copy-done.15, bf16[64,256]{1,0:T(8,128)(2,1)} %copy-done.14, bf16[64,256]{1,0:T(8,128)(2,1)} %copy-done.13), kind=kOutput, calls=%fused_computation.1 | convolution fusion | flops 453279744 | bytes 5996544 | tf_op jit(solution)/shard_map/dot_general | solution.py:30
  71.9 5.7 %all-to-all-done.2 = f32[8,96,128]{2,1,0:T(8,128)} async-done(((f32[8,96,128]{2,1,0:T(8,128)}), f32[8,96,128]{2,1,0:T(8,128)}, u32[]{:S(2)}, u32[]{:S(2)}) %all-to-all-start.2) | async-done | bytes 393248 | tf_op jit(solution)/shard_map/all_to_all | solution.py:151
  79.2 6.4 %collective-permute-done.12.refs_11_ = bf16[64,4608]{1,0:T(8,128)(2,1)} collective-permute-done((bf16[64,4608]{1,0:T(8,128)(2,1)S(1)}, bf16[64,4608]{1,0:T(8,128)(2,1)}, u32[]{:S(2)}, u32[]{:S(2)}) %collective-permute-start.12) | collective-permute-done | bytes 589856 | tf_op jit(solution)/shard_map/ppermute | solution.py:34
  90.0 9.5 %collective-permute-done.3.refs_4_ = bf16[64,4608]{1,0:T(8,128)(2,1)} collective-permute-done((bf16[64,4608]{1,0:T(8,128)(2,1)S(1)}, bf16[64,4608]{1,0:T(8,128)(2,1)}, u32[]{:S(2)}, u32[]{:S(2)}) %collective-permute-start.3) | collective-permute-done | bytes 589856 | tf_op jit(solution)/shard_map/ppermute | solution.py:34
  100.9 2.7 %collective-permute-start.13 = (bf16[64,4608]{1,0:T(8,128)(2,1)}, bf16[64,4608]{1,0:T(8,128)(2,1)}, u32[]{:S(2)}, u32[]{:S(2)}) collective-permute-start(bf16[64,4608]{1,0:T(8,128)(2,1)} %collective-permute-done.12.refs_11_), channel_id=1, source_target_pairs={{0,7},{1,0},{2,1},{3,2},{4,3},{5,4},{6,5},{7,6},{8,15},{9,8},{10,9... | collective-permute-start | bytes 1769480 | tf_op jit(solution)/shard_map/ppermute | solution.py:34
  106.7 4.2 %all-to-all-start.3 = ((f32[16,2,4608]{2,1,0:T(2,128)}), f32[16,2,4608]{2,1,0:T(2,128)}, u32[]{:S(2)}, u32[]{:S(2)}) async-start(f32[16,2,4608]{2,1,0:T(2,128)} %reshape.98), calls=%async_computation.3 | async-start | bytes 1179648 | tf_op jit(solution)/shard_map/all_to_all | solution.py:161
  112.5 9.4 %all-to-all-done.3 = f32[16,2,4608]{2,1,0:T(2,128)} async-done(((f32[16,2,4608]{2,1,0:T(2,128)}), f32[16,2,4608]{2,1,0:T(2,128)}, u32[]{:S(2)}, u32[]{:S(2)}) %all-to-all-start.3) | async-done | bytes 589856 | tf_op jit(solution)/shard_map/all_to_all | solution.py:161
  125.4 4.2 %all-to-all-start.4 = ((f32[8,2,4608]{2,1,0:T(2,128)}), f32[8,2,4608]{2,1,0:T(2,128)}, u32[]{:S(2)}, u32[]{:S(2)}) async-start(f32[8,2,4608]{2,1,0:T(2,128)} %broadcast_in_dim.14), calls=%async_computation.4 | async-start | bytes 589824 | tf_op jit(solution)/shard_map/all_to_all | solution.py:38
  143.1 4.3 %all-to-all-start.5 = ((f32[16,2,4608]{2,1,0:T(2,128)}), f32[16,2,4608]{2,1,0:T(2,128)}, u32[]{:S(2)}, u32[]{:S(2)}) async-start(f32[16,2,4608]{2,1,0:T(2,128)} %broadcast_in_dim.15), calls=%async_computation.5 | async-start | bytes 1179648 | tf_op jit(solution)/shard_map/all_to_all | solution.py:38
  151.0 6.6 %cholesky.17 = f32[64,64]{1,0:T(8,128)S(1)} custom-call(f32[64,64]{1,0:T(8,128)} %fusion.28), custom_call_target="Cholesky" | custom-call | tf_op jit(solution)/shard_map/jit(cholesky)/cholesky | solution.py:170
  160.6 5.0 %collective-permute-start.17 = (f32[32,4608]{1,0:T(8,128)}, f32[32,4608]{1,0:T(8,128)}, u32[]{:S(2)}, u32[]{:S(2)}) collective-permute-start(f32[32,4608]{1,0:T(8,128)} %reshape.99), channel_id=1, source_target_pairs={{0,8},{8,0},{1,9},{9,1},{2,10},{10,2},{3,11},{11,3},{4,12},{12,4},... | collective-permute-start | bytes 1769480 | tf_op jit(solution)/shard_map/ppermute | solution.py:34
  166.2 4.9 %custom-call.7 = f32[1,64,64]{1,2,0:T(8,128)S(1)} custom-call(f32[1,64,64]{2,1,0:T(8,128)S(1)} %fusion.24), custom_call_target="InvertDiagBlocksLowerTriangular" | custom-call | tf_op jit(solution)/shard_map/jit(_solve_triangular)/triangular_solve | solution.py:171
  174.2 11.8 %shard_map.84 = (bf16[1,256,4608]{2,1,0:T(8,128)(2,1)}, bf16[1024,256]{1,0:T(8,128)(2,1)}, f32[4608,64]{1,0:T(8,128)S(1)}) custom-call(s32[1]{0:T(128)} %bitcast.z_ref, bf16[128,4608]{1,0:T(8,128)(2,1)S(1)} %copy-done.1, bf16[64,4608]{1,0:T(8,128)(2,1)S(1)} %collective-permute-done.refs_1_, bf16[64,4608]{1,0:T(8,128)(2,1)S(1)} %copy-done.5, ...), custom_call_target="tpu_custom_call" | custom-call | flops 4831838208 | bytes 18874368 | tf_op jit(solution)/shard_map/pallas_call | solution.py:89
  187.3 2.8 %copy.38 = f32[4608,64]{0,1:T(8,128)} copy(f32[4608,64]{1,0:T(8,128)} %copy-done.2) | data formatting | bytes 2359296
  (112 shorter events, 55.1 us)
Async XLA Ops:
  0.6 27.0 %copy-start = (bf16[1024,256]{1,0:T(8,128)(2,1)S(1)}, bf16[1024,256]{1,0:T(8,128)(2,1)}, u32[]{:S(2)}) copy-start(bf16[1024,256]{1,0:T(8,128)(2,1)} %param.6) | copy-start | bytes 1572868
  3.1 24.5 %collective-permute-start = (bf16[64,4608]{1,0:T(8,128)(2,1)}, bf16[64,4608]{1,0:T(8,128)(2,1)S(1)}, u32[]{:S(2)}, u32[]{:S(2)}) collective-permute-start(bf16[64,4608]{1,0:T(8,128)(2,1)} %get-tuple-element.48), channel_id=1, source_target_pairs={{0,1},{1,2},{2,3},{3,4},{4,5},{5,6},{6,7},{7,0},{8,9},{9,10},{10,1... | collective-permute-start | bytes 1769480 | tf_op jit(solution)/shard_map/ppermute | solution.py:34
  5.6 22.0 %collective-permute-start.11 = (bf16[64,4608]{1,0:T(8,128)(2,1)}, bf16[64,4608]{1,0:T(8,128)(2,1)S(1)}, u32[]{:S(2)}, u32[]{:S(2)}) collective-permute-start(bf16[64,4608]{1,0:T(8,128)(2,1)} %get-tuple-element.48), channel_id=1, source_target_pairs={{0,7},{1,0},{2,1},{3,2},{4,3},{5,4},{6,5},{7,6},{8,15},{9,8},{10,9... | collective-permute-start | bytes 1769480 | tf_op jit(solution)/shard_map/ppermute | solution.py:34
  11.7 15.9 %all-to-all-start = ((f32[8,64,128]{2,1,0:T(8,128)}), f32[8,64,128]{2,1,0:T(8,128)S(1)}, u32[]{:S(2)}, u32[]{:S(2)}) async-start(f32[8,64,128]{2,1,0:T(8,128)} %broadcast_in_dim.11), calls=%async_computation | async-start | bytes 524288 | tf_op jit(solution)/shard_map/all_to_all | solution.py:38
  28.0 6.4 %collective-permute-start.14 = (f32[32,256]{1,0:T(8,128)S(1)}, f32[32,256]{1,0:T(8,128)S(1)}, u32[]{:S(2)}, u32[]{:S(2)}) collective-permute-start(f32[32,256]{1,0:T(8,128)S(1)} %slice_select_fusion.1), channel_id=1, source_target_pairs={{0,8},{8,0},{1,9},{9,1},{2,10},{10,2},{3,11},{11,3},{4,12},{12,4},... | collective-permute-start | bytes 98312 | tf_op jit(solution)/shard_map/ppermute | solution.py:34
  30.6 22.0 %collective-permute-start.1 = (bf16[64,4608]{1,0:T(8,128)(2,1)}, bf16[64,4608]{1,0:T(8,128)(2,1)S(1)}, u32[]{:S(2)}, u32[]{:S(2)}) collective-permute-start(bf16[64,4608]{1,0:T(8,128)(2,1)} %get-tuple-element.47), channel_id=1, source_target_pairs={{0,1},{1,2},{2,3},{3,4},{4,5},{5,6},{6,7},{7,0},{8,9},{9,10},{10,1... | collective-permute-start | bytes 1769480 | tf_op jit(solution)/shard_map/ppermute | solution.py:34
  34.4 18.2 %collective-permute-start.7 = (bf16[64,4608]{1,0:T(8,128)(2,1)}, bf16[64,4608]{1,0:T(8,128)(2,1)}, u32[]{:S(2)}, u32[]{:S(2)}) collective-permute-start(bf16[64,4608]{1,0:T(8,128)(2,1)} %get-tuple-element.47), channel_id=1, source_target_pairs={{0,7},{1,0},{2,1},{3,2},{4,3},{5,4},{6,5},{7,6},{8,15},{9,8},{10,9... | collective-permute-start | bytes 1769480 | tf_op jit(solution)/shard_map/ppermute | solution.py:34
  52.7 3.0 %collective-permute-start.15 = (f32[32,256]{1,0:T(8,128)S(1)}, f32[32,256]{1,0:T(8,128)S(1)}, u32[]{:S(2)}, u32[]{:S(2)}) collective-permute-start(f32[32,256]{1,0:T(8,128)S(1)} %reduce_sum.36), channel_id=1, source_target_pairs={{0,8},{8,0},{1,9},{9,1},{2,10},{10,2},{3,11},{11,3},{4,12},{12,4},... | collective-permute-start | bytes 98312 | tf_op jit(solution)/shard_map/ppermute | solution.py:34
  58.4 19.2 %all-to-all-start.2 = ((f32[8,96,128]{2,1,0:T(8,128)}), f32[8,96,128]{2,1,0:T(8,128)}, u32[]{:S(2)}, u32[]{:S(2)}) async-start(f32[8,96,128]{2,1,0:T(8,128)} %pad_maximum_fusion.4), calls=%async_computation.2 | async-start | bytes 786432 | tf_op jit(solution)/shard_map/all_to_all | solution.py:151
  62.5 23.2 %collective-permute-start.12 = (bf16[64,4608]{1,0:T(8,128)(2,1)S(1)}, bf16[64,4608]{1,0:T(8,128)(2,1)}, u32[]{:S(2)}, u32[]{:S(2)}) collective-permute-start(bf16[64,4608]{1,0:T(8,128)(2,1)S(1)} %collective-permute-done.11.refs_13_), channel_id=1, source_target_pairs={{0,7},{1,0},{2,1},{3,2},{4,3},{5,4},{6,5},{7,6},{8,15},{9,8},{10,9... | collective-permute-start | bytes 1769480 | tf_op jit(solution)/shard_map/ppermute | solution.py:34
  65.0 21.8 %collective-permute-start.2 = (bf16[64,4608]{1,0:T(8,128)(2,1)S(1)}, bf16[64,4608]{1,0:T(8,128)(2,1)}, u32[]{:S(2)}, u32[]{:S(2)}) collective-permute-start(bf16[64,4608]{1,0:T(8,128)(2,1)S(1)} %collective-permute-done.refs_1_), channel_id=1, source_target_pairs={{0,1},{1,2},{2,3},{3,4},{4,5},{5,6},{6,7},{7,0},{8,9},{9,10},{10,1... | collective-permute-start | bytes 1769480 | tf_op jit(solution)/shard_map/ppermute | solution.py:34
  65.1 34.5 %collective-permute-start.3 = (bf16[64,4608]{1,0:T(8,128)(2,1)S(1)}, bf16[64,4608]{1,0:T(8,128)(2,1)}, u32[]{:S(2)}, u32[]{:S(2)}) collective-permute-start(bf16[64,4608]{1,0:T(8,128)(2,1)S(1)} %collective-permute-done.1.refs_2_), channel_id=1, source_target_pairs={{0,1},{1,2},{2,3},{3,4},{4,5},{5,6},{6,7},{7,0},{8,9},{9,10},{10,1... | collective-permute-start | bytes 1769480 | tf_op jit(solution)/shard_map/ppermute | solution.py:34
  65.4 34.1 %collective-permute-start.8 = (bf16[64,4608]{1,0:T(8,128)(2,1)}, bf16[64,4608]{1,0:T(8,128)(2,1)}, u32[]{:S(2)}, u32[]{:S(2)}) collective-permute-start(bf16[64,4608]{1,0:T(8,128)(2,1)} %collective-permute-done.7.refs_14_), channel_id=1, source_target_pairs={{0,7},{1,0},{2,1},{3,2},{4,3},{5,4},{6,5},{7,6},{8,15},{9,8},{10,9... | collective-permute-start | bytes 1769480 | tf_op jit(solution)/shard_map/ppermute | solution.py:34
  99.6 3.9 %collective-permute-start.16 = (f32[32,4608]{1,0:T(8,128)S(1)}, f32[32,4608]{1,0:T(8,128)S(1)}, u32[]{:S(2)}, u32[]{:S(2)}) collective-permute-start(f32[32,4608]{1,0:T(8,128)S(1)} %slice_select_fusion), channel_id=1, source_target_pairs={{0,8},{8,0},{1,9},{9,1},{2,10},{10,2},{3,11},{11,3},{4,12},{12,4},... | collective-permute-start | bytes 1769480 | tf_op jit(solution)/shard_map/ppermute | solution.py:34
  100.9 22.9 %collective-permute-start.4 = (bf16[64,4608]{1,0:T(8,128)(2,1)}, bf16[64,4608]{1,0:T(8,128)(2,1)S(1)}, u32[]{:S(2)}, u32[]{:S(2)}) collective-permute-start(bf16[64,4608]{1,0:T(8,128)(2,1)} %collective-permute-done.2.refs_3_), channel_id=1, source_target_pairs={{0,1},{1,2},{2,3},{3,4},{4,5},{5,6},{6,7},{7,0},{8,9},{9,10},{10,1... | collective-permute-start | bytes 1769480 | tf_op jit(solution)/shard_map/ppermute | solution.py:34
  100.9 22.9 %collective-permute-start.13 = (bf16[64,4608]{1,0:T(8,128)(2,1)}, bf16[64,4608]{1,0:T(8,128)(2,1)}, u32[]{:S(2)}, u32[]{:S(2)}) collective-permute-start(bf16[64,4608]{1,0:T(8,128)(2,1)} %collective-permute-done.12.refs_11_), channel_id=1, source_target_pairs={{0,7},{1,0},{2,1},{3,2},{4,3},{5,4},{6,5},{7,6},{8,15},{9,8},{10,9... | collective-permute-start | bytes 1769480 | tf_op jit(solution)/shard_map/ppermute | solution.py:34
  106.7 15.2 %all-to-all-start.3 = ((f32[16,2,4608]{2,1,0:T(2,128)}), f32[16,2,4608]{2,1,0:T(2,128)}, u32[]{:S(2)}, u32[]{:S(2)}) async-start(f32[16,2,4608]{2,1,0:T(2,128)} %reshape.98), calls=%async_computation.3 | async-start | bytes 1179648 | tf_op jit(solution)/shard_map/all_to_all | solution.py:161
  110.9 22.9 %collective-permute-start.9 = (bf16[64,4608]{1,0:T(8,128)(2,1)}, bf16[64,4608]{1,0:T(8,128)(2,1)}, u32[]{:S(2)}, u32[]{:S(2)}) collective-permute-start(bf16[64,4608]{1,0:T(8,128)(2,1)} %collective-permute-done.8.refs_12_), channel_id=1, source_target_pairs={{0,7},{1,0},{2,1},{3,2},{4,3},{5,4},{6,5},{7,6},{8,15},{9,8},{10,9... | collective-permute-start | bytes 1769480 | tf_op jit(solution)/shard_map/ppermute | solution.py:34
  111.2 30.2 %collective-permute-start.5 = (bf16[64,4608]{1,0:T(8,128)(2,1)}, bf16[64,4608]{1,0:T(8,128)(2,1)}, u32[]{:S(2)}, u32[]{:S(2)}) collective-permute-start(bf16[64,4608]{1,0:T(8,128)(2,1)} %collective-permute-done.3.refs_4_), channel_id=1, source_target_pairs={{0,1},{1,2},{2,3},{3,4},{4,5},{5,6},{6,7},{7,0},{8,9},{9,10},{10,1... | collective-permute-start | bytes 1769480 | tf_op jit(solution)/shard_map/ppermute | solution.py:34
  125.4 14.3 %all-to-all-start.4 = ((f32[8,2,4608]{2,1,0:T(2,128)}), f32[8,2,4608]{2,1,0:T(2,128)}, u32[]{:S(2)}, u32[]{:S(2)}) async-start(f32[8,2,4608]{2,1,0:T(2,128)} %broadcast_in_dim.14), calls=%async_computation.4 | async-start | bytes 589824 | tf_op jit(solution)/shard_map/all_to_all | solution.py:38
  132.2 40.8 %collective-permute-start.6 = (bf16[64,4608]{1,0:T(8,128)(2,1)}, bf16[64,4608]{1,0:T(8,128)(2,1)}, u32[]{:S(2)}, u32[]{:S(2)}) collective-permute-start(bf16[64,4608]{1,0:T(8,128)(2,1)} %copy-done.6), channel_id=1, source_target_pairs={{0,1},{1,2},{2,3},{3,4},{4,5},{5,6},{6,7},{7,0},{8,9},{9,10},{10,1... | collective-permute-start | bytes 1769480 | tf_op jit(solution)/shard_map/ppermute | solution.py:34
  133.8 39.2 %collective-permute-start.10 = (bf16[64,4608]{1,0:T(8,128)(2,1)}, bf16[64,4608]{1,0:T(8,128)(2,1)}, u32[]{:S(2)}, u32[]{:S(2)}) collective-permute-start(bf16[64,4608]{1,0:T(8,128)(2,1)} %collective-permute-done.9.refs_10_), channel_id=1, source_target_pairs={{0,7},{1,0},{2,1},{3,2},{4,3},{5,4},{6,5},{7,6},{8,15},{9,8},{10,9... | collective-permute-start | bytes 1769480 | tf_op jit(solution)/shard_map/ppermute | solution.py:34
  143.1 15.1 %all-to-all-start.5 = ((f32[16,2,4608]{2,1,0:T(2,128)}), f32[16,2,4608]{2,1,0:T(2,128)}, u32[]{:S(2)}, u32[]{:S(2)}) async-start(f32[16,2,4608]{2,1,0:T(2,128)} %broadcast_in_dim.15), calls=%async_computation.5 | async-start | bytes 1179648 | tf_op jit(solution)/shard_map/all_to_all | solution.py:38
  160.6 11.0 %collective-permute-start.17 = (f32[32,4608]{1,0:T(8,128)}, f32[32,4608]{1,0:T(8,128)}, u32[]{:S(2)}, u32[]{:S(2)}) collective-permute-start(f32[32,4608]{1,0:T(8,128)} %reshape.99), channel_id=1, source_target_pairs={{0,8},{8,0},{1,9},{9,1},{2,10},{10,2},{3,11},{11,3},{4,12},{12,4},... | collective-permute-start | bytes 1769480 | tf_op jit(solution)/shard_map/ppermute | solution.py:34
  (16 other events, 49.5 us)

commit v2 on v0

v2 whole, which is shorter than its diff:
```python
import functools

import jax
import jax.numpy as jnp
from jax import lax
from jax.experimental import pallas as pl
from jax.experimental.pallas import tpu as pltpu
from jax.sharding import Mesh
from jax.sharding import PartitionSpec as P

D, K, NZ, NXY = 4608, 64, 8, 16
TILE = 1152
PIECES = 1
NT = D // TILE
HI = lax.Precision.HIGHEST
F32, BF16 = jnp.float32, jnp.bfloat16
SMEM = pl.BlockSpec(memory_space=pltpu.SMEM)


def split3(v):
    hi = v.astype(BF16)
    rest = v - hi.astype(F32)
    mid = rest.astype(BF16)
    low = (rest - mid.astype(F32)).astype(BF16)
    return jnp.concatenate([hi, mid, low], axis=0)


def fold3(v):
    n = v.shape[0] // 3
    return v[:n] + v[n : 2 * n] + v[2 * n :]


def dot(a, b, ca, cb, precision=None):
    return lax.dot_general(
        a, b, (((ca,), (cb,)), ((), ())), precision=precision, preferred_element_type=F32
    )


def whole(shape):
    return pl.BlockSpec(shape, lambda *_: (0,) * len(shape))


def out(shape, dtype=F32):
    return jax.ShapeDtypeStruct(shape, dtype)


def call(
    kernel, operands, in_specs, out_shapes, out_specs, grid=(1,), flops=0, scratch=(), mib=16,
    hbm_in=(), hbm_out=(),
):
    size = sum(v.size * v.dtype.itemsize for v in operands) + sum(
        s.size * jnp.dtype(s.dtype).itemsize for s in out_shapes
    )
    operands = [
        pltpu.with_memory_space_constraint(v, pltpu.HBM) if i in hbm_in else v
        for i, v in enumerate(operands)
    ]
    out_shapes = [
        pltpu.HBM(s.shape, s.dtype) if i in hbm_out else s for i, s in enumerate(out_shapes)
    ]
    return pl.pallas_call(
        kernel,
        grid=grid,
        in_specs=in_specs,
        out_specs=out_specs,
        out_shape=out_shapes,
        scratch_shapes=scratch,
        compiler_params=pltpu.CompilerParams(vmem_limit_bytes=mib * 1024 * 1024),
        cost_estimate=pl.CostEstimate(flops=flops, bytes_accessed=size, transcendentals=0),
    )(*operands)


def simple(kernel, operands, out_shapes, flops=0):
    specs = [SMEM if v.dtype == jnp.int32 else whole(v.shape) for v in operands]
    return call(kernel, operands, specs, out_shapes, [whole(s.shape) for s in out_shapes], flops=flops)


def rows_kernel(q_ref, g_ref, y_ref):
    y = fold3(dot(split3(q_ref[...]), g_ref[...], 1, 1))
    for j in range(NZ):
        y_ref[j] = y


def error_rows_kernel(q_ref, e_ref, a_ref, out_ref, a_t_ref):
    out_ref[...] = fold3(dot(split3(q_ref[...]), e_ref[0], 1, 1))
    a_t_ref[...] = a_ref[...].T


def pick(core_ref, a, b):
    return jnp.where(core_ref[0] == 0, a, b)


def left_kernel(core_ref, y_ref, a_ref, eq_ref, mine_ref, other_ref):
    y = jnp.concatenate([y_ref[j] for j in range(NZ)], axis=1)
    p = fold3(dot(split3(y), a_ref[...], 1, 0)) + eq_ref[...]
    mine_ref[...] = pick(core_ref, p[:32], p[32:])
    other_ref[...] = pick(core_ref, p[32:], p[:32])


def total(ref):
    acc = ref[0]
    for j in range(1, ref.shape[0]):
        acc = acc + ref[j]
    return acc


def total_kernel(in_ref, out_ref):
    out_ref[...] = total(in_ref)


def spread_kernel(in_ref, out_ref):
    acc = total(in_ref)
    for j in range(out_ref.shape[0]):
        out_ref[j] = acc


def pair_kernel(a_ref, b_ref, out_ref):
    acc = a_ref[...] + b_ref[...]
    for j in range(out_ref.shape[0]):
        out_ref[j] = acc


def add_kernel(a_ref, b_ref, out_ref):
    out_ref[...] = a_ref[...] + b_ref[...]


def terms_kernel(core_ref, mine_ref, other_ref, a_ref, p_ref, sent_ref):
    mine, other = mine_ref[...], other_ref[...]
    p = jnp.concatenate([pick(core_ref, mine, other), pick(core_ref, other, mine)], axis=0)
    p_ref[...] = p
    terms = fold3(dot(split3(p), a_ref[...], 1, 0))
    gram = dot(p, p, 1, 1, HI)
    packed = jnp.concatenate([gram[:32], gram[32:]], axis=1)
    for j in range(NZ):
        sent_ref[j, :K] = terms[:, 128 * j : 128 * (j + 1)]
        sent_ref[j, K:] = packed


def error_terms_kernel(p_ref, e_ref, out_ref):
    out_ref[...] = fold3(dot(split3(p_ref[...]), e_ref[0], 1, 0))


def right_kernel(core_ref, got_ref, ep_ref, g_ref, mine_ref, other_ref, gram_ref):
    got = total(got_ref)
    gram_ref[...] = jnp.concatenate([got[K:, :K], got[K:, K:]], axis=0)
    q = fold3(dot(split3(got[:K]), g_ref[...], 1, 0)) + ep_ref[...]
    mine_ref[:, 0] = pick(core_ref, q[:32], q[32:]).reshape(4, 8, TILE)
    other_ref[:, 0] = pick(core_ref, q[32:], q[:32]).reshape(4, 8, TILE)


def factor_kernel(gram_ref, p_ref, linv_ref, pf_ref):
    row = lax.broadcasted_iota(jnp.int32, (K, K), 0)
    lane = lax.broadcasted_iota(jnp.int32, (K, K), 1)
    eye = jnp.where(row == lane, 1.0, 0.0)
    both = jnp.concatenate([gram_ref[...], eye], axis=1)
    tiles = [both[8 * t : 8 * t + 8] for t in range(8)]
    sub = lax.broadcasted_iota(jnp.int32, (8, 128), 0)
    for i in range(K):
        b, r = divmod(i, 8)
        pivot = tiles[b][r : r + 1]
        scaled = pivot * (1.0 / pivot[:, i : i + 1])
        for t in range(b, 8):
            factor = jnp.broadcast_to(tiles[t][:, i : i + 1], (8, 128))
            if t == b:
                factor = jnp.where(sub > r, factor, 0.0)
            tiles[t] = tiles[t] - factor * scaled
    both = jnp.concatenate(tiles, axis=0)
    pivots = jnp.sum(both[:, :K] * eye, axis=1, keepdims=True)
    linv = both[:, K:] * lax.rsqrt(pivots)
    linv_ref[...] = linv
    pf_ref[...] = dot(linv, p_ref[...], 1, 0, HI)


def bulk_kernel(first, last, *refs):
    if first:
        rows_ref, a_ref, e_ref, w_ref = refs[:4]
    else:
        rows_ref, a_ref, e_ref, w_ref, sum_ref = refs[:5]
    if last:
        merged_ref, grad_ref, acc_ref = refs[-3:]
    else:
        merged_ref, acc_ref = refs[-2:]
    step = pl.program_id(0)
    rows = rows_ref[...]
    merged_ref[...] = jnp.dot(
        a_ref[...], rows, preferred_element_type=F32
    ) + e_ref[0].astype(F32)
    part = dot(rows, w_ref[...], 1, 1)

    @pl.when(step == 0)
    def _():
        acc_ref[...] = part if first else sum_ref[...] + part

    @pl.when(step > 0)
    def _():
        acc_ref[...] += part

    if last:

        @pl.when(step == pl.num_programs(0) - 1)
        def _():
            grad_ref[...] = acc_ref[...].astype(BF16)


def bulk(piece, rows, a_t, error_prev, out_weight, grad_sum):
    first, last = piece == 0, piece == PIECES - 1
    steps = rows.shape[1] // TILE
    base = piece * steps
    operands = [rows, a_t, error_prev, out_weight] + ([] if first else [grad_sum])
    specs = [
        pl.BlockSpec((1024, TILE), lambda i: (0, i)),
        whole((256, 1024)),
        pl.BlockSpec((1, 256, TILE), lambda i: (0, 0, base + i)),
        pl.BlockSpec((256, TILE), lambda i: (0, base + i)),
    ] + ([] if first else [whole((1024, 256))])
    out_shapes = [out((256, rows.shape[1])), out((1024, 256), BF16 if last else F32)]
    return call(
        functools.partial(bulk_kernel, first, last), operands, specs, out_shapes,
        [pl.BlockSpec((256, TILE), lambda i: (0, i)), whole((1024, 256))], grid=(steps,),
        flops=4 * 256 * 1024 * rows.shape[1],
        scratch=[pltpu.VMEM((1024, 256), F32)] if last else [], mib=28,
        hbm_in=(0, 1, 2, 3), hbm_out=(0, 1) if last else (0,),
    )


def tail_kernel(core_ref, mine_ref, other_ref, linv_ref, pf_ref, *refs):
    merged_refs, (err_ref, q_ref) = refs[:-2], refs[-2:]
    merged = merged_refs[-1][...]
    for piece in range(PIECES - 1):
        here = pl.program_id(0) // (NT // PIECES) == piece
        merged = jnp.where(here, merged_refs[piece][...], merged)
    mine = mine_ref[:, 0].reshape(32, TILE)
    other = other_ref[:, 0].reshape(32, TILE)
    raw = jnp.concatenate([pick(core_ref, mine, other), pick(core_ref, other, mine)], axis=0)
    qf = dot(linv_ref[...], raw, 1, 0, HI) * (1.0 / 32)
    q_ref[...] = qf
    pf = pf_ref[...]
    pf_hi = pf.astype(BF16)
    pf_lo = (pf - pf_hi.astype(F32)).astype(BF16)
    q_hi = qf.astype(BF16)
    q_lo = (qf - q_hi.astype(F32)).astype(BF16)
    low = dot(
        jnp.concatenate([pf_hi, pf_hi, pf_lo], axis=0),
        jnp.concatenate([q_hi, q_lo, q_hi], axis=0), 0, 0,
    )
    err_ref[0] = (merged - low).astype(BF16)


def shift(v, axis, size, by):
    return lax.ppermute(v, axis, [(i, (i + by) % size) for i in range(size)])


def after(v, *others):
    return lax.optimization_barrier((v,) + others)[0]


def on_device(grad_out, attn_out, out_weight, error_prev, q_prev):
    core = lax.axis_index("core").astype(jnp.int32).reshape(1)
    swap = lambda v: shift(v, "core", 2, 1)
    plane = lambda v: lax.all_to_all(v, ("x", "y"), 0, 0)
    column = lambda v: lax.all_to_all(v, "z", 0, 0)
    q_prev_t = q_prev.T
    tile = lambda rows: pl.BlockSpec((rows, TILE), lambda i: (0, i))
    err_tile = pl.BlockSpec((1, 256, TILE), lambda i: (0, 0, i))
    chunk_tile = pl.BlockSpec((4, 1, 8, TILE), lambda i: (0, i, 0, 0))
    chunks = (NXY, 8, TILE)
    width = D // PIECES
    gathered = [
        lax.all_gather(grad_out[:, i * width : (i + 1) * width], "z", axis=0, tiled=True)
        for i in range(PIECES)
    ]

    (y,) = simple(
        rows_kernel, [q_prev_t, grad_out], [out((NZ, K, 128))], flops=2 * 192 * 128 * D
    )
    y = column(y)
    eq_t, a_t = simple(
        error_rows_kernel, [q_prev_t, error_prev, attn_out],
        [out((K, 256)), out((256, 1024), BF16)], flops=2 * 192 * 256 * D,
    )
    mine, other = simple(
        left_kernel, [core, y, attn_out, eq_t], [out((32, 256)), out((32, 256))],
        flops=2 * 192 * 256 * 1024,
    )
    (mine,) = simple(pair_kernel, [mine, swap(other)], [out((NXY, 32, 256))])
    (mine,) = simple(total_kernel, [plane(mine)], [out((32, 256))])

    p_t, sent = simple(
        terms_kernel, [core, mine, swap(mine), a_t], [out((K, 256)), out((NZ, 96, 128))],
        flops=2 * 192 * 256 * 1024,
    )
    got = column(sent)
    (ep,) = call(
        error_terms_kernel, [p_t, error_prev], [whole((K, 256)), err_tile], [out((K, D))],
        [tile(K)], grid=(NT,), flops=2 * 192 * 256 * D,
    )
    mine, other, gram = call(
        right_kernel, [core, got, ep, grad_out],
        [SMEM, whole((NZ, 96, 128)), tile(K), tile(128)],
        [out((4, NT, 8, TILE)), out((4, NT, 8, TILE)), out((K, K))],
        [chunk_tile, chunk_tile, whole((K, K))], grid=(NT,), flops=2 * 192 * 128 * D,
    )

    (mine,) = simple(add_kernel, [mine.reshape(chunks), swap(other).reshape(chunks)], [out(chunks)])
    mine = plane(mine)
    linv, pf_t = simple(factor_kernel, [gram, p_t], [out((K, K)), out((K, 256))], flops=300000000)
    mine, linv, pf_t = lax.optimization_barrier((mine, linv, pf_t))
    (mine,) = simple(spread_kernel, [mine], [out((NZ, 8, TILE))])
    mine = column(mine)
    merged, grad_attn = [], None
    for piece in range(PIECES):
        if piece == PIECES - 1:
            (mine,) = simple(spread_kernel, [mine], [out(chunks)])
            mine = plane(mine)
        part, grad_attn = bulk(piece, gathered[piece], a_t, error_prev, out_weight, grad_attn)
        merged.append(part)
        mine, grad_attn, *merged = lax.optimization_barrier((mine, grad_attn, *merged))
    other = swap(mine)
    per = NT // PIECES
    slot = lambda piece: pl.BlockSpec((256, TILE), lambda i: (0, jnp.clip(i - piece * per, 0, per - 1)))
    error_new, q_t = call(
        tail_kernel,
        [core, mine.reshape(4, NT, 8, TILE), other.reshape(4, NT, 8, TILE), linv, pf_t, *merged],
        [SMEM, chunk_tile, chunk_tile, whole((K, K)), whole((K, 256))]
        + [slot(piece) for piece in range(PIECES)],
        [out((1, 256, D), BF16), out((K, D))], [err_tile, tile(K)], grid=(NT,),
        flops=2 * 256 * 192 * D, hbm_in=(5, 6), hbm_out=(0, 1),
    )
    return grad_attn, pf_t.T, q_t.T, error_new


def solution(mesh):
    fine = Mesh(mesh.devices.reshape(4, 4, 2, 8), ("x", "y", "core", "z"))
    dp = ("x", "y", "core")
    in_specs = (P(dp + ("z",), None), P(dp, "z"), P("z", None), P(dp, "z", None), P())
    out_specs = (P(dp, "z"), P("z", None), P(), P(dp, "z", None))
    return jax.shard_map(
        on_device, mesh=fine, in_specs=in_specs, out_specs=out_specs, check_vma=False
    )
```

time: 558 us -> 161 us (0.29)
  waiting for transfers between devices: 467 us -> 37.4 us
  matrix products: 35.4 us -> 0 us
  Pallas kernels: 0 us -> 31.9 us
  starting transfers between devices: 0.12 us -> 30.2 us
  other arithmetic: 13.4 us -> 0 us
  blocking collectives: 23.4 us -> 34.2 us
  local copies, waits for them, and re-layouts: 2.33 us -> 12.1 us
    psum x2 -> x0, waiting for transfers between devices: 356 us -> none  [the longest x1 252 us: on_device(): q_total = lax.psum(q_term, ('dp', 'tensor'))]
    all_gather x1, waiting for transfers between devices: 110 us -> 4.64 us  [on_device(): lax.all_gather(grad_out[:, i * width:(i + 1) * width], 'z', axis=0, tiled...]
    dot_general x6 -> x0, matrix products: 34.3 us -> none  [the longest x1 7.32 us: on_device(): lax.dot_general(attn_out, row_block, (((0,), (0,)), ((), ())), preferred_...]
    all_to_all x0 -> x2, blocking collectives: none -> 34.2 us  [the longest x1 17.2 us: on_device(): column = lambda v: lax.all_to_all(v, 'z', 0, 0)]
    pallas_call x0 -> x14, Pallas kernels: none -> 31.9 us  [call(): pl.pallas_call(kernel, grid=grid, in_specs=in_specs, out_specs=out_specs,...]
    all_to_all x0 -> x4, waiting for transfers between devices: none -> 27.1 us  [the longest x2 22.7 us: on_device(): column = lambda v: lax.all_to_all(v, 'z', 0, 0)]
    psum x1 -> x0, blocking collectives: 23.4 us -> none  [on_device(): gram_matrix = lax.psum(gram_part, 'tensor')]
    all_to_all x0 -> x4, starting transfers between devices: none -> 22 us  [the longest x2 13.1 us: on_device(): column = lambda v: lax.all_to_all(v, 'z', 0, 0)]
  transfers between devices with their start and end apart: 3 -> 9, of which waited for: 3 -> 8; matrix products, arithmetic and copies ran while one was open for 1% -> 0% of each run, Pallas kernels for 0% -> 16%
where the time goes in v2:
time: 161 us; the launch traced here: 160 us
  waiting for transfers between devices  37.4 us (23%)
  blocking collectives  34.2 us (21%)
  Pallas kernels  31.9 us (20%)
  starting transfers between devices  30.2 us (19%)
  between operations  14.2 us (9%)
  local copies, waits for them, and re-layouts  12.1 us (8%)
    pallas_call x14, Pallas kernels, call(): pl.pallas_call(kernel, grid=grid, in_specs=in_specs, out_specs=out_specs,...  31.9 us
    all_to_all x2, waiting for transfers between devices, on_device(): column = lambda v: lax.all_to_all(v, 'z', 0, 0)  22.7 us
    all_to_all x1, blocking collectives, on_device(): column = lambda v: lax.all_to_all(v, 'z', 0, 0)  17.2 us
    all_to_all x1, blocking collectives, on_device(): plane = lambda v: lax.all_to_all(v, ('x', 'y'), 0, 0)  17.1 us
    all_to_all x2, starting transfers between devices, on_device(): column = lambda v: lax.all_to_all(v, 'z', 0, 0)  13.1 us
    unnamed x38, local copies, waits for them, and re-layouts  12.1 us
    all_to_all x2, starting transfers between devices, on_device(): plane = lambda v: lax.all_to_all(v, ('x', 'y'), 0, 0)  8.91 us
    ppermute x4, starting transfers between devices, shift(): return lax.ppermute(v, axis, [(i, (i + by) % size) for i in range(size)])  8.11 us
  transfers between devices with their start and end apart: 9, of which 8 were waited for; matrix products, arithmetic and copies ran while one was open for 0% of the time, Pallas kernels for 16%

profile of v2, /device:TPU:1, one launch (start us, length us, event | category | flops | bytes accessed | tf_op | source)
XLA Modules:
  0.0 160.0 jit_solution(4084293465426797165)
XLA Ops:
  7.9 1.3 copy-done
  9.2 1.3 copy-done.5
  11.8 9.0 %all-to-all-start = ((f32[8,64,128]{2,1,0:T(8,128)}), f32[8,64,128]{2,1,0:T(8,128)}, u32[]{:S(2)}, u32[]{:S(2)}) async-start(f32[8,64,128]{2,1,0:T(8,128)} %copy-done.9), calls=%async_computation | async-start | bytes 524288 | tf_op jit(solution)/shard_map/all_to_all | solution.py:261
  24.3 7.0 %all-to-all-done.y_ref = f32[8,64,128]{2,1,0:T(8,128)} async-done(((f32[8,64,128]{2,1,0:T(8,128)}), f32[8,64,128]{2,1,0:T(8,128)}, u32[]{:S(2)}, u32[]{:S(2)}) %all-to-all-start) | async-done | bytes 262176 | tf_op jit(solution)/shard_map/all_to_all | solution.py:261
  33.2 1.3 shard_map.86
  34.5 4.2 %collective-permute-start = (f32[32,256]{1,0:T(8,128)S(1)}, f32[32,256]{1,0:T(8,128)S(1)}, u32[]{:S(2)}, u32[]{:S(2)}) collective-permute-start(f32[32,256]{1,0:T(8,128)S(1)} %get-tuple-element.27), channel_id=1, source_target_pairs={{0,8},{8,0},{1,9},{9,1},{2,10},{10,2},{3,11},{11,3},{4,12},{12,4},... | collective-permute-start | bytes 98312 | tf_op jit(solution)/shard_map/ppermute | solution.py:250
  39.6 17.1 %all_to_all.30.in_ref = f32[16,32,256]{2,1,0:T(8,128)S(1)} all-to-all(f32[16,32,256]{2,1,0:T(8,128)S(1)} %shard_map.87), channel_id=1, replica_groups=mesh['x'=4,'y'=4,'core'=2,'z'=8] {'x','y'}, dimensions={0} | all-to-all | bytes 1048576 | tf_op jit(solution)/shard_map/all_to_all | solution.py:260
  56.7 2.2 %collective-permute-start.1 = (f32[32,256]{1,0:T(8,128)S(1)}, f32[32,256]{1,0:T(8,128)S(1)}, u32[]{:S(2)}, u32[]{:S(2)}) collective-permute-start(f32[32,256]{1,0:T(8,128)S(1)} %shard_map.88.mine_ref), channel_id=1, source_target_pairs={{0,8},{8,0},{1,9},{9,1},{2,10},{10,2},{3,11},{11,3},{4,12},{12,4},... | collective-permute-start | bytes 98312 | tf_op jit(solution)/shard_map/ppermute | solution.py:250
  61.5 4.1 %all-to-all-start.2 = ((f32[8,96,128]{2,1,0:T(8,128)}), f32[8,96,128]{2,1,0:T(8,128)}, u32[]{:S(2)}, u32[]{:S(2)}) async-start(f32[8,96,128]{2,1,0:T(8,128)} %copy-done.12), calls=%async_computation.2 | async-start | bytes 786432 | tf_op jit(solution)/shard_map/all_to_all | solution.py:261
  66.4 1.5 shard_map.90.ep_ref
  69.0 15.7 %all-to-all-done.2.got_ref = f32[8,96,128]{2,1,0:T(8,128)} async-done(((f32[8,96,128]{2,1,0:T(8,128)}), f32[8,96,128]{2,1,0:T(8,128)}, u32[]{:S(2)}, u32[]{:S(2)}) %all-to-all-start.2) | async-done | bytes 393248 | tf_op jit(solution)/shard_map/all_to_all | solution.py:261
  84.7 1.3 copy-done.4
  85.9 2.3 %shard_map.91 = (f32[4,4,8,1152]{3,2,1,0:T(8,128)S(1)}, f32[4,4,8,1152]{3,2,1,0:T(8,128)S(1)}, f32[64,64]{1,0:T(8,128)S(1)}) custom-call(s32[1]{0:T(128)} %bitcast.core_ref, f32[8,96,128]{2,1,0:T(8,128)} %all-to-all-done.2.got_ref, f32[64,4608]{1,0:T(8,128)S(1)} %copy-done.4, bf16[128,4608]{1,0:T(8,128)(2,1)S(1)} %copy-done.1), custom_call_target="tpu_custom_call" | custom-call | flops 226492416 | bytes 3948548 | tf_op jit(solution)/shard_map/pallas_call | solution.py:61
  88.3 1.2 collective-permute-start.2
  89.4 1.6 %collective-permute-done.2 = f32[4,4,8,1152]{3,2,1,0:T(8,128)S(1)} collective-permute-done((f32[4,4,8,1152]{3,2,1,0:T(8,128)S(1)}, f32[4,4,8,1152]{3,2,1,0:T(8,128)S(1)}, u32[]{:S(2)}, u32[]{:S(2)}) %collective-permute-start.2) | collective-permute-done | bytes 589856 | tf_op jit(solution)/shard_map/ppermute | solution.py:250
  92.0 3.6 %all-to-all-start.3 = ((f32[16,8,1152]{2,1,0:T(8,128)}), f32[16,8,1152]{2,1,0:T(8,128)S(1)}, u32[]{:S(2)}, u32[]{:S(2)}) async-start(f32[16,8,1152]{2,1,0:T(8,128)} %shard_map.92), calls=%async_computation.3 | async-start | bytes 1179648 | tf_op jit(solution)/shard_map/all_to_all | solution.py:260
  95.6 6.3 %shard_map.93 = (f32[64,64]{1,0:T(8,128)S(1)}, f32[64,256]{1,0:T(8,128)}) custom-call(f32[64,64]{1,0:T(8,128)S(1)} %get-tuple-element.33.gram_ref, f32[64,256]{1,0:T(8,128)S(1)} %copy-done.16), custom_call_target="tpu_custom_call" | custom-call | flops 300000000 | bytes 163840 | tf_op jit(solution)/shard_map/pallas_call | solution.py:61
  101.9 4.4 %all-to-all-done.3.in_ref = f32[16,8,1152]{2,1,0:T(8,128)S(1)} async-done(((f32[16,8,1152]{2,1,0:T(8,128)}), f32[16,8,1152]{2,1,0:T(8,128)S(1)}, u32[]{:S(2)}, u32[]{:S(2)}) %all-to-all-start.3) | async-done | bytes 589856 | tf_op jit(solution)/shard_map/all_to_all | solution.py:260
  106.3 17.2 %all_to_all.31.in_ref = f32[8,8,1152]{2,1,0:T(8,128)S(1)} all-to-all(f32[8,8,1152]{2,1,0:T(8,128)S(1)} %shard_map.94), channel_id=1, replica_groups=mesh['x'=4,'y'=4,'core'=2,'z'=8] {'z'}, dimensions={0} | all-to-all | bytes 589824 | tf_op jit(solution)/shard_map/all_to_all | solution.py:261
  124.3 5.3 %all-to-all-start.5 = ((f32[16,8,1152]{2,1,0:T(8,128)}), f32[16,8,1152]{2,1,0:T(8,128)S(1)}, u32[]{:S(2)}, u32[]{:S(2)}) async-start(f32[16,8,1152]{2,1,0:T(8,128)} %shard_map.95), calls=%async_computation.5 | async-start | bytes 1179648 | tf_op jit(solution)/shard_map/all_to_all | solution.py:260
  129.7 4.6 %all-gather.2.cloned.1.call-done.refs_0_ = bf16[1024,4608]{1,0:T(8,128)(2,1)} async-done(((bf16[128,4608]{1,0:T(8,128)(2,1)}), bf16[1024,4608]{1,0:T(8,128)(2,1)}) %all-gather.2.cloned.1.call-update) | async-done | bytes 9437200 | tf_op jit(solution)/shard_map/all_gather | solution.py:269
  134.3 11.0 %shard_map.96 = (f32[256,4608]{1,0:T(8,128)}, bf16[1024,256]{1,0:T(8,128)(2,1)}) custom-call(bf16[1024,4608]{1,0:T(8,128)(2,1)} %all-gather.2.cloned.1.call-done.refs_0_, bf16[256,1024]{1,0:T(8,128)(2,1)} %copy-done.10, bf16[1,256,4608]{2,1,0:T(8,128)(2,1)} %refs_2_.1, bf16[256,4608]{1,0:T(8,128)(2,1)} %refs_3_.1), custom_call_target="tpu_custom_call" | custom-call | flops 4831838208 | bytes 19922944 | tf_op jit(solution)/shard_map/pallas_call | solution.py:61
  145.8 1.6 %collective-permute-done.3 = f32[16,8,1152]{2,1,0:T(8,128)S(1)} collective-permute-done((f32[16,8,1152]{2,1,0:T(8,128)S(1)}, f32[16,8,1152]{2,1,0:T(8,128)S(1)}, u32[]{:S(2)}, u32[]{:S(2)}) %collective-permute-start.3) | collective-permute-done | bytes 589856 | tf_op jit(solution)/shard_map/ppermute | solution.py:250
  147.5 5.7 %shard_map.97 = (bf16[1,256,4608]{2,1,0:T(8,128)(2,1)}, f32[64,4608]{1,0:T(8,128)}) custom-call(s32[1]{0:T(128)} %bitcast.core_ref, f32[4,4,8,1152]{3,2,1,0:T(8,128)S(1)} %bitcast.10, f32[4,4,8,1152]{3,2,1,0:T(8,128)S(1)} %bitcast.11, f32[64,64]{1,0:T(8,128)S(1)} %get-tuple-element.42.linv_ref, f32[64,256]{1,0:T(8,128)S(1)} %copy-done.13, ...), custom_call_target="tpu_custom_call" | custom-call | flops 452984832 | bytes 9519108 | tf_op jit(solution)/shard_map/pallas_call | solution.py:61
  (49 shorter events, 15.1 us)
Async XLA Ops:
  7.2 13.7 %copy-start.6 = (f32[4608,64]{0,1:T(8,128)S(1)}, f32[4608,64]{0,1:T(8,128)}, u32[]{:S(2)}) copy-start(f32[4608,64]{0,1:T(8,128)} %param.9) | copy-start | bytes 3538948
  7.2 127.2 %all-gather.2.cloned.1.call-start = ((), (), s32[]{:S(2)}) async-start(), calls=%async_computation.6 | async-start | bytes 10616832 | tf_op jit(solution)/shard_map/all_gather | solution.py:269
  7.9 1.3 copy-start
  9.2 1.3 copy-start.5
  10.5 10.4 %copy-start.2 = (bf16[1,256,4608]{2,1,0:T(8,128)(2,1)S(1)}, bf16[1,256,4608]{2,1,0:T(8,128)(2,1)}, u32[]{:S(2)}) copy-start(bf16[1,256,4608]{2,1,0:T(8,128)(2,1)} %refs_2_.1) | copy-start | bytes 7077892
  11.8 19.5 %all-to-all-start = ((f32[8,64,128]{2,1,0:T(8,128)}), f32[8,64,128]{2,1,0:T(8,128)}, u32[]{:S(2)}, u32[]{:S(2)}) async-start(f32[8,64,128]{2,1,0:T(8,128)} %copy-done.9), calls=%async_computation | async-start | bytes 524288 | tf_op jit(solution)/shard_map/all_to_all | solution.py:261
  20.8 1.0 copy-start.7
  22.8 0.8 copy-start.10
  31.3 1.0 copy-start.8
  32.3 0.8 copy-start.18
  33.2 26.6 %copy-start.11 = (bf16[256,1024]{1,0:T(8,128)(2,1)S(1)}, bf16[256,1024]{1,0:T(8,128)(2,1)}, u32[]{:S(2)}) copy-start(bf16[256,1024]{1,0:T(8,128)(2,1)} %copy-done.10) | copy-start | bytes 1572868
  34.5 5.1 %collective-permute-start = (f32[32,256]{1,0:T(8,128)S(1)}, f32[32,256]{1,0:T(8,128)S(1)}, u32[]{:S(2)}, u32[]{:S(2)}) collective-permute-start(f32[32,256]{1,0:T(8,128)S(1)} %get-tuple-element.27), channel_id=1, source_target_pairs={{0,8},{8,0},{1,9},{9,1},{2,10},{10,2},{3,11},{11,3},{4,12},{12,4},... | collective-permute-start | bytes 98312 | tf_op jit(solution)/shard_map/ppermute | solution.py:250
  56.7 3.0 %collective-permute-start.1 = (f32[32,256]{1,0:T(8,128)S(1)}, f32[32,256]{1,0:T(8,128)S(1)}, u32[]{:S(2)}, u32[]{:S(2)}) collective-permute-start(f32[32,256]{1,0:T(8,128)S(1)} %shard_map.88.mine_ref), channel_id=1, source_target_pairs={{0,8},{8,0},{1,9},{9,1},{2,10},{10,2},{3,11},{11,3},{4,12},{12,4},... | collective-permute-start | bytes 98312 | tf_op jit(solution)/shard_map/ppermute | solution.py:250
  59.7 24.9 %copy-start.1 = (bf16[128,4608]{1,0:T(8,128)(2,1)S(1)}, bf16[128,4608]{1,0:T(8,128)(2,1)}, u32[]{:S(2)}) copy-start(bf16[128,4608]{1,0:T(8,128)(2,1)} %g_ref.3) | copy-start | bytes 3538948
  61.5 23.2 %all-to-all-start.2 = ((f32[8,96,128]{2,1,0:T(8,128)}), f32[8,96,128]{2,1,0:T(8,128)}, u32[]{:S(2)}, u32[]{:S(2)}) async-start(f32[8,96,128]{2,1,0:T(8,128)} %copy-done.12), calls=%async_computation.2 | async-start | bytes 786432 | tf_op jit(solution)/shard_map/all_to_all | solution.py:261
  65.6 0.8 copy-start.15
  67.9 1.0 copy-start.3
  84.7 1.3 copy-start.4
  85.9 9.6 %copy-start.16 = (f32[64,256]{1,0:T(8,128)S(1)}, f32[64,256]{1,0:T(8,128)}, u32[]{:S(2)}) copy-start(f32[64,256]{1,0:T(8,128)} %copy-done.14) | copy-start | bytes 196612
  88.3 2.8 %collective-permute-start.2 = (f32[4,4,8,1152]{3,2,1,0:T(8,128)S(1)}, f32[4,4,8,1152]{3,2,1,0:T(8,128)S(1)}, u32[]{:S(2)}, u32[]{:S(2)}) collective-permute-start(f32[4,4,8,1152]{3,2,1,0:T(8,128)S(1)} %get-tuple-element.32), channel_id=1, source_target_pairs={{0,8},{8,0},{1,9},{9,1},{2,10},{10,2},{3,11},{11,3},{4,12},{12,4},... | collective-permute-start | bytes 1769480 | tf_op jit(solution)/shard_map/ppermute | solution.py:250
  92.0 14.3 %all-to-all-start.3 = ((f32[16,8,1152]{2,1,0:T(8,128)}), f32[16,8,1152]{2,1,0:T(8,128)S(1)}, u32[]{:S(2)}, u32[]{:S(2)}) async-start(f32[16,8,1152]{2,1,0:T(8,128)} %shard_map.92), calls=%async_computation.3 | async-start | bytes 1179648 | tf_op jit(solution)/shard_map/all_to_all | solution.py:260
  124.3 21.0 %all-to-all-start.5 = ((f32[16,8,1152]{2,1,0:T(8,128)}), f32[16,8,1152]{2,1,0:T(8,128)S(1)}, u32[]{:S(2)}, u32[]{:S(2)}) async-start(f32[16,8,1152]{2,1,0:T(8,128)} %shard_map.95), calls=%async_computation.5 | async-start | bytes 1179648 | tf_op jit(solution)/shard_map/all_to_all | solution.py:260
  129.7 17.8 %copy-start.13 = (f32[64,256]{1,0:T(8,128)S(1)}, f32[64,256]{1,0:T(8,128)}, u32[]{:S(2)}) copy-start(f32[64,256]{1,0:T(8,128)} %get-tuple-element.40.pf_ref) | copy-start | bytes 196612
  145.3 2.2 %collective-permute-start.3 = (f32[16,8,1152]{2,1,0:T(8,128)S(1)}, f32[16,8,1152]{2,1,0:T(8,128)S(1)}, u32[]{:S(2)}, u32[]{:S(2)}) collective-permute-start(f32[16,8,1152]{2,1,0:T(8,128)S(1)} %all-to-all-done.5), channel_id=1, source_target_pairs={{0,8},{8,0},{1,9},{9,1},{2,10},{10,2},{3,11},{11,3},{4,12},{12,4},... | collective-permute-start | bytes 1769480 | tf_op jit(solution)/shard_map/ppermute | solution.py:250
  (4 other events, 2.7 us)
Sparse Core Ops, SparseCore 0:
  9.8 124.4 all-gather.1

commit v3 on v2

v3 whole, which is shorter than its diff:
```python
import jax
import jax.numpy as jnp
from jax import lax
from jax.experimental import pallas as pl
from jax.experimental.pallas import tpu as pltpu
from jax.sharding import Mesh
from jax.sharding import PartitionSpec as P

D, K, NZ, NXY = 4608, 64, 8, 16
TILE = 1152
FAR = (7, 8, 9, 10)
NEAR = tuple(h for h in range(16) if h not in FAR)
NT = D // TILE
HI = lax.Precision.HIGHEST
F32, BF16 = jnp.float32, jnp.bfloat16
SMEM = pl.BlockSpec(memory_space=pltpu.SMEM)


def split3(v):
    hi = v.astype(BF16)
    rest = v - hi.astype(F32)
    mid = rest.astype(BF16)
    low = (rest - mid.astype(F32)).astype(BF16)
    return jnp.concatenate([hi, mid, low], axis=0)


def fold3(v):
    n = v.shape[0] // 3
    return v[:n] + v[n : 2 * n] + v[2 * n :]


def dot(a, b, ca, cb, precision=None):
    return lax.dot_general(
        a, b, (((ca,), (cb,)), ((), ())), precision=precision, preferred_element_type=F32
    )


def whole(shape):
    return pl.BlockSpec(shape, lambda *_: (0,) * len(shape))


def out(shape, dtype=F32):
    return jax.ShapeDtypeStruct(shape, dtype)


def call(
    kernel, operands, in_specs, out_shapes, out_specs, grid=(1,), flops=0, scratch=(), mib=16,
    hbm_in=(), hbm_out=(), size=0,
):
    operands = [
        pltpu.with_memory_space_constraint(v, pltpu.HBM) if i in hbm_in else v
        for i, v in enumerate(operands)
    ]
    out_shapes = [
        pltpu.HBM(s.shape, s.dtype) if i in hbm_out else s for i, s in enumerate(out_shapes)
    ]
    return pl.pallas_call(
        kernel,
        grid=grid,
        in_specs=in_specs,
        out_specs=out_specs,
        out_shape=out_shapes,
        scratch_shapes=scratch,
        compiler_params=pltpu.CompilerParams(vmem_limit_bytes=mib * 1024 * 1024),
        cost_estimate=pl.CostEstimate(flops=flops, bytes_accessed=size, transcendentals=0),
    )(*operands)


def simple(kernel, operands, out_shapes, **kwargs):
    specs = [SMEM if v.dtype == jnp.int32 else whole(v.shape) for v in operands]
    return call(kernel, operands, specs, out_shapes, [whole(s.shape) for s in out_shapes], **kwargs)


def rows_kernel(q_ref, g_ref, y_ref, ga_ref, gb_ref, acc_ref):
    rows = g_ref[...]
    ga_ref[...] = rows[:64]
    gb_ref[...] = rows[64:]
    accumulate(acc_ref, fold3(dot(split3(q_ref[...]), rows, 1, 1)))

    @pl.when(pl.program_id(0) == pl.num_programs(0) - 1)
    def _():
        y = acc_ref[...]
        for j in range(NZ):
            y_ref[j] = y


def error_rows_kernel(q_ref, e_ref, out_ref):
    out_ref[...] = fold3(dot(split3(q_ref[...]), e_ref[0], 1, 1))


def turn_kernel(z_ref, a_ref, near_ref, far_ref):
    parts = []
    for hops in range(NZ):
        src = lax.rem(z_ref[0] + (NZ - hops), NZ)
        parts.append(a_ref[pl.ds(pl.multiple_of(src * 128, 128), 128), :].T)
    turned = jnp.concatenate(parts, axis=1)
    near_ref[...] = jnp.concatenate([turned[:, :448], turned[:, 704:]], axis=1)
    far_ref[...] = turned[:, 448:704]


def pick(core_ref, a, b):
    return jnp.where(core_ref[0] == 0, a, b)


def left_kernel(core_ref, y_ref, a_ref, eq_ref, mine_ref, other_ref):
    y = jnp.concatenate([y_ref[j] for j in range(NZ)], axis=1)
    p = fold3(dot(split3(y), a_ref[...], 1, 0)) + eq_ref[...]
    mine_ref[...] = pick(core_ref, p[:32], p[32:])
    other_ref[...] = pick(core_ref, p[32:], p[:32])


def total(ref):
    acc = ref[0]
    for j in range(1, ref.shape[0]):
        acc = acc + ref[j]
    return acc


def total_kernel(in_ref, out_ref):
    out_ref[...] = total(in_ref)


def spread_kernel(in_ref, out_ref):
    acc = total(in_ref)
    for j in range(out_ref.shape[0]):
        out_ref[j] = acc


def pair_kernel(a_ref, b_ref, out_ref):
    acc = a_ref[...] + b_ref[...]
    for j in range(out_ref.shape[0]):
        out_ref[j] = acc


def add_kernel(a_ref, b_ref, out_ref):
    out_ref[...] = a_ref[...] + b_ref[...]


def terms_kernel(core_ref, mine_ref, other_ref, a_ref, p_ref, sent_ref):
    mine, other = mine_ref[...], other_ref[...]
    p = jnp.concatenate([pick(core_ref, mine, other), pick(core_ref, other, mine)], axis=0)
    p_ref[...] = p
    terms = fold3(dot(split3(p), a_ref[...], 1, 1))
    gram = dot(p, p, 1, 1, HI)
    packed = jnp.concatenate([gram[:32], gram[32:]], axis=1)
    for j in range(NZ):
        sent_ref[j, :K] = terms[:, 128 * j : 128 * (j + 1)]
        sent_ref[j, K:] = packed


def error_terms_kernel(p_ref, e_ref, out_ref):
    out_ref[...] = fold3(dot(split3(p_ref[...]), e_ref[0], 1, 0))


def right_kernel(core_ref, got_ref, ep_ref, g_ref, mine_ref, other_ref, gram_ref):
    got = total(got_ref)
    gram_ref[...] = jnp.concatenate([got[K:, :K], got[K:, K:]], axis=0)
    q = fold3(dot(split3(got[:K]), g_ref[...], 1, 0)) + ep_ref[...]
    mine_ref[:, 0] = pick(core_ref, q[:32], q[32:]).reshape(4, 8, TILE)
    other_ref[:, 0] = pick(core_ref, q[32:], q[:32]).reshape(4, 8, TILE)


def factor_kernel(gram_ref, p_ref, linv_ref, pf_ref):
    row = lax.broadcasted_iota(jnp.int32, (K, K), 0)
    lane = lax.broadcasted_iota(jnp.int32, (K, K), 1)
    eye = jnp.where(row == lane, 1.0, 0.0)
    both = jnp.concatenate([gram_ref[...], eye], axis=1)
    tiles = [both[8 * t : 8 * t + 8] for t in range(8)]
    sub = lax.broadcasted_iota(jnp.int32, (8, 128), 0)
    for i in range(K):
        b, r = divmod(i, 8)
        pivot = tiles[b][r : r + 1]
        scaled = pivot * (1.0 / pivot[:, i : i + 1])
        for t in range(b, 8):
            factor = jnp.broadcast_to(tiles[t][:, i : i + 1], (8, 128))
            if t == b:
                factor = jnp.where(sub > r, factor, 0.0)
            tiles[t] = tiles[t] - factor * scaled
    both = jnp.concatenate(tiles, axis=0)
    pivots = jnp.sum(both[:, :K] * eye, axis=1, keepdims=True)
    linv = both[:, K:] * lax.rsqrt(pivots)
    linv_ref[...] = linv
    pf_ref[...] = dot(linv, p_ref[...], 1, 0, HI)


def place(grad_ref, z_ref, halves, acc_ref):
    for slot, half in enumerate(halves):
        src = lax.rem(z_ref[0] + (NZ - half // 2), NZ) * 128 + (half % 2) * 64
        grad_ref[pl.ds(pl.multiple_of(src, 64), 64), :] = acc_ref[
            64 * slot : 64 * (slot + 1)
        ].astype(BF16)


def accumulate(acc_ref, part):
    @pl.when(pl.program_id(0) == 0)
    def _():
        acc_ref[...] = part

    @pl.when(pl.program_id(0) > 0)
    def _():
        acc_ref[...] += part


def near_kernel(z_ref, *refs):
    blocks = refs[:-6]
    a_ref, e_ref, w_ref, merged_ref, grad_ref, acc_ref = refs[-6:]
    rows = jnp.concatenate([b[...] for b in blocks], axis=0)
    merged_ref[...] = jnp.dot(
        a_ref[...], rows, preferred_element_type=F32
    ) + e_ref[0].astype(F32)
    accumulate(acc_ref, dot(rows, w_ref[...], 1, 1))

    @pl.when(pl.program_id(0) == pl.num_programs(0) - 1)
    def _():
        place(grad_ref, z_ref, NEAR, acc_ref)


def tail_kernel(z_ref, core_ref, *refs):
    blocks = refs[:4]
    a_ref, w_ref, sum_ref, near_ref, mine_ref, other_ref, linv_ref, pf_ref = refs[4:12]
    err_ref, q_ref, grad_ref, acc_ref = refs[12:]
    mine = mine_ref[:, 0].reshape(32, TILE)
    other = other_ref[:, 0].reshape(32, TILE)
    raw = jnp.concatenate([pick(core_ref, mine, other), pick(core_ref, other, mine)], axis=0)
    qf = dot(linv_ref[...], raw, 1, 0, HI) * (1.0 / 32)
    q_ref[...] = qf
    pf = pf_ref[...]
    pf_hi = pf.astype(BF16)
    pf_lo = (pf - pf_hi.astype(F32)).astype(BF16)
    q_hi = qf.astype(BF16)
    q_lo = (qf - q_hi.astype(F32)).astype(BF16)
    low = dot(
        jnp.concatenate([pf_hi, pf_hi, pf_lo], axis=0),
        jnp.concatenate([q_hi, q_lo, q_hi], axis=0), 0, 0,
    )
    rows = jnp.concatenate([b[...] for b in blocks], axis=0)
    merged = sum_ref[...] + jnp.dot(a_ref[...], rows, preferred_element_type=F32)
    err_ref[0] = (merged - low).astype(BF16)
    accumulate(acc_ref, dot(rows, w_ref[...], 1, 1))

    @pl.when(pl.program_id(0) == pl.num_programs(0) - 1)
    def _():
        grad_ref[...] = near_ref[...]
        place(grad_ref, z_ref, FAR, acc_ref)


def shift(v, axis, size, by):
    return lax.ppermute(v, axis, [(i, (i + by) % size) for i in range(size)])


def on_device(grad_out, attn_out, out_weight, error_prev, q_prev):
    z = lax.axis_index("z").astype(jnp.int32).reshape(1)
    core = lax.axis_index("core").astype(jnp.int32).reshape(1)
    up = lambda v: shift(v, "z", NZ, 1)
    down = lambda v: shift(v, "z", NZ, NZ - 1)
    swap = lambda v: shift(v, "core", 2, 1)
    plane = lambda v: lax.all_to_all(v, ("x", "y"), 0, 0)
    column = lambda v: lax.all_to_all(v, "z", 0, 0)
    tied = lambda *v: lax.optimization_barrier(v)
    q_prev_t = q_prev.T
    tile = lambda rows: pl.BlockSpec((rows, TILE), lambda i: (0, i))
    err_tile = pl.BlockSpec((1, 256, TILE), lambda i: (0, 0, i))
    chunk_tile = pl.BlockSpec((4, 1, 8, TILE), lambda i: (0, i, 0, 0))
    chunks = (NXY, 8, TILE)

    y, ga, gb = call(
        rows_kernel, [q_prev_t, grad_out], [tile(K), tile(128)],
        [out((NZ, K, 128)), out((64, D), BF16), out((64, D), BF16)],
        [whole((NZ, K, 128)), tile(64), tile(64)], grid=(NT,),
        scratch=[pltpu.VMEM((K, 128), F32)], hbm_in=(0, 1), hbm_out=(1, 2),
    )
    y = column(y)
    (eq_t,) = simple(
        error_rows_kernel, [q_prev_t, error_prev], [out((K, 256))]
    )
    u1a, d1b = up(ga), down(gb)
    u1b, d1a = up(gb), down(ga)
    mine, other = simple(
        left_kernel, [core, y, attn_out, eq_t], [out((32, 256)), out((32, 256))]
    )
    (mine,) = simple(pair_kernel, [mine, swap(other)], [out((NXY, 32, 256))])
    mine, shadow = tied(mine, attn_out)
    mine = plane(mine)
    a_near, a_far = simple(
        turn_kernel, [z, shadow], [out((256, 768), BF16), out((256, 256), BF16)]
    )
    a_near, u1a, d1b, u1b, d1a = tied(a_near, u1a, d1b, u1b, d1a)
    u2a, d2b = up(u1a), down(d1b)
    u2b, d2a = up(u1b), down(d1a)
    mine, a_near, a_far = tied(mine, a_near, a_far)
    (mine,) = simple(total_kernel, [mine], [out((32, 256))])

    p_t, sent = simple(
        terms_kernel, [core, mine, swap(mine), attn_out], [out((K, 256)), out((NZ, 96, 128))]
    )
    got = column(sent)
    (ep,) = call(
        error_terms_kernel, [p_t, error_prev], [whole((K, 256)), err_tile], [out((K, D))],
        [tile(K)], grid=(NT,)
    )
    mine, other, gram = call(
        right_kernel, [core, got, ep, grad_out],
        [SMEM, whole((NZ, 96, 128)), tile(K), tile(128)],
        [out((4, NT, 8, TILE)), out((4, NT, 8, TILE)), out((K, K))],
        [chunk_tile, chunk_tile, whole((K, K))], grid=(NT,), hbm_in=(3,),
    )

    mine, other, u2a, d2b = tied(mine, swap(other), u2a, d2b)
    (mine,) = simple(add_kernel, [mine.reshape(chunks), other.reshape(chunks)], [out(chunks)])
    mine, gram, p_t = tied(mine, gram, p_t)
    mine = plane(mine)
    linv, pf_t = simple(factor_kernel, [gram, p_t], [out((K, K)), out((K, 256))])
    linv, u2a, d2b = tied(linv, u2a, d2b)
    u3a, d3b = up(u2a), down(d2b)
    mine, linv, pf_t = tied(mine, linv, pf_t)
    (mine,) = simple(spread_kernel, [mine], [out((NZ, 8, TILE))])
    mine, u2b, d2a = tied(mine, u2b, d2a)
    u3b, d3a = up(u2b), down(d2a)
    far_a, far_b = up(u3a), down(d3b)
    mine = column(mine)
    (mine,) = simple(spread_kernel, [mine], [out(chunks)])
    mine, a_near, u3a, d3b = tied(mine, a_near, u3a, d3b)
    mine = plane(mine)
    a_near, u3b, d3a = tied(a_near, u3b, d3a)
    near = [grad_out, u1a, u1b, u2a, u2b, u3a, d3b, d2a, d2b, d1a, d1b]
    specs = lambda blocks, a: [tile(v.shape[0]) for v in blocks] + [whole(a.shape)]
    merged, grad_near = call(
        near_kernel, [z, *near, a_near, error_prev, out_weight],
        [SMEM] + specs(near, a_near) + [err_tile, tile(256)],
        [out((256, D)), out((1024, 256), BF16)], [tile(256), whole((1024, 256))], grid=(NT,),
        scratch=[pltpu.VMEM((768, 256), F32)], mib=28,
        hbm_in=range(1, len(near) + 4), hbm_out=(0, 1),
    )
    mine, merged, grad_near = tied(mine, merged, grad_near)
    other = swap(mine)
    far = [u3b, far_a, far_b, d3a]
    error_new, q_t, grad_attn = call(
        tail_kernel,
        [z, core, *far, a_far, out_weight, merged, grad_near, mine.reshape(4, NT, 8, TILE),
         other.reshape(4, NT, 8, TILE), linv, pf_t],
        [SMEM, SMEM] + specs(far, a_far) + [tile(256), tile(256), whole((1024, 256)), chunk_tile,
         chunk_tile, whole((K, K)), whole((K, 256))],
        [out((1, 256, D), BF16), out((K, D)), out((1024, 256), BF16)],
        [err_tile, tile(K), whole((1024, 256))], grid=(NT,),
        scratch=[pltpu.VMEM((256, 256), F32)], mib=28, hbm_in=range(2, 10), hbm_out=(0, 1, 2),
    )
    return grad_attn, pf_t.T, q_t.T, error_new


def solution(mesh):
    fine = Mesh(mesh.devices.reshape(4, 4, 2, 8), ("x", "y", "core", "z"))
    dp = ("x", "y", "core")
    in_specs = (P(dp + ("z",), None), P(dp, "z"), P("z", None), P(dp, "z", None), P())
    out_specs = (P(dp, "z"), P("z", None), P(), P(dp, "z", None))
    return jax.shard_map(
        on_device, mesh=fine, in_specs=in_specs, out_specs=out_specs, check_vma=False
    )
```

time: 161 us -> 155 us (0.963)
  starting transfers between devices: 30.2 us -> 68.3 us
  blocking collectives: 34.2 us -> 0 us
  between operations: 14.2 us -> 1 us
  local copies, waits for them, and re-layouts: 12.1 us -> 4.94 us
  Pallas kernels: 31.9 us -> 38.8 us
  waiting for transfers between devices: 37.4 us -> 41.4 us
    all_to_all x2 -> x0, blocking collectives: 34.2 us -> none  [the longest x1 17.2 us: on_device(): column = lambda v: lax.all_to_all(v, 'z', 0, 0)]
    ppermute x4 -> x18, starting transfers between devices: 8.11 us -> 28.5 us  [shift(): return lax.ppermute(v, axis, [(i, (i + by) % size) for i in range(size)])]
    ppermute x4 -> x18, waiting for transfers between devices: 4.98 us -> 19 us  [shift(): return lax.ppermute(v, axis, [(i, (i + by) % size) for i in range(size)])]
    all_to_all x2 -> x3, starting transfers between devices: 8.91 us -> 19.9 us  [on_device(): plane = lambda v: lax.all_to_all(v, ('x', 'y'), 0, 0)]
    unnamed x38 -> x28, local copies, waits for them, and re-layouts: 12.1 us -> 4.94 us
    pallas_call x14 -> x15, Pallas kernels: 31.9 us -> 38.8 us  [call(): pl.pallas_call(kernel, grid=grid, in_specs=in_specs, out_specs=out_specs,...]
    all_to_all x2 -> x3, starting transfers between devices: 13.1 us -> 19.8 us  [on_device(): column = lambda v: lax.all_to_all(v, 'z', 0, 0)]
    all_gather x1 -> x0, waiting for transfers between devices: 4.64 us -> none  [on_device(): lax.all_gather(grad_out[:, i * width:(i + 1) * width], 'z', axis=0, tiled...]
  transfers between devices with their start and end apart: 9 -> 24, of which waited for: 8 -> 10; matrix products, arithmetic and copies ran while one was open for 0% -> 0% of each run, Pallas kernels for 16% -> 16%
where the time goes in v3:
time: 155 us; the launch traced here: 154 us
  starting transfers between devices  68.3 us (44%)
  waiting for transfers between devices  41.4 us (27%)
  Pallas kernels  38.8 us (25%)
  local copies, waits for them, and re-layouts  4.94 us (3%)
    pallas_call x15, Pallas kernels, call(): pl.pallas_call(kernel, grid=grid, in_specs=in_specs, out_specs=out_specs,...  38.8 us
    ppermute x18, starting transfers between devices, shift(): return lax.ppermute(v, axis, [(i, (i + by) % size) for i in range(size)])  28.5 us
    all_to_all x3, waiting for transfers between devices, on_device(): column = lambda v: lax.all_to_all(v, 'z', 0, 0)  21.7 us
    all_to_all x3, starting transfers between devices, on_device(): plane = lambda v: lax.all_to_all(v, ('x', 'y'), 0, 0)  19.9 us
    all_to_all x3, starting transfers between devices, on_device(): column = lambda v: lax.all_to_all(v, 'z', 0, 0)  19.8 us
    ppermute x18, waiting for transfers between devices, shift(): return lax.ppermute(v, axis, [(i, (i + by) % size) for i in range(size)])  19 us
    unnamed x28, local copies, waits for them, and re-layouts  4.94 us
  transfers between devices with their start and end apart: 24, of which 10 were waited for; matrix products, arithmetic and copies ran while one was open for 0% of the time, Pallas kernels for 16%

profile of v3, /device:TPU:1, one launch (start us, length us, event | category | flops | bytes accessed | tf_op | source)
XLA Modules:
  0.0 154.4 jit_solution(14500218570051279420)
XLA Ops:
  0.6 4.4 %shard_map.84 = (f32[8,64,128]{2,1,0:T(8,128)}, bf16[64,4608]{1,0:T(8,128)(2,1)}, bf16[64,4608]{1,0:T(8,128)(2,1)}) custom-call(f32[64,4608]{1,0:T(8,128)} %bitcast.9, bf16[128,4608]{1,0:T(8,128)(2,1)} %refs_0_.1), custom_call_target="tpu_custom_call" | custom-call | tf_op jit(solution)/shard_map/pallas_call | solution.py:57
  5.1 9.1 %all-to-all-start = ((f32[8,64,128]{2,1,0:T(8,128)}), f32[8,64,128]{2,1,0:T(8,128)S(1)}, u32[]{:S(2)}, u32[]{:S(2)}) async-start(f32[8,64,128]{2,1,0:T(8,128)} %get-tuple-element.59), calls=%async_computation | async-start | bytes 524288 | tf_op jit(solution)/shard_map/all_to_all | solution.py:258
  17.2 2.5 %collective-permute-start.4 = (bf16[64,4608]{1,0:T(8,128)(2,1)}, bf16[64,4608]{1,0:T(8,128)(2,1)}, u32[]{:S(2)}, u32[]{:S(2)}) collective-permute-start(bf16[64,4608]{1,0:T(8,128)(2,1)} %get-tuple-element.65), channel_id=1, source_target_pairs={{0,7},{1,0},{2,1},{3,2},{4,3},{5,4},{6,5},{7,6},{8,15},{9,8},{10,9... | collective-permute-start | bytes 1769480 | tf_op jit(solution)/shard_map/ppermute | solution.py:248
  21.8 3.0 %all-to-all-done.y_ref = f32[8,64,128]{2,1,0:T(8,128)S(1)} async-done(((f32[8,64,128]{2,1,0:T(8,128)}), f32[8,64,128]{2,1,0:T(8,128)S(1)}, u32[]{:S(2)}, u32[]{:S(2)}) %all-to-all-start) | async-done | bytes 262176 | tf_op jit(solution)/shard_map/all_to_all | solution.py:258
  25.1 3.1 %collective-permute-start = (f32[32,256]{1,0:T(8,128)S(1)}, f32[32,256]{1,0:T(8,128)S(1)}, u32[]{:S(2)}, u32[]{:S(2)}) collective-permute-start(f32[32,256]{1,0:T(8,128)S(1)} %get-tuple-element.61), channel_id=1, source_target_pairs={{0,8},{8,0},{1,9},{9,1},{2,10},{10,2},{3,11},{11,3},{4,12},{12,4},... | collective-permute-start | bytes 98312 | tf_op jit(solution)/shard_map/ppermute | solution.py:248
  29.9 6.8 %all-to-all-start.1 = ((f32[16,32,256]{2,1,0:T(8,128)}), f32[16,32,256]{2,1,0:T(8,128)S(1)}, u32[]{:S(2)}, u32[]{:S(2)}) async-start(f32[16,32,256]{2,1,0:T(8,128)} %copy-done.3), calls=%async_computation.1 | async-start | bytes 1048576 | tf_op jit(solution)/shard_map/all_to_all | solution.py:257
  38.4 9.9 %collective-permute-done.3.refs_2_ = bf16[64,4608]{1,0:T(8,128)(2,1)} collective-permute-done((bf16[64,4608]{1,0:T(8,128)(2,1)}, bf16[64,4608]{1,0:T(8,128)(2,1)}, u32[]{:S(2)}, u32[]{:S(2)}) %collective-permute-start.3) | collective-permute-done | bytes 589856 | tf_op jit(solution)/shard_map/ppermute | solution.py:248
  48.4 1.5 collective-permute-start.5
  52.5 4.3 %all-to-all-start.2 = ((f32[8,96,128]{2,1,0:T(8,128)}), f32[8,96,128]{2,1,0:T(8,128)}, u32[]{:S(2)}, u32[]{:S(2)}) async-start(f32[8,96,128]{2,1,0:T(8,128)} %get-tuple-element.70), calls=%async_computation.2 | async-start | bytes 786432 | tf_op jit(solution)/shard_map/all_to_all | solution.py:258
  60.3 1.5 shard_map.91.ep_ref
  61.9 9.8 %all-to-all-done.2.got_ref = f32[8,96,128]{2,1,0:T(8,128)} async-done(((f32[8,96,128]{2,1,0:T(8,128)}), f32[8,96,128]{2,1,0:T(8,128)}, u32[]{:S(2)}, u32[]{:S(2)}) %all-to-all-start.2) | async-done | bytes 393248 | tf_op jit(solution)/shard_map/all_to_all | solution.py:258
  71.7 3.0 %shard_map.92 = (f32[4,4,8,1152]{3,2,1,0:T(8,128)S(1)}, f32[4,4,8,1152]{3,2,1,0:T(8,128)S(1)}, f32[64,64]{1,0:T(8,128)S(1)}) custom-call(s32[1]{0:T(128)} %bitcast.1.core_ref, f32[8,96,128]{2,1,0:T(8,128)} %all-to-all-done.2.got_ref, f32[64,4608]{1,0:T(8,128)S(1)} %shard_map.91.ep_ref, bf16[128,4608]{1,0:T(8,128)(2,1)} %refs_0_.1), custom_call_target="tpu_custom_call" | custom-call | tf_op jit(solution)/shard_map/pallas_call | solution.py:57
  77.1 4.0 %collective-permute-done.7.refs_3_ = bf16[64,4608]{1,0:T(8,128)(2,1)} collective-permute-done((bf16[64,4608]{1,0:T(8,128)(2,1)}, bf16[64,4608]{1,0:T(8,128)(2,1)}, u32[]{:S(2)}, u32[]{:S(2)}) %collective-permute-start.7) | collective-permute-done | bytes 589856 | tf_op jit(solution)/shard_map/ppermute | solution.py:248
  82.0 6.8 %all-to-all-start.3 = ((f32[16,8,1152]{2,1,0:T(8,128)}), f32[16,8,1152]{2,1,0:T(8,128)S(1)}, u32[]{:S(2)}, u32[]{:S(2)}) async-start(f32[16,8,1152]{2,1,0:T(8,128)} %shard_map.93), calls=%async_computation.3 | async-start | bytes 1179648 | tf_op jit(solution)/shard_map/all_to_all | solution.py:257
  88.7 6.3 %shard_map.94 = (f32[64,64]{1,0:T(8,128)S(1)}, f32[64,256]{1,0:T(8,128)}) custom-call(f32[64,64]{1,0:T(8,128)S(1)} %get-tuple-element.80.gram_ref, f32[64,256]{1,0:T(8,128)S(1)} %copy-done.7), custom_call_target="tpu_custom_call" | custom-call | tf_op jit(solution)/shard_map/pallas_call | solution.py:57
  95.1 2.7 %collective-permute-start.12 = (bf16[64,4608]{1,0:T(8,128)(2,1)}, bf16[64,4608]{1,0:T(8,128)(2,1)S(1)}, u32[]{:S(2)}, u32[]{:S(2)}) collective-permute-start(bf16[64,4608]{1,0:T(8,128)(2,1)} %collective-permute-done.8.refs_8_), channel_id=1, source_target_pairs={{0,7},{1,0},{2,1},{3,2},{4,3},{5,4},{6,5},{7,6},{8,15},{9,8},{10,9... | collective-permute-start | bytes 1769480 | tf_op jit(solution)/shard_map/ppermute | solution.py:248
  99.2 6.4 %all-to-all-start.4 = ((f32[8,8,1152]{2,1,0:T(8,128)}), f32[8,8,1152]{2,1,0:T(8,128)S(1)}, u32[]{:S(2)}, u32[]{:S(2)}) async-start(f32[8,8,1152]{2,1,0:T(8,128)} %shard_map.95), calls=%async_computation.4 | async-start | bytes 589824 | tf_op jit(solution)/shard_map/all_to_all | solution.py:258
  108.4 8.8 %all-to-all-done.4.in_ref = f32[8,8,1152]{2,1,0:T(8,128)S(1)} async-done(((f32[8,8,1152]{2,1,0:T(8,128)}), f32[8,8,1152]{2,1,0:T(8,128)S(1)}, u32[]{:S(2)}, u32[]{:S(2)}) %all-to-all-start.4) | async-done | bytes 294944 | tf_op jit(solution)/shard_map/all_to_all | solution.py:258
  118.1 6.4 %all-to-all-start.5 = ((f32[16,8,1152]{2,1,0:T(8,128)}), f32[16,8,1152]{2,1,0:T(8,128)S(1)}, u32[]{:S(2)}, u32[]{:S(2)}) async-start(f32[16,8,1152]{2,1,0:T(8,128)} %shard_map.96), calls=%async_computation.5 | async-start | bytes 1179648 | tf_op jit(solution)/shard_map/all_to_all | solution.py:257
  127.3 1.7 %collective-permute-done.13.refs_0_ = bf16[64,4608]{1,0:T(8,128)(2,1)} collective-permute-done((bf16[64,4608]{1,0:T(8,128)(2,1)S(1)}, bf16[64,4608]{1,0:T(8,128)(2,1)}, u32[]{:S(2)}, u32[]{:S(2)}) %collective-permute-start.13) | collective-permute-done | bytes 589856 | tf_op jit(solution)/shard_map/ppermute | solution.py:248
  129.0 9.7 %shard_map.97 = (f32[256,4608]{1,0:T(8,128)}, bf16[1024,256]{1,0:T(8,128)(2,1)}) custom-call(s32[1]{0:T(128)} %bitcast.z_ref, bf16[128,4608]{1,0:T(8,128)(2,1)} %refs_0_.1, bf16[64,4608]{1,0:T(8,128)(2,1)} %collective-permute-done.1.refs_1_, bf16[64,4608]{1,0:T(8,128)(2,1)} %collective-permute-done.3.refs_2_, ...), custom_call_target="tpu_custom_call" | custom-call | tf_op jit(solution)/shard_map/pallas_call | solution.py:57
  138.7 5.4 %collective-permute-start.17 = (f32[16,8,1152]{2,1,0:T(8,128)S(1)}, f32[16,8,1152]{2,1,0:T(8,128)S(1)}, u32[]{:S(2)}, u32[]{:S(2)}) collective-permute-start(f32[16,8,1152]{2,1,0:T(8,128)S(1)} %all-to-all-done.5), channel_id=1, source_target_pairs={{0,8},{8,0},{1,9},{9,1},{2,10},{10,2},{3,11},{11,3},{4,12},{12,4},... | collective-permute-start | bytes 1769480 | tf_op jit(solution)/shard_map/ppermute | solution.py:248
  144.1 1.6 %collective-permute-done.17 = f32[16,8,1152]{2,1,0:T(8,128)S(1)} collective-permute-done((f32[16,8,1152]{2,1,0:T(8,128)S(1)}, f32[16,8,1152]{2,1,0:T(8,128)S(1)}, u32[]{:S(2)}, u32[]{:S(2)}) %collective-permute-start.17) | collective-permute-done | bytes 589856 | tf_op jit(solution)/shard_map/ppermute | solution.py:248
  145.7 8.6 %shard_map.98 = (bf16[1,256,4608]{2,1,0:T(8,128)(2,1)}, f32[64,4608]{1,0:T(8,128)}, bf16[1024,256]{1,0:T(8,128)(2,1)}) custom-call(s32[1]{0:T(128)} %bitcast.z_ref, s32[1]{0:T(128)} %bitcast.1.core_ref, bf16[64,4608]{1,0:T(8,128)(2,1)} %collective-permute-done.13.refs_0_, bf16[64,4608]{1,0:T(8,128)(2,1)} %collective-permute-done.15.refs_1_, ...), custom_call_target="tpu_custom_call" | custom-call | tf_op jit(solution)/shard_map/pallas_call | solution.py:57
  (67 shorter events, 26.1 us)
Async XLA Ops:
  5.1 19.8 %all-to-all-start = ((f32[8,64,128]{2,1,0:T(8,128)}), f32[8,64,128]{2,1,0:T(8,128)S(1)}, u32[]{:S(2)}, u32[]{:S(2)}) async-start(f32[8,64,128]{2,1,0:T(8,128)} %get-tuple-element.59), calls=%async_computation | async-start | bytes 524288 | tf_op jit(solution)/shard_map/all_to_all | solution.py:258
  14.2 24.1 %collective-permute-start.1 = (bf16[64,4608]{1,0:T(8,128)(2,1)}, bf16[64,4608]{1,0:T(8,128)(2,1)}, u32[]{:S(2)}, u32[]{:S(2)}) collective-permute-start(bf16[64,4608]{1,0:T(8,128)(2,1)} %get-tuple-element.65), channel_id=1, source_target_pairs={{0,1},{1,2},{2,3},{3,4},{4,5},{5,6},{6,7},{7,0},{8,9},{9,10},{10,1... | collective-permute-start | bytes 1769480 | tf_op jit(solution)/shard_map/ppermute | solution.py:248
  15.7 22.7 %collective-permute-start.2 = (bf16[64,4608]{1,0:T(8,128)(2,1)}, bf16[64,4608]{1,0:T(8,128)(2,1)}, u32[]{:S(2)}, u32[]{:S(2)}) collective-permute-start(bf16[64,4608]{1,0:T(8,128)(2,1)} %get-tuple-element.66), channel_id=1, source_target_pairs={{0,7},{1,0},{2,1},{3,2},{4,3},{5,4},{6,5},{7,6},{8,15},{9,8},{10,9... | collective-permute-start | bytes 1769480 | tf_op jit(solution)/shard_map/ppermute | solution.py:248
  16.9 31.4 %collective-permute-start.3 = (bf16[64,4608]{1,0:T(8,128)(2,1)}, bf16[64,4608]{1,0:T(8,128)(2,1)}, u32[]{:S(2)}, u32[]{:S(2)}) collective-permute-start(bf16[64,4608]{1,0:T(8,128)(2,1)} %get-tuple-element.66), channel_id=1, source_target_pairs={{0,1},{1,2},{2,3},{3,4},{4,5},{5,6},{6,7},{7,0},{8,9},{9,10},{10,1... | collective-permute-start | bytes 1769480 | tf_op jit(solution)/shard_map/ppermute | solution.py:248
  17.2 31.1 %collective-permute-start.4 = (bf16[64,4608]{1,0:T(8,128)(2,1)}, bf16[64,4608]{1,0:T(8,128)(2,1)}, u32[]{:S(2)}, u32[]{:S(2)}) collective-permute-start(bf16[64,4608]{1,0:T(8,128)(2,1)} %get-tuple-element.65), channel_id=1, source_target_pairs={{0,7},{1,0},{2,1},{3,2},{4,3},{5,4},{6,5},{7,6},{8,15},{9,8},{10,9... | collective-permute-start | bytes 1769480 | tf_op jit(solution)/shard_map/ppermute | solution.py:248
  25.1 3.9 %collective-permute-start = (f32[32,256]{1,0:T(8,128)S(1)}, f32[32,256]{1,0:T(8,128)S(1)}, u32[]{:S(2)}, u32[]{:S(2)}) collective-permute-start(f32[32,256]{1,0:T(8,128)S(1)} %get-tuple-element.61), channel_id=1, source_target_pairs={{0,8},{8,0},{1,9},{9,1},{2,10},{10,2},{3,11},{11,3},{4,12},{12,4},... | collective-permute-start | bytes 98312 | tf_op jit(solution)/shard_map/ppermute | solution.py:248
  29.9 18.4 %all-to-all-start.1 = ((f32[16,32,256]{2,1,0:T(8,128)}), f32[16,32,256]{2,1,0:T(8,128)S(1)}, u32[]{:S(2)}, u32[]{:S(2)}) async-start(f32[16,32,256]{2,1,0:T(8,128)} %copy-done.3), calls=%async_computation.1 | async-start | bytes 1048576 | tf_op jit(solution)/shard_map/all_to_all | solution.py:257
  48.4 2.4 %collective-permute-start.5 = (f32[32,256]{1,0:T(8,128)S(1)}, f32[32,256]{1,0:T(8,128)S(1)}, u32[]{:S(2)}, u32[]{:S(2)}) collective-permute-start(f32[32,256]{1,0:T(8,128)S(1)} %shard_map.89.mine_ref), channel_id=1, source_target_pairs={{0,8},{8,0},{1,9},{9,1},{2,10},{10,2},{3,11},{11,3},{4,12},{12,4},... | collective-permute-start | bytes 98312 | tf_op jit(solution)/shard_map/ppermute | solution.py:248
  52.5 19.2 %all-to-all-start.2 = ((f32[8,96,128]{2,1,0:T(8,128)}), f32[8,96,128]{2,1,0:T(8,128)}, u32[]{:S(2)}, u32[]{:S(2)}) async-start(f32[8,96,128]{2,1,0:T(8,128)} %get-tuple-element.70), calls=%async_computation.2 | async-start | bytes 786432 | tf_op jit(solution)/shard_map/all_to_all | solution.py:258
  56.8 24.3 %collective-permute-start.7 = (bf16[64,4608]{1,0:T(8,128)(2,1)}, bf16[64,4608]{1,0:T(8,128)(2,1)}, u32[]{:S(2)}, u32[]{:S(2)}) collective-permute-start(bf16[64,4608]{1,0:T(8,128)(2,1)} %collective-permute-done.1.refs_1_), channel_id=1, source_target_pairs={{0,1},{1,2},{2,3},{3,4},{4,5},{5,6},{6,7},{7,0},{8,9},{9,10},{10,1... | collective-permute-start | bytes 1769480 | tf_op jit(solution)/shard_map/ppermute | solution.py:248
  58.3 22.8 %collective-permute-start.8 = (bf16[64,4608]{1,0:T(8,128)(2,1)}, bf16[64,4608]{1,0:T(8,128)(2,1)}, u32[]{:S(2)}, u32[]{:S(2)}) collective-permute-start(bf16[64,4608]{1,0:T(8,128)(2,1)} %collective-permute-done.2.refs_10_), channel_id=1, source_target_pairs={{0,7},{1,0},{2,1},{3,2},{4,3},{5,4},{6,5},{7,6},{8,15},{9,8},{10,9... | collective-permute-start | bytes 1769480 | tf_op jit(solution)/shard_map/ppermute | solution.py:248
  74.8 6.3 %collective-permute-start.6 = (f32[4,4,8,1152]{3,2,1,0:T(8,128)S(1)}, f32[4,4,8,1152]{3,2,1,0:T(8,128)S(1)}, u32[]{:S(2)}, u32[]{:S(2)}) collective-permute-start(f32[4,4,8,1152]{3,2,1,0:T(8,128)S(1)} %get-tuple-element.73), channel_id=1, source_target_pairs={{0,8},{8,0},{1,9},{9,1},{2,10},{10,2},{3,11},{11,3},{4,12},{12,4},... | collective-permute-start | bytes 1769480 | tf_op jit(solution)/shard_map/ppermute | solution.py:248
  75.6 23.6 %collective-permute-start.10 = (bf16[64,4608]{1,0:T(8,128)(2,1)}, bf16[64,4608]{1,0:T(8,128)(2,1)S(1)}, u32[]{:S(2)}, u32[]{:S(2)}) collective-permute-start(bf16[64,4608]{1,0:T(8,128)(2,1)} %collective-permute-done.4.refs_9_), channel_id=1, source_target_pairs={{0,7},{1,0},{2,1},{3,2},{4,3},{5,4},{6,5},{7,6},{8,15},{9,8},{10,9... | collective-permute-start | bytes 1769480 | tf_op jit(solution)/shard_map/ppermute | solution.py:248
  75.8 23.5 %collective-permute-start.9 = (bf16[64,4608]{1,0:T(8,128)(2,1)}, bf16[64,4608]{1,0:T(8,128)(2,1)S(1)}, u32[]{:S(2)}, u32[]{:S(2)}) collective-permute-start(bf16[64,4608]{1,0:T(8,128)(2,1)} %collective-permute-done.3.refs_2_), channel_id=1, source_target_pairs={{0,1},{1,2},{2,3},{3,4},{4,5},{5,6},{6,7},{7,0},{8,9},{9,10},{10,1... | collective-permute-start | bytes 1769480 | tf_op jit(solution)/shard_map/ppermute | solution.py:248
  82.0 16.5 %all-to-all-start.3 = ((f32[16,8,1152]{2,1,0:T(8,128)}), f32[16,8,1152]{2,1,0:T(8,128)S(1)}, u32[]{:S(2)}, u32[]{:S(2)}) async-start(f32[16,8,1152]{2,1,0:T(8,128)} %shard_map.93), calls=%async_computation.3 | async-start | bytes 1179648 | tf_op jit(solution)/shard_map/all_to_all | solution.py:257
  95.1 23.0 %collective-permute-start.11 = (bf16[64,4608]{1,0:T(8,128)(2,1)}, bf16[64,4608]{1,0:T(8,128)(2,1)S(1)}, u32[]{:S(2)}, u32[]{:S(2)}) collective-permute-start(bf16[64,4608]{1,0:T(8,128)(2,1)} %collective-permute-done.7.refs_3_), channel_id=1, source_target_pairs={{0,1},{1,2},{2,3},{3,4},{4,5},{5,6},{6,7},{7,0},{8,9},{9,10},{10,1... | collective-permute-start | bytes 1769480 | tf_op jit(solution)/shard_map/ppermute | solution.py:248
  95.1 23.0 %collective-permute-start.12 = (bf16[64,4608]{1,0:T(8,128)(2,1)}, bf16[64,4608]{1,0:T(8,128)(2,1)S(1)}, u32[]{:S(2)}, u32[]{:S(2)}) collective-permute-start(bf16[64,4608]{1,0:T(8,128)(2,1)} %collective-permute-done.8.refs_8_), channel_id=1, source_target_pairs={{0,7},{1,0},{2,1},{3,2},{4,3},{5,4},{6,5},{7,6},{8,15},{9,8},{10,9... | collective-permute-start | bytes 1769480 | tf_op jit(solution)/shard_map/ppermute | solution.py:248
  99.2 18.0 %all-to-all-start.4 = ((f32[8,8,1152]{2,1,0:T(8,128)}), f32[8,8,1152]{2,1,0:T(8,128)S(1)}, u32[]{:S(2)}, u32[]{:S(2)}) async-start(f32[8,8,1152]{2,1,0:T(8,128)} %shard_map.95), calls=%async_computation.4 | async-start | bytes 589824 | tf_op jit(solution)/shard_map/all_to_all | solution.py:258
  105.7 23.3 %collective-permute-start.13 = (bf16[64,4608]{1,0:T(8,128)(2,1)S(1)}, bf16[64,4608]{1,0:T(8,128)(2,1)}, u32[]{:S(2)}, u32[]{:S(2)}) collective-permute-start(bf16[64,4608]{1,0:T(8,128)(2,1)S(1)} %collective-permute-done.9.refs_4_), channel_id=1, source_target_pairs={{0,1},{1,2},{2,3},{3,4},{4,5},{5,6},{6,7},{7,0},{8,9},{9,10},{10,1... | collective-permute-start | bytes 1769480 | tf_op jit(solution)/shard_map/ppermute | solution.py:248
  107.2 21.8 %collective-permute-start.14 = (bf16[64,4608]{1,0:T(8,128)(2,1)S(1)}, bf16[64,4608]{1,0:T(8,128)(2,1)}, u32[]{:S(2)}, u32[]{:S(2)}) collective-permute-start(bf16[64,4608]{1,0:T(8,128)(2,1)S(1)} %collective-permute-done.10.refs_7_), channel_id=1, source_target_pairs={{0,7},{1,0},{2,1},{3,2},{4,3},{5,4},{6,5},{7,6},{8,15},{9,8},{10,9... | collective-permute-start | bytes 1769480 | tf_op jit(solution)/shard_map/ppermute | solution.py:248
  118.1 20.6 %all-to-all-start.5 = ((f32[16,8,1152]{2,1,0:T(8,128)}), f32[16,8,1152]{2,1,0:T(8,128)S(1)}, u32[]{:S(2)}, u32[]{:S(2)}) async-start(f32[16,8,1152]{2,1,0:T(8,128)} %shard_map.96), calls=%async_computation.5 | async-start | bytes 1179648 | tf_op jit(solution)/shard_map/all_to_all | solution.py:257
  124.5 19.6 %collective-permute-start.15 = (bf16[64,4608]{1,0:T(8,128)(2,1)S(1)}, bf16[64,4608]{1,0:T(8,128)(2,1)}, u32[]{:S(2)}, u32[]{:S(2)}) collective-permute-start(bf16[64,4608]{1,0:T(8,128)(2,1)S(1)} %collective-permute-done.11.refs_5_), channel_id=1, source_target_pairs={{0,1},{1,2},{2,3},{3,4},{4,5},{5,6},{6,7},{7,0},{8,9},{9,10},{10,1... | collective-permute-start | bytes 1769480 | tf_op jit(solution)/shard_map/ppermute | solution.py:248
  125.8 18.3 %collective-permute-start.16 = (bf16[64,4608]{1,0:T(8,128)(2,1)S(1)}, bf16[64,4608]{1,0:T(8,128)(2,1)}, u32[]{:S(2)}, u32[]{:S(2)}) collective-permute-start(bf16[64,4608]{1,0:T(8,128)(2,1)S(1)} %collective-permute-done.12.refs_6_), channel_id=1, source_target_pairs={{0,7},{1,0},{2,1},{3,2},{4,3},{5,4},{6,5},{7,6},{8,15},{9,8},{10,9... | collective-permute-start | bytes 1769480 | tf_op jit(solution)/shard_map/ppermute | solution.py:248
  138.7 7.0 %collective-permute-start.17 = (f32[16,8,1152]{2,1,0:T(8,128)S(1)}, f32[16,8,1152]{2,1,0:T(8,128)S(1)}, u32[]{:S(2)}, u32[]{:S(2)}) collective-permute-start(f32[16,8,1152]{2,1,0:T(8,128)S(1)} %all-to-all-done.5), channel_id=1, source_target_pairs={{0,8},{8,0},{1,9},{9,1},{2,10},{10,2},{3,11},{11,3},{4,12},{12,4},... | collective-permute-start | bytes 1769480 | tf_op jit(solution)/shard_map/ppermute | solution.py:248
  (14 other events, 173.0 us)

commit v4 on v3

--- a/solution.py
+++ b/solution.py
@@ -8,8 +8,9 @@
 
 D, K, NZ, NXY = 4608, 64, 8, 16
 TILE = 1152
+FIRST = (0, 1, 2, 3, 14, 15)
+SECOND = (4, 5, 6, 11, 12, 13)
 FAR = (7, 8, 9, 10)
-NEAR = tuple(h for h in range(16) if h not in FAR)
 NT = D // TILE
 HI = lax.Precision.HIGHEST
 F32, BF16 = jnp.float32, jnp.bfloat16
@@ -88,14 +89,19 @@
     out_ref[...] = fold3(dot(split3(q_ref[...]), e_ref[0], 1, 1))
 
 
-def turn_kernel(z_ref, a_ref, near_ref, far_ref):
+def turn_kernel(z_ref, a_ref, first_ref, second_ref, far_ref):
     parts = []
     for hops in range(NZ):
         src = lax.rem(z_ref[0] + (NZ - hops), NZ)
         parts.append(a_ref[pl.ds(pl.multiple_of(src * 128, 128), 128), :].T)
     turned = jnp.concatenate(parts, axis=1)
-    near_ref[...] = jnp.concatenate([turned[:, :448], turned[:, 704:]], axis=1)
+    first_ref[...] = jnp.concatenate([turned[:, :256], turned[:, 896:]], axis=1)
+    second_ref[...] = jnp.concatenate([turned[:, 256:448], turned[:, 704:896]], axis=1)
     far_ref[...] = turned[:, 448:704]
+
+
+def copy_kernel(in_ref, out_ref):
+    out_ref[...] = in_ref[...]
 
 
 def pick(core_ref, a, b):
@@ -160,14 +166,13 @@
     other_ref[:, 0] = pick(core_ref, q[32:], q[:32]).reshape(4, 8, TILE)
 
 
-def factor_kernel(gram_ref, p_ref, linv_ref, pf_ref):
-    row = lax.broadcasted_iota(jnp.int32, (K, K), 0)
-    lane = lax.broadcasted_iota(jnp.int32, (K, K), 1)
-    eye = jnp.where(row == lane, 1.0, 0.0)
-    both = jnp.concatenate([gram_ref[...], eye], axis=1)
+EARLY = 8
+
+
+def eliminate(both, first, last):
     tiles = [both[8 * t : 8 * t + 8] for t in range(8)]
     sub = lax.broadcasted_iota(jnp.int32, (8, 128), 0)
-    for i in range(K):
+    for i in range(first, last):
         b, r = divmod(i, 8)
         pivot = tiles[b][r : r + 1]
         scaled = pivot * (1.0 / pivot[:, i : i + 1])
@@ -176,17 +181,31 @@
             if t == b:
                 factor = jnp.where(sub > r, factor, 0.0)
             tiles[t] = tiles[t] - factor * scaled
-    both = jnp.concatenate(tiles, axis=0)
-    pivots = jnp.sum(both[:, :K] * eye, axis=1, keepdims=True)
+    return jnp.concatenate(tiles, axis=0)
+
+
+def identity():
+    row = lax.broadcasted_iota(jnp.int32, (K, K), 0)
+    lane = lax.broadcasted_iota(jnp.int32, (K, K), 1)
+    return jnp.where(row == lane, 1.0, 0.0)
+
+
+def early_kernel(gram_ref, both_ref):
+    both_ref[...] = eliminate(jnp.concatenate([gram_ref[...], identity()], axis=1), 0, EARLY)
+
+
+def factor_kernel(both_ref, p_ref, linv_ref, pf_ref):
+    both = eliminate(both_ref[...], EARLY, K)
+    pivots = jnp.sum(both[:, :K] * identity(), axis=1, keepdims=True)
     linv = both[:, K:] * lax.rsqrt(pivots)
     linv_ref[...] = linv
     pf_ref[...] = dot(linv, p_ref[...], 1, 0, HI)
 
 
-def place(grad_ref, z_ref, halves, acc_ref):
+def place(grad_ref, z_ref, halves, value_ref):
     for slot, half in enumerate(halves):
         src = lax.rem(z_ref[0] + (NZ - half // 2), NZ) * 128 + (half % 2) * 64
-        grad_ref[pl.ds(pl.multiple_of(src, 64), 64), :] = acc_ref[
+        grad_ref[pl.ds(pl.multiple_of(src, 64), 64), :] = value_ref[
             64 * slot : 64 * (slot + 1)
         ].astype(BF16)
 
@@ -201,24 +220,23 @@
         acc_ref[...] += part
 
 
-def near_kernel(z_ref, *refs):
+def near_kernel(*refs):
     blocks = refs[:-6]
-    a_ref, e_ref, w_ref, merged_ref, grad_ref, acc_ref = refs[-6:]
+    a_ref, w_ref, sum_ref, merged_ref, grad_ref, acc_ref = refs[-6:]
     rows = jnp.concatenate([b[...] for b in blocks], axis=0)
-    merged_ref[...] = jnp.dot(
-        a_ref[...], rows, preferred_element_type=F32
-    ) + e_ref[0].astype(F32)
+    before = sum_ref[...].reshape(256, TILE).astype(F32)
+    merged_ref[...] = before + jnp.dot(a_ref[...], rows, preferred_element_type=F32)
     accumulate(acc_ref, dot(rows, w_ref[...], 1, 1))
 
     @pl.when(pl.program_id(0) == pl.num_programs(0) - 1)
     def _():
-        place(grad_ref, z_ref, NEAR, acc_ref)
+        grad_ref[...] = acc_ref[...].astype(BF16)
 
 
 def tail_kernel(z_ref, core_ref, *refs):
     blocks = refs[:4]
-    a_ref, w_ref, sum_ref, near_ref, mine_ref, other_ref, linv_ref, pf_ref = refs[4:12]
-    err_ref, q_ref, grad_ref, acc_ref = refs[12:]
+    a_ref, w_ref, sum_ref, first_ref, second_ref, mine_ref, other_ref, linv_ref, pf_ref = refs[4:13]
+    err_ref, q_ref, grad_ref, acc_ref = refs[13:]
     mine = mine_ref[:, 0].reshape(32, TILE)
     other = other_ref[:, 0].reshape(32, TILE)
     raw = jnp.concatenate([pick(core_ref, mine, other), pick(core_ref, other, mine)], axis=0)
@@ -240,7 +258,8 @@
 
     @pl.when(pl.program_id(0) == pl.num_programs(0) - 1)
     def _():
-        grad_ref[...] = near_ref[...]
+        place(grad_ref, z_ref, FIRST, first_ref)
+        place(grad_ref, z_ref, SECOND, second_ref)
         place(grad_ref, z_ref, FAR, acc_ref)
 
 
@@ -263,6 +282,16 @@
     chunk_tile = pl.BlockSpec((4, 1, 8, TILE), lambda i: (0, i, 0, 0))
     chunks = (NXY, 8, TILE)
 
+    specs = lambda blocks, a: [tile(v.shape[0]) for v in blocks] + [whole(a.shape), tile(256)]
+
+    def near(blocks, a, before, before_spec):
+        return call(
+            near_kernel, [*blocks, a, out_weight, before], specs(blocks, a) + [before_spec],
+            [out((256, D)), out((384, 256), BF16)], [tile(256), whole((384, 256))], grid=(NT,),
+            scratch=[pltpu.VMEM((384, 256), F32)], mib=28, hbm_in=range(len(blocks) + 3),
+            hbm_out=(0, 1),
+        )
+
     y, ga, gb = call(
         rows_kernel, [q_prev_t, grad_out], [tile(K), tile(128)],
         [out((NZ, K, 128)), out((64, D), BF16), out((64, D), BF16)],
@@ -270,9 +299,7 @@
         scratch=[pltpu.VMEM((K, 128), F32)], hbm_in=(0, 1), hbm_out=(1, 2),
     )
     y = column(y)
-    (eq_t,) = simple(
-        error_rows_kernel, [q_prev_t, error_prev], [out((K, 256))]
-    )
+    (eq_t,) = simple(error_rows_kernel, [q_prev_t, error_prev], [out((K, 256))])
     u1a, d1b = up(ga), down(gb)
     u1b, d1a = up(gb), down(ga)
     mine, other = simple(
@@ -281,23 +308,28 @@
     (mine,) = simple(pair_kernel, [mine, swap(other)], [out((NXY, 32, 256))])
     mine, shadow = tied(mine, attn_out)
     mine = plane(mine)
-    a_near, a_far = simple(
-        turn_kernel, [z, shadow], [out((256, 768), BF16), out((256, 256), BF16)]
-    )
-    a_near, u1a, d1b, u1b, d1a = tied(a_near, u1a, d1b, u1b, d1a)
+    a_first, a_second, a_far = simple(
+        turn_kernel, [z, shadow],
+        [out((256, 384), BF16), out((256, 384), BF16), out((256, 256), BF16)],
+    )
+    a_first, u1a, d1b, u1b, d1a = tied(a_first, u1a, d1b, u1b, d1a)
     u2a, d2b = up(u1a), down(d1b)
     u2b, d2a = up(u1b), down(d1a)
-    mine, a_near, a_far = tied(mine, a_near, a_far)
+    mine, a_first, a_second, a_far = tied(mine, a_first, a_second, a_far)
     (mine,) = simple(total_kernel, [mine], [out((32, 256))])
 
     p_t, sent = simple(
         terms_kernel, [core, mine, swap(mine), attn_out], [out((K, 256)), out((NZ, 96, 128))]
     )
+    sent, p_t, a_first = tied(sent, p_t, a_first)
     got = column(sent)
+    merged, grad_first = near([grad_out, u1a, u1b, d1a, d1b], a_first, error_prev, err_tile)
+    p_then, u2a, d2b = tied(p_t, u2a, d2b)
     (ep,) = call(
-        error_terms_kernel, [p_t, error_prev], [whole((K, 256)), err_tile], [out((K, D))],
-        [tile(K)], grid=(NT,)
-    )
+        error_terms_kernel, [p_then, error_prev], [whole((K, 256)), err_tile], [out((K, D))],
+        [tile(K)], grid=(NT,), flops=3 * 10**9,
+    )
+    got, merged, grad_first = tied(got, merged, grad_first)
     mine, other, gram = call(
         right_kernel, [core, got, ep, grad_out],
         [SMEM, whole((NZ, 96, 128)), tile(K), tile(128)],
@@ -305,44 +337,38 @@
         [chunk_tile, chunk_tile, whole((K, K))], grid=(NT,), hbm_in=(3,),
     )
 
-    mine, other, u2a, d2b = tied(mine, swap(other), u2a, d2b)
+    other = swap(other)
     (mine,) = simple(add_kernel, [mine.reshape(chunks), other.reshape(chunks)], [out(chunks)])
     mine, gram, p_t = tied(mine, gram, p_t)
     mine = plane(mine)
-    linv, pf_t = simple(factor_kernel, [gram, p_t], [out((K, K)), out((K, 256))])
-    linv, u2a, d2b = tied(linv, u2a, d2b)
+    (early,) = simple(early_kernel, [gram], [out((K, 128))])
+    early, u2a, d2b = tied(early, u2a, d2b)
     u3a, d3b = up(u2a), down(d2b)
+    linv, pf_t = simple(factor_kernel, [early, p_t], [out((K, K)), out((K, 256))])
     mine, linv, pf_t = tied(mine, linv, pf_t)
     (mine,) = simple(spread_kernel, [mine], [out((NZ, 8, TILE))])
     mine, u2b, d2a = tied(mine, u2b, d2a)
+    mine = column(mine)
     u3b, d3a = up(u2b), down(d2a)
     far_a, far_b = up(u3a), down(d3b)
-    mine = column(mine)
     (mine,) = simple(spread_kernel, [mine], [out(chunks)])
-    mine, a_near, u3a, d3b = tied(mine, a_near, u3a, d3b)
+    mine, a_second, a_far, merged = tied(mine, a_second, a_far, merged)
     mine = plane(mine)
-    a_near, u3b, d3a = tied(a_near, u3b, d3a)
-    near = [grad_out, u1a, u1b, u2a, u2b, u3a, d3b, d2a, d2b, d1a, d1b]
-    specs = lambda blocks, a: [tile(v.shape[0]) for v in blocks] + [whole(a.shape)]
-    merged, grad_near = call(
-        near_kernel, [z, *near, a_near, error_prev, out_weight],
-        [SMEM] + specs(near, a_near) + [err_tile, tile(256)],
-        [out((256, D)), out((1024, 256), BF16)], [tile(256), whole((1024, 256))], grid=(NT,),
-        scratch=[pltpu.VMEM((768, 256), F32)], mib=28,
-        hbm_in=range(1, len(near) + 4), hbm_out=(0, 1),
-    )
-    mine, merged, grad_near = tied(mine, merged, grad_near)
+    merged, grad_second = near([u2a, u2b, u3a, d3b, d2a, d2b], a_second, merged, tile(256))
+    a_far, merged, u3b, far_a, far_b, d3a = tied(a_far, merged, u3b, far_a, far_b, d3a)
+    (a_far,) = simple(copy_kernel, [a_far], [out((256, 256), BF16)])
+    mine, a_far, merged, grad_second = tied(mine, a_far, merged, grad_second)
     other = swap(mine)
     far = [u3b, far_a, far_b, d3a]
     error_new, q_t, grad_attn = call(
         tail_kernel,
-        [z, core, *far, a_far, out_weight, merged, grad_near, mine.reshape(4, NT, 8, TILE),
-         other.reshape(4, NT, 8, TILE), linv, pf_t],
-        [SMEM, SMEM] + specs(far, a_far) + [tile(256), tile(256), whole((1024, 256)), chunk_tile,
-         chunk_tile, whole((K, K)), whole((K, 256))],
+        [z, core, *far, a_far, out_weight, merged, grad_first, grad_second,
+         mine.reshape(4, NT, 8, TILE), other.reshape(4, NT, 8, TILE), linv, pf_t],
+        [SMEM, SMEM] + specs(far, a_far) + [tile(256), whole((384, 256)), whole((384, 256)),
+         chunk_tile, chunk_tile, whole((K, K)), whole((K, 256))],
         [out((1, 256, D), BF16), out((K, D)), out((1024, 256), BF16)],
         [err_tile, tile(K), whole((1024, 256))], grid=(NT,),
-        scratch=[pltpu.VMEM((256, 256), F32)], mib=28, hbm_in=range(2, 10), hbm_out=(0, 1, 2),
+        scratch=[pltpu.VMEM((256, 256), F32)], mib=28, hbm_in=range(2, 11), hbm_out=(0, 1, 2),
     )
     return grad_attn, pf_t.T, q_t.T, error_new
 

time: 155 us -> 153 us (0.987)
  Pallas kernels: 38.8 us -> 46.1 us
  waiting for transfers between devices: 41.4 us -> 35.2 us
  starting transfers between devices: 68.3 us -> 66.1 us
  local copies, waits for them, and re-layouts: 4.94 us -> 3.38 us
    all_to_all x3, waiting for transfers between devices: 21.7 us -> 8.31 us  [on_device(): column = lambda v: lax.all_to_all(v, 'z', 0, 0)]
    pallas_call x15 -> x18, Pallas kernels: 38.8 us -> 46.1 us  [call(): pl.pallas_call(kernel, grid=grid, in_specs=in_specs, out_specs=out_specs,...]
    ppermute x18, waiting for transfers between devices: 19 us -> 25.2 us  [shift(): return lax.ppermute(v, axis, [(i, (i + by) % size) for i in range(size)])]
    all_to_all x3, starting transfers between devices: 19.8 us -> 16.9 us  [on_device(): column = lambda v: lax.all_to_all(v, 'z', 0, 0)]
    unnamed x28 -> x26, local copies, waits for them, and re-layouts: 4.94 us -> 3.38 us
  transfers between devices with their start and end apart: 24 -> 24, of which waited for: 10 -> 10; matrix products, arithmetic and copies ran while one was open for 0% -> 0% of each run, Pallas kernels for 16% -> 20%
where the time goes in v4:
time: 153 us; the launch traced here: 152 us
  starting transfers between devices  66.1 us (43%)
  Pallas kernels  46.1 us (30%)
  waiting for transfers between devices  35.2 us (23%)
  local copies, waits for them, and re-layouts  3.38 us (2%)
    pallas_call x18, Pallas kernels, call(): pl.pallas_call(kernel, grid=grid, in_specs=in_specs, out_specs=out_specs,...  46.1 us
    ppermute x18, starting transfers between devices, shift(): return lax.ppermute(v, axis, [(i, (i + by) % size) for i in range(size)])  28.9 us
    ppermute x18, waiting for transfers between devices, shift(): return lax.ppermute(v, axis, [(i, (i + by) % size) for i in range(size)])  25.2 us
    all_to_all x3, starting transfers between devices, on_device(): plane = lambda v: lax.all_to_all(v, ('x', 'y'), 0, 0)  20.3 us
    all_to_all x3, starting transfers between devices, on_device(): column = lambda v: lax.all_to_all(v, 'z', 0, 0)  16.9 us
    all_to_all x3, waiting for transfers between devices, on_device(): column = lambda v: lax.all_to_all(v, 'z', 0, 0)  8.31 us
    unnamed x26, local copies, waits for them, and re-layouts  3.38 us
  transfers between devices with their start and end apart: 24, of which 10 were waited for; matrix products, arithmetic and copies ran while one was open for 0% of the time, Pallas kernels for 20%

profile of v4, /device:TPU:1, one launch (start us, length us, event | category | flops | bytes accessed | tf_op | source)
XLA Modules:
  0.0 151.8 jit_solution(14239285783394977331)
XLA Ops:
  0.6 4.4 %shard_map.84 = (f32[8,64,128]{2,1,0:T(8,128)}, bf16[64,4608]{1,0:T(8,128)(2,1)}, bf16[64,4608]{1,0:T(8,128)(2,1)}) custom-call(f32[64,4608]{1,0:T(8,128)} %bitcast.9, bf16[128,4608]{1,0:T(8,128)(2,1)} %g_ref.3), custom_call_target="tpu_custom_call" | custom-call | tf_op jit(solution)/shard_map/pallas_call | solution.py:58
  5.1 9.1 %all-to-all-start = ((f32[8,64,128]{2,1,0:T(8,128)}), f32[8,64,128]{2,1,0:T(8,128)S(1)}, u32[]{:S(2)}, u32[]{:S(2)}) async-start(f32[8,64,128]{2,1,0:T(8,128)} %get-tuple-element.72), calls=%async_computation | async-start | bytes 524288 | tf_op jit(solution)/shard_map/all_to_all | solution.py:277
  17.2 2.5 %collective-permute-start.4 = (bf16[64,4608]{1,0:T(8,128)(2,1)}, bf16[64,4608]{1,0:T(8,128)(2,1)}, u32[]{:S(2)}, u32[]{:S(2)}) collective-permute-start(bf16[64,4608]{1,0:T(8,128)(2,1)} %get-tuple-element.78), channel_id=1, source_target_pairs={{0,7},{1,0},{2,1},{3,2},{4,3},{5,4},{6,5},{7,6},{8,15},{9,8},{10,9... | collective-permute-start | bytes 1769480 | tf_op jit(solution)/shard_map/ppermute | solution.py:267
  21.8 3.0 %all-to-all-done.y_ref = f32[8,64,128]{2,1,0:T(8,128)S(1)} async-done(((f32[8,64,128]{2,1,0:T(8,128)}), f32[8,64,128]{2,1,0:T(8,128)S(1)}, u32[]{:S(2)}, u32[]{:S(2)}) %all-to-all-start) | async-done | bytes 262176 | tf_op jit(solution)/shard_map/all_to_all | solution.py:277
  25.1 3.1 %collective-permute-start = (f32[32,256]{1,0:T(8,128)S(1)}, f32[32,256]{1,0:T(8,128)S(1)}, u32[]{:S(2)}, u32[]{:S(2)}) collective-permute-start(f32[32,256]{1,0:T(8,128)S(1)} %get-tuple-element.74), channel_id=1, source_target_pairs={{0,8},{8,0},{1,9},{9,1},{2,10},{10,2},{3,11},{11,3},{4,12},{12,4},... | collective-permute-start | bytes 98312 | tf_op jit(solution)/shard_map/ppermute | solution.py:267
  29.9 6.8 %all-to-all-start.1 = ((f32[16,32,256]{2,1,0:T(8,128)}), f32[16,32,256]{2,1,0:T(8,128)S(1)}, u32[]{:S(2)}, u32[]{:S(2)}) async-start(f32[16,32,256]{2,1,0:T(8,128)} %shard_map.87), calls=%async_computation.1 | async-start | bytes 1048576 | tf_op jit(solution)/shard_map/all_to_all | solution.py:276
  38.3 10.0 %collective-permute-done.3.refs_2_ = bf16[64,4608]{1,0:T(8,128)(2,1)} collective-permute-done((bf16[64,4608]{1,0:T(8,128)(2,1)}, bf16[64,4608]{1,0:T(8,128)(2,1)}, u32[]{:S(2)}, u32[]{:S(2)}) %collective-permute-start.3) | collective-permute-done | bytes 589856 | tf_op jit(solution)/shard_map/ppermute | solution.py:267
  48.5 2.5 %collective-permute-start.7 = (bf16[64,4608]{1,0:T(8,128)(2,1)}, bf16[64,4608]{1,0:T(8,128)(2,1)}, u32[]{:S(2)}, u32[]{:S(2)}) collective-permute-start(bf16[64,4608]{1,0:T(8,128)(2,1)} %collective-permute-done.2.refs_4_), channel_id=1, source_target_pairs={{0,7},{1,0},{2,1},{3,2},{4,3},{5,4},{6,5},{7,6},{8,15},{9,8},{10,9... | collective-permute-start | bytes 1769480 | tf_op jit(solution)/shard_map/ppermute | solution.py:267
  51.0 2.1 %collective-permute-start.5 = (f32[32,256]{1,0:T(8,128)S(1)}, f32[32,256]{1,0:T(8,128)S(1)}, u32[]{:S(2)}, u32[]{:S(2)}) collective-permute-start(f32[32,256]{1,0:T(8,128)S(1)} %shard_map.89.mine_ref), channel_id=1, source_target_pairs={{0,8},{8,0},{1,9},{9,1},{2,10},{10,2},{3,11},{11,3},{4,12},{12,4},... | collective-permute-start | bytes 98312 | tf_op jit(solution)/shard_map/ppermute | solution.py:267
  55.2 4.3 %all-to-all-start.2 = ((f32[8,96,128]{2,1,0:T(8,128)}), f32[8,96,128]{2,1,0:T(8,128)S(1)}, u32[]{:S(2)}, u32[]{:S(2)}) async-start(f32[8,96,128]{2,1,0:T(8,128)} %get-tuple-element.87), calls=%async_computation.2 | async-start | bytes 786432 | tf_op jit(solution)/shard_map/all_to_all | solution.py:277
  59.4 8.1 %shard_map.91 = (f32[256,4608]{1,0:T(8,128)}, bf16[384,256]{1,0:T(8,128)(2,1)}) custom-call(bf16[128,4608]{1,0:T(8,128)(2,1)} %g_ref.3, bf16[64,4608]{1,0:T(8,128)(2,1)} %collective-permute-done.1.refs_1_, bf16[64,4608]{1,0:T(8,128)(2,1)} %collective-permute-done.3.refs_2_, bf16[64,4608]{1,0:T(8,128)(2,1)} %collective-permute-done.4.refs_3_, ...), custom_call_target="tpu_custom_call" | custom-call | tf_op jit(solution)/shard_map/pallas_call | solution.py:58
  69.1 3.0 %all-to-all-done.2.got_ref = f32[8,96,128]{2,1,0:T(8,128)S(1)} async-done(((f32[8,96,128]{2,1,0:T(8,128)}), f32[8,96,128]{2,1,0:T(8,128)S(1)}, u32[]{:S(2)}, u32[]{:S(2)}) %all-to-all-start.2) | async-done | bytes 393248 | tf_op jit(solution)/shard_map/all_to_all | solution.py:277
  72.0 2.9 %shard_map.93 = (f32[4,4,8,1152]{3,2,1,0:T(8,128)S(1)}, f32[4,4,8,1152]{3,2,1,0:T(8,128)S(1)}, f32[64,64]{1,0:T(8,128)S(1)}) custom-call(s32[1]{0:T(128)} %bitcast.1.core_ref, f32[8,96,128]{2,1,0:T(8,128)S(1)} %all-to-all-done.2.got_ref, f32[64,4608]{1,0:T(8,128)S(1)} %shard_map.92.ep_ref, bf16[128,4608]{1,0:T(8,128)(2,1)} %g_ref.3), custom_call_target="tpu_custom_call" | custom-call | tf_op jit(solution)/shard_map/pallas_call | solution.py:58
  75.0 1.9 %collective-permute-start.8 = (f32[4,4,8,1152]{3,2,1,0:T(8,128)S(1)}, f32[4,4,8,1152]{3,2,1,0:T(8,128)S(1)}, u32[]{:S(2)}, u32[]{:S(2)}) collective-permute-start(f32[4,4,8,1152]{3,2,1,0:T(8,128)S(1)} %get-tuple-element.99), channel_id=1, source_target_pairs={{0,8},{8,0},{1,9},{9,1},{2,10},{10,2},{3,11},{11,3},{4,12},{12,4},... | collective-permute-start | bytes 1769480 | tf_op jit(solution)/shard_map/ppermute | solution.py:267
  76.9 2.4 %collective-permute-start.10 = (bf16[64,4608]{1,0:T(8,128)(2,1)}, bf16[64,4608]{1,0:T(8,128)(2,1)}, u32[]{:S(2)}, u32[]{:S(2)}) collective-permute-start(bf16[64,4608]{1,0:T(8,128)(2,1)} %collective-permute-done.4.refs_3_), channel_id=1, source_target_pairs={{0,7},{1,0},{2,1},{3,2},{4,3},{5,4},{6,5},{7,6},{8,15},{9,8},{10,9... | collective-permute-start | bytes 1769480 | tf_op jit(solution)/shard_map/ppermute | solution.py:267
  81.7 6.8 %all-to-all-start.3 = ((f32[16,8,1152]{2,1,0:T(8,128)}), f32[16,8,1152]{2,1,0:T(8,128)S(1)}, u32[]{:S(2)}, u32[]{:S(2)}) async-start(f32[16,8,1152]{2,1,0:T(8,128)} %shard_map.94), calls=%async_computation.3 | async-start | bytes 1179648 | tf_op jit(solution)/shard_map/all_to_all | solution.py:276
  92.1 5.6 %shard_map.96 = (f32[64,64]{1,0:T(8,128)S(1)}, f32[64,256]{1,0:T(8,128)}) custom-call(f32[64,128]{1,0:T(8,128)S(1)} %shard_map.95.both_ref, f32[64,256]{1,0:T(8,128)S(1)} %get-tuple-element.106.p_ref), custom_call_target="tpu_custom_call" | custom-call | tf_op jit(solution)/shard_map/pallas_call | solution.py:58
  100.1 3.5 %all-to-all-start.4 = ((f32[8,8,1152]{2,1,0:T(8,128)}), f32[8,8,1152]{2,1,0:T(8,128)S(1)}, u32[]{:S(2)}, u32[]{:S(2)}) async-start(f32[8,8,1152]{2,1,0:T(8,128)} %shard_map.97), calls=%async_computation.4 | async-start | bytes 589824 | tf_op jit(solution)/shard_map/all_to_all | solution.py:277
  108.5 2.2 %collective-permute-start.15 = (bf16[64,4608]{1,0:T(8,128)(2,1)}, bf16[64,4608]{1,0:T(8,128)(2,1)S(1)}, u32[]{:S(2)}, u32[]{:S(2)}) collective-permute-start(bf16[64,4608]{1,0:T(8,128)(2,1)} %collective-permute-done.12.refs_3_), channel_id=1, source_target_pairs={{0,7},{1,0},{2,1},{3,2},{4,3},{5,4},{6,5},{7,6},{8,15},{9,8},{10,9... | collective-permute-start | bytes 1769480 | tf_op jit(solution)/shard_map/ppermute | solution.py:267
  110.7 2.3 %all-to-all-done.4.in_ref = f32[8,8,1152]{2,1,0:T(8,128)S(1)} async-done(((f32[8,8,1152]{2,1,0:T(8,128)}), f32[8,8,1152]{2,1,0:T(8,128)S(1)}, u32[]{:S(2)}, u32[]{:S(2)}) %all-to-all-start.4) | async-done | bytes 294944 | tf_op jit(solution)/shard_map/all_to_all | solution.py:277
  113.9 6.8 %all-to-all-start.5 = ((f32[16,8,1152]{2,1,0:T(8,128)}), f32[16,8,1152]{2,1,0:T(8,128)S(1)}, u32[]{:S(2)}, u32[]{:S(2)}) async-start(f32[16,8,1152]{2,1,0:T(8,128)} %shard_map.98), calls=%async_computation.5 | async-start | bytes 1179648 | tf_op jit(solution)/shard_map/all_to_all | solution.py:276
  120.7 8.3 %shard_map.99 = (f32[256,4608]{1,0:T(8,128)}, bf16[384,256]{1,0:T(8,128)(2,1)}) custom-call(bf16[64,4608]{1,0:T(8,128)(2,1)} %copy-done.12, bf16[64,4608]{1,0:T(8,128)(2,1)} %collective-permute-done.9.refs_1_, bf16[64,4608]{1,0:T(8,128)(2,1)} %collective-permute-done.11.refs_2_, bf16[64,4608]{1,0:T(8,128)(2,1)} %collective-permute-done.12.refs_3_, ...), custom_call_target="tpu_custom_call" | custom-call | tf_op jit(solution)/shard_map/pallas_call | solution.py:58
  129.0 10.2 %collective-permute-done.14.refs_1_ = bf16[64,4608]{1,0:T(8,128)(2,1)S(1)} collective-permute-done((bf16[64,4608]{1,0:T(8,128)(2,1)}, bf16[64,4608]{1,0:T(8,128)(2,1)S(1)}, u32[]{:S(2)}, u32[]{:S(2)}) %collective-permute-start.14) | collective-permute-done | bytes 589856 | tf_op jit(solution)/shard_map/ppermute | solution.py:267
  143.1 8.5 %shard_map.101 = (bf16[1,256,4608]{2,1,0:T(8,128)(2,1)}, f32[64,4608]{1,0:T(8,128)}, bf16[1024,256]{1,0:T(8,128)(2,1)}) custom-call(s32[1]{0:T(128)} %bitcast.z_ref, s32[1]{0:T(128)} %bitcast.1.core_ref, bf16[64,4608]{1,0:T(8,128)(2,1)} %copy-done.8, bf16[64,4608]{1,0:T(8,128)(2,1)} %copy-done.10, bf16[64,4608]{1,0:T(8,128)(2,1)} %copy-done.11, ...), custom_call_target="tpu_custom_call" | custom-call | tf_op jit(solution)/shard_map/pallas_call | solution.py:58
  (68 shorter events, 30.6 us)
Async XLA Ops:
  5.1 19.8 %all-to-all-start = ((f32[8,64,128]{2,1,0:T(8,128)}), f32[8,64,128]{2,1,0:T(8,128)S(1)}, u32[]{:S(2)}, u32[]{:S(2)}) async-start(f32[8,64,128]{2,1,0:T(8,128)} %get-tuple-element.72), calls=%async_computation | async-start | bytes 524288 | tf_op jit(solution)/shard_map/all_to_all | solution.py:277
  14.2 24.1 %collective-permute-start.1 = (bf16[64,4608]{1,0:T(8,128)(2,1)}, bf16[64,4608]{1,0:T(8,128)(2,1)}, u32[]{:S(2)}, u32[]{:S(2)}) collective-permute-start(bf16[64,4608]{1,0:T(8,128)(2,1)} %get-tuple-element.78), channel_id=1, source_target_pairs={{0,1},{1,2},{2,3},{3,4},{4,5},{5,6},{6,7},{7,0},{8,9},{9,10},{10,1... | collective-permute-start | bytes 1769480 | tf_op jit(solution)/shard_map/ppermute | solution.py:267
  15.7 22.6 %collective-permute-start.2 = (bf16[64,4608]{1,0:T(8,128)(2,1)}, bf16[64,4608]{1,0:T(8,128)(2,1)}, u32[]{:S(2)}, u32[]{:S(2)}) collective-permute-start(bf16[64,4608]{1,0:T(8,128)(2,1)} %get-tuple-element.79), channel_id=1, source_target_pairs={{0,7},{1,0},{2,1},{3,2},{4,3},{5,4},{6,5},{7,6},{8,15},{9,8},{10,9... | collective-permute-start | bytes 1769480 | tf_op jit(solution)/shard_map/ppermute | solution.py:267
  16.9 31.4 %collective-permute-start.3 = (bf16[64,4608]{1,0:T(8,128)(2,1)}, bf16[64,4608]{1,0:T(8,128)(2,1)}, u32[]{:S(2)}, u32[]{:S(2)}) collective-permute-start(bf16[64,4608]{1,0:T(8,128)(2,1)} %get-tuple-element.79), channel_id=1, source_target_pairs={{0,1},{1,2},{2,3},{3,4},{4,5},{5,6},{6,7},{7,0},{8,9},{9,10},{10,1... | collective-permute-start | bytes 1769480 | tf_op jit(solution)/shard_map/ppermute | solution.py:267
  17.2 31.1 %collective-permute-start.4 = (bf16[64,4608]{1,0:T(8,128)(2,1)}, bf16[64,4608]{1,0:T(8,128)(2,1)}, u32[]{:S(2)}, u32[]{:S(2)}) collective-permute-start(bf16[64,4608]{1,0:T(8,128)(2,1)} %get-tuple-element.78), channel_id=1, source_target_pairs={{0,7},{1,0},{2,1},{3,2},{4,3},{5,4},{6,5},{7,6},{8,15},{9,8},{10,9... | collective-permute-start | bytes 1769480 | tf_op jit(solution)/shard_map/ppermute | solution.py:267
  25.1 3.9 %collective-permute-start = (f32[32,256]{1,0:T(8,128)S(1)}, f32[32,256]{1,0:T(8,128)S(1)}, u32[]{:S(2)}, u32[]{:S(2)}) collective-permute-start(f32[32,256]{1,0:T(8,128)S(1)} %get-tuple-element.74), channel_id=1, source_target_pairs={{0,8},{8,0},{1,9},{9,1},{2,10},{10,2},{3,11},{11,3},{4,12},{12,4},... | collective-permute-start | bytes 98312 | tf_op jit(solution)/shard_map/ppermute | solution.py:267
  29.9 21.1 %all-to-all-start.1 = ((f32[16,32,256]{2,1,0:T(8,128)}), f32[16,32,256]{2,1,0:T(8,128)S(1)}, u32[]{:S(2)}, u32[]{:S(2)}) async-start(f32[16,32,256]{2,1,0:T(8,128)} %shard_map.87), calls=%async_computation.1 | async-start | bytes 1048576 | tf_op jit(solution)/shard_map/all_to_all | solution.py:276
  48.3 19.2 %collective-permute-start.6 = (bf16[64,4608]{1,0:T(8,128)(2,1)}, bf16[64,4608]{1,0:T(8,128)(2,1)S(1)}, u32[]{:S(2)}, u32[]{:S(2)}) collective-permute-start(bf16[64,4608]{1,0:T(8,128)(2,1)} %collective-permute-done.1.refs_1_), channel_id=1, source_target_pairs={{0,1},{1,2},{2,3},{3,4},{4,5},{5,6},{6,7},{7,0},{8,9},{9,10},{10,1... | collective-permute-start | bytes 1769480 | tf_op jit(solution)/shard_map/ppermute | solution.py:267
  48.5 19.0 %collective-permute-start.7 = (bf16[64,4608]{1,0:T(8,128)(2,1)}, bf16[64,4608]{1,0:T(8,128)(2,1)}, u32[]{:S(2)}, u32[]{:S(2)}) collective-permute-start(bf16[64,4608]{1,0:T(8,128)(2,1)} %collective-permute-done.2.refs_4_), channel_id=1, source_target_pairs={{0,7},{1,0},{2,1},{3,2},{4,3},{5,4},{6,5},{7,6},{8,15},{9,8},{10,9... | collective-permute-start | bytes 1769480 | tf_op jit(solution)/shard_map/ppermute | solution.py:267
  51.0 3.0 %collective-permute-start.5 = (f32[32,256]{1,0:T(8,128)S(1)}, f32[32,256]{1,0:T(8,128)S(1)}, u32[]{:S(2)}, u32[]{:S(2)}) collective-permute-start(f32[32,256]{1,0:T(8,128)S(1)} %shard_map.89.mine_ref), channel_id=1, source_target_pairs={{0,8},{8,0},{1,9},{9,1},{2,10},{10,2},{3,11},{11,3},{4,12},{12,4},... | collective-permute-start | bytes 98312 | tf_op jit(solution)/shard_map/ppermute | solution.py:267
  55.2 16.9 %all-to-all-start.2 = ((f32[8,96,128]{2,1,0:T(8,128)}), f32[8,96,128]{2,1,0:T(8,128)S(1)}, u32[]{:S(2)}, u32[]{:S(2)}) async-start(f32[8,96,128]{2,1,0:T(8,128)} %get-tuple-element.87), calls=%async_computation.2 | async-start | bytes 786432 | tf_op jit(solution)/shard_map/all_to_all | solution.py:277
  75.0 5.8 %collective-permute-start.8 = (f32[4,4,8,1152]{3,2,1,0:T(8,128)S(1)}, f32[4,4,8,1152]{3,2,1,0:T(8,128)S(1)}, u32[]{:S(2)}, u32[]{:S(2)}) collective-permute-start(f32[4,4,8,1152]{3,2,1,0:T(8,128)S(1)} %get-tuple-element.99), channel_id=1, source_target_pairs={{0,8},{8,0},{1,9},{9,1},{2,10},{10,2},{3,11},{11,3},{4,12},{12,4},... | collective-permute-start | bytes 1769480 | tf_op jit(solution)/shard_map/ppermute | solution.py:267
  76.9 23.2 %collective-permute-start.10 = (bf16[64,4608]{1,0:T(8,128)(2,1)}, bf16[64,4608]{1,0:T(8,128)(2,1)}, u32[]{:S(2)}, u32[]{:S(2)}) collective-permute-start(bf16[64,4608]{1,0:T(8,128)(2,1)} %collective-permute-done.4.refs_3_), channel_id=1, source_target_pairs={{0,7},{1,0},{2,1},{3,2},{4,3},{5,4},{6,5},{7,6},{8,15},{9,8},{10,9... | collective-permute-start | bytes 1769480 | tf_op jit(solution)/shard_map/ppermute | solution.py:267
  79.3 20.8 %collective-permute-start.9 = (bf16[64,4608]{1,0:T(8,128)(2,1)}, bf16[64,4608]{1,0:T(8,128)(2,1)}, u32[]{:S(2)}, u32[]{:S(2)}) collective-permute-start(bf16[64,4608]{1,0:T(8,128)(2,1)} %collective-permute-done.3.refs_2_), channel_id=1, source_target_pairs={{0,1},{1,2},{2,3},{3,4},{4,5},{5,6},{6,7},{7,0},{8,9},{9,10},{10,1... | collective-permute-start | bytes 1769480 | tf_op jit(solution)/shard_map/ppermute | solution.py:267
  81.7 17.7 %all-to-all-start.3 = ((f32[16,8,1152]{2,1,0:T(8,128)}), f32[16,8,1152]{2,1,0:T(8,128)S(1)}, u32[]{:S(2)}, u32[]{:S(2)}) async-start(f32[16,8,1152]{2,1,0:T(8,128)} %shard_map.94), calls=%async_computation.3 | async-start | bytes 1179648 | tf_op jit(solution)/shard_map/all_to_all | solution.py:276
  89.2 18.9 %collective-permute-start.11 = (bf16[64,4608]{1,0:T(8,128)(2,1)S(1)}, bf16[64,4608]{1,0:T(8,128)(2,1)}, u32[]{:S(2)}, u32[]{:S(2)}) collective-permute-start(bf16[64,4608]{1,0:T(8,128)(2,1)S(1)} %collective-permute-done.6.refs_0_), channel_id=1, source_target_pairs={{0,1},{1,2},{2,3},{3,4},{4,5},{5,6},{6,7},{7,0},{8,9},{9,10},{10,1... | collective-permute-start | bytes 1769480 | tf_op jit(solution)/shard_map/ppermute | solution.py:267
  91.1 17.5 %collective-permute-start.12 = (bf16[64,4608]{1,0:T(8,128)(2,1)}, bf16[64,4608]{1,0:T(8,128)(2,1)}, u32[]{:S(2)}, u32[]{:S(2)}) collective-permute-start(bf16[64,4608]{1,0:T(8,128)(2,1)} %collective-permute-done.7.refs_5_), channel_id=1, source_target_pairs={{0,7},{1,0},{2,1},{3,2},{4,3},{5,4},{6,5},{7,6},{8,15},{9,8},{10,9... | collective-permute-start | bytes 1769480 | tf_op jit(solution)/shard_map/ppermute | solution.py:267
  100.1 12.9 %all-to-all-start.4 = ((f32[8,8,1152]{2,1,0:T(8,128)}), f32[8,8,1152]{2,1,0:T(8,128)S(1)}, u32[]{:S(2)}, u32[]{:S(2)}) async-start(f32[8,8,1152]{2,1,0:T(8,128)} %shard_map.97), calls=%async_computation.4 | async-start | bytes 589824 | tf_op jit(solution)/shard_map/all_to_all | solution.py:277
  103.6 25.4 %collective-permute-start.13 = (bf16[64,4608]{1,0:T(8,128)(2,1)}, bf16[64,4608]{1,0:T(8,128)(2,1)S(1)}, u32[]{:S(2)}, u32[]{:S(2)}) collective-permute-start(bf16[64,4608]{1,0:T(8,128)(2,1)} %collective-permute-done.9.refs_1_), channel_id=1, source_target_pairs={{0,1},{1,2},{2,3},{3,4},{4,5},{5,6},{6,7},{7,0},{8,9},{9,10},{10,1... | collective-permute-start | bytes 1769480 | tf_op jit(solution)/shard_map/ppermute | solution.py:267
  105.2 23.8 %collective-permute-start.16 = (bf16[64,4608]{1,0:T(8,128)(2,1)}, bf16[64,4608]{1,0:T(8,128)(2,1)S(1)}, u32[]{:S(2)}, u32[]{:S(2)}) collective-permute-start(bf16[64,4608]{1,0:T(8,128)(2,1)} %collective-permute-done.10.refs_4_), channel_id=1, source_target_pairs={{0,7},{1,0},{2,1},{3,2},{4,3},{5,4},{6,5},{7,6},{8,15},{9,8},{10,9... | collective-permute-start | bytes 1769480 | tf_op jit(solution)/shard_map/ppermute | solution.py:267
  108.0 31.2 %collective-permute-start.14 = (bf16[64,4608]{1,0:T(8,128)(2,1)}, bf16[64,4608]{1,0:T(8,128)(2,1)S(1)}, u32[]{:S(2)}, u32[]{:S(2)}) collective-permute-start(bf16[64,4608]{1,0:T(8,128)(2,1)} %collective-permute-done.11.refs_2_), channel_id=1, source_target_pairs={{0,1},{1,2},{2,3},{3,4},{4,5},{5,6},{6,7},{7,0},{8,9},{9,10},{10,1... | collective-permute-start | bytes 1769480 | tf_op jit(solution)/shard_map/ppermute | solution.py:267
  108.5 30.7 %collective-permute-start.15 = (bf16[64,4608]{1,0:T(8,128)(2,1)}, bf16[64,4608]{1,0:T(8,128)(2,1)S(1)}, u32[]{:S(2)}, u32[]{:S(2)}) collective-permute-start(bf16[64,4608]{1,0:T(8,128)(2,1)} %collective-permute-done.12.refs_3_), channel_id=1, source_target_pairs={{0,7},{1,0},{2,1},{3,2},{4,3},{5,4},{6,5},{7,6},{8,15},{9,8},{10,9... | collective-permute-start | bytes 1769480 | tf_op jit(solution)/shard_map/ppermute | solution.py:267
  113.9 26.1 %all-to-all-start.5 = ((f32[16,8,1152]{2,1,0:T(8,128)}), f32[16,8,1152]{2,1,0:T(8,128)S(1)}, u32[]{:S(2)}, u32[]{:S(2)}) async-start(f32[16,8,1152]{2,1,0:T(8,128)} %shard_map.98), calls=%async_computation.5 | async-start | bytes 1179648 | tf_op jit(solution)/shard_map/all_to_all | solution.py:276
  140.0 3.1 %collective-permute-start.17 = (f32[16,8,1152]{2,1,0:T(8,128)S(1)}, f32[16,8,1152]{2,1,0:T(8,128)S(1)}, u32[]{:S(2)}, u32[]{:S(2)}) collective-permute-start(f32[16,8,1152]{2,1,0:T(8,128)S(1)} %all-to-all-done.5), channel_id=1, source_target_pairs={{0,8},{8,0},{1,9},{9,1},{2,10},{10,2},{3,11},{11,3},{4,12},{12,4},... | collective-permute-start | bytes 1769480 | tf_op jit(solution)/shard_map/ppermute | solution.py:267
  (13 other events, 130.2 us)

commit v5 on v4

--- a/solution.py
+++ b/solution.py
@@ -72,11 +72,13 @@
     return call(kernel, operands, specs, out_shapes, [whole(s.shape) for s in out_shapes], **kwargs)
 
 
-def rows_kernel(q_ref, g_ref, y_ref, ga_ref, gb_ref, acc_ref):
-    rows = g_ref[...]
-    ga_ref[...] = rows[:64]
-    gb_ref[...] = rows[64:]
-    accumulate(acc_ref, fold3(dot(split3(q_ref[...]), rows, 1, 1)))
+def halves_kernel(g_ref, ga_ref, gb_ref):
+    ga_ref[...] = g_ref[:64]
+    gb_ref[...] = g_ref[64:]
+
+
+def rows_kernel(q_ref, g_ref, y_ref, acc_ref):
+    accumulate(acc_ref, fold3(dot(split3(q_ref[...]), g_ref[...], 1, 1)))
 
     @pl.when(pl.program_id(0) == pl.num_programs(0) - 1)
     def _():
@@ -292,18 +294,21 @@
             hbm_out=(0, 1),
         )
 
-    y, ga, gb = call(
-        rows_kernel, [q_prev_t, grad_out], [tile(K), tile(128)],
-        [out((NZ, K, 128)), out((64, D), BF16), out((64, D), BF16)],
-        [whole((NZ, K, 128)), tile(64), tile(64)], grid=(NT,),
-        scratch=[pltpu.VMEM((K, 128), F32)], hbm_in=(0, 1), hbm_out=(1, 2),
+    (y,) = call(
+        rows_kernel, [q_prev_t, grad_out], [tile(K), tile(128)], [out((NZ, K, 128))],
+        [whole((NZ, K, 128))], grid=(NT,), scratch=[pltpu.VMEM((K, 128), F32)], hbm_in=(0, 1),
+        hbm_out=(0,),
+    )
+    ga, gb = call(
+        halves_kernel, [grad_out], [tile(128)], [out((64, D), BF16)] * 2, [tile(64)] * 2,
+        grid=(NT,), hbm_in=(0,), hbm_out=(0, 1),
     )
     y = column(y)
-    (eq_t,) = simple(error_rows_kernel, [q_prev_t, error_prev], [out((K, 256))])
+    (eq_t,) = simple(error_rows_kernel, [q_prev_t, error_prev], [out((K, 256))], hbm_out=(0,))
     u1a, d1b = up(ga), down(gb)
     u1b, d1a = up(gb), down(ga)
     mine, other = simple(
-        left_kernel, [core, y, attn_out, eq_t], [out((32, 256)), out((32, 256))]
+        left_kernel, [core, y, attn_out, eq_t], [out((32, 256)), out((32, 256))], hbm_in=(2, 3)
     )
     (mine,) = simple(pair_kernel, [mine, swap(other)], [out((NXY, 32, 256))])
     mine, shadow = tied(mine, attn_out)
@@ -355,9 +360,9 @@
     mine, a_second, a_far, merged = tied(mine, a_second, a_far, merged)
     mine = plane(mine)
     merged, grad_second = near([u2a, u2b, u3a, d3b, d2a, d2b], a_second, merged, tile(256))
-    a_far, merged, u3b, far_a, far_b, d3a = tied(a_far, merged, u3b, far_a, far_b, d3a)
-    (a_far,) = simple(copy_kernel, [a_far], [out((256, 256), BF16)])
-    mine, a_far, merged, grad_second = tied(mine, a_far, merged, grad_second)
+    linv, merged, u3b, far_a, far_b, d3a = tied(linv, merged, u3b, far_a, far_b, d3a)
+    (linv,) = simple(copy_kernel, [linv], [out((K, K))])
+    mine, linv, merged, grad_second = tied(mine, linv, merged, grad_second)
     other = swap(mine)
     far = [u3b, far_a, far_b, d3a]
     error_new, q_t, grad_attn = call(

time: 153 us -> 152 us (level)
  Pallas kernels: 46.1 us -> 50.9 us
  waiting for transfers between devices: 35.2 us -> 31.7 us
    pallas_call x18 -> x19, Pallas kernels: 46.1 us -> 50.9 us  [call(): pl.pallas_call(kernel, grid=grid, in_specs=in_specs, out_specs=out_specs,...]
    ppermute x18, waiting for transfers between devices: 25.2 us -> 21 us  [shift(): return lax.ppermute(v, axis, [(i, (i + by) % size) for i in range(size)])]
    ppermute x18, starting transfers between devices: 28.9 us -> 25.8 us  [shift(): return lax.ppermute(v, axis, [(i, (i + by) % size) for i in range(size)])]
    unnamed x26 -> x28, local copies, waits for them, and re-layouts: 3.38 us -> 2.1 us
  transfers between devices with their start and end apart: 24 -> 24, of which waited for: 10 -> 10; matrix products, arithmetic and copies ran while one was open for 0% -> 0% of each run, Pallas kernels for 20% -> 24%
where the time goes in v5:
time: 152 us; the launch traced here: 151 us
  starting transfers between devices  64.9 us (43%)
  Pallas kernels  50.9 us (33%)
  waiting for transfers between devices  31.7 us (21%)
  local copies, waits for them, and re-layouts  2.1 us (1%)
    pallas_call x19, Pallas kernels, call(): pl.pallas_call(kernel, grid=grid, in_specs=in_specs, out_specs=out_specs,...  50.9 us
    ppermute x18, starting transfers between devices, shift(): return lax.ppermute(v, axis, [(i, (i + by) % size) for i in range(size)])  25.8 us
    ppermute x18, waiting for transfers between devices, shift(): return lax.ppermute(v, axis, [(i, (i + by) % size) for i in range(size)])  21 us
    all_to_all x3, starting transfers between devices, on_device(): plane = lambda v: lax.all_to_all(v, ('x', 'y'), 0, 0)  20.6 us
    all_to_all x3, starting transfers between devices, on_device(): column = lambda v: lax.all_to_all(v, 'z', 0, 0)  18.4 us
    all_to_all x3, waiting for transfers between devices, on_device(): column = lambda v: lax.all_to_all(v, 'z', 0, 0)  9.04 us
  transfers between devices with their start and end apart: 24, of which 10 were waited for; matrix products, arithmetic and copies ran while one was open for 0% of the time, Pallas kernels for 24%

profile of v5, /device:TPU:1, one launch (start us, length us, event | category | flops | bytes accessed | tf_op | source)
XLA Modules:
  0.0 150.6 jit_solution(2535283990036496878)
XLA Ops:
  0.7 4.0 %shard_map.84 = f32[8,64,128]{2,1,0:T(8,128)} custom-call(f32[64,4608]{1,0:T(8,128)} %bitcast.9, bf16[128,4608]{1,0:T(8,128)(2,1)} %g_ref.5), custom_call_target="tpu_custom_call" | custom-call | tf_op jit(solution)/shard_map/pallas_call | solution.py:58
  4.6 9.0 %all-to-all-start = ((f32[8,64,128]{2,1,0:T(8,128)}), f32[8,64,128]{2,1,0:T(8,128)}, u32[]{:S(2)}, u32[]{:S(2)}) async-start(f32[8,64,128]{2,1,0:T(8,128)} %shard_map.84), calls=%async_computation | async-start | bytes 524288 | tf_op jit(solution)/shard_map/all_to_all | solution.py:279
  13.6 3.4 %shard_map.89 = (bf16[64,4608]{1,0:T(8,128)(2,1)}, bf16[64,4608]{1,0:T(8,128)(2,1)}) custom-call(bf16[128,4608]{1,0:T(8,128)(2,1)} %g_ref.5), custom_call_target="tpu_custom_call" | custom-call | tf_op jit(solution)/shard_map/pallas_call | solution.py:58
  20.0 2.4 %collective-permute-start.4 = (bf16[64,4608]{1,0:T(8,128)(2,1)}, bf16[64,4608]{1,0:T(8,128)(2,1)}, u32[]{:S(2)}, u32[]{:S(2)}) collective-permute-start(bf16[64,4608]{1,0:T(8,128)(2,1)} %get-tuple-element.76), channel_id=1, source_target_pairs={{0,7},{1,0},{2,1},{3,2},{4,3},{5,4},{6,5},{7,6},{8,15},{9,8},{10,9... | collective-permute-start | bytes 1769480 | tf_op jit(solution)/shard_map/ppermute | solution.py:269
  25.5 3.3 %collective-permute-start = (f32[32,256]{1,0:T(8,128)S(1)}, f32[32,256]{1,0:T(8,128)S(1)}, u32[]{:S(2)}, u32[]{:S(2)}) collective-permute-start(f32[32,256]{1,0:T(8,128)S(1)} %get-tuple-element.72), channel_id=1, source_target_pairs={{0,8},{8,0},{1,9},{9,1},{2,10},{10,2},{3,11},{11,3},{4,12},{12,4},... | collective-permute-start | bytes 98312 | tf_op jit(solution)/shard_map/ppermute | solution.py:269
  30.5 6.8 %all-to-all-start.1 = ((f32[16,32,256]{2,1,0:T(8,128)}), f32[16,32,256]{2,1,0:T(8,128)S(1)}, u32[]{:S(2)}, u32[]{:S(2)}) async-start(f32[16,32,256]{2,1,0:T(8,128)} %shard_map.87), calls=%async_computation.1 | async-start | bytes 1048576 | tf_op jit(solution)/shard_map/all_to_all | solution.py:278
  39.6 8.9 %collective-permute-done.3.refs_2_ = bf16[64,4608]{1,0:T(8,128)(2,1)} collective-permute-done((bf16[64,4608]{1,0:T(8,128)(2,1)}, bf16[64,4608]{1,0:T(8,128)(2,1)}, u32[]{:S(2)}, u32[]{:S(2)}) %collective-permute-start.3) | collective-permute-done | bytes 589856 | tf_op jit(solution)/shard_map/ppermute | solution.py:269
  48.5 2.7 %collective-permute-start.7 = (bf16[64,4608]{1,0:T(8,128)(2,1)}, bf16[64,4608]{1,0:T(8,128)(2,1)S(1)}, u32[]{:S(2)}, u32[]{:S(2)}) collective-permute-start(bf16[64,4608]{1,0:T(8,128)(2,1)} %collective-permute-done.2.refs_4_), channel_id=1, source_target_pairs={{0,7},{1,0},{2,1},{3,2},{4,3},{5,4},{6,5},{7,6},{8,15},{9,8},{10,9... | collective-permute-start | bytes 1769480 | tf_op jit(solution)/shard_map/ppermute | solution.py:269
  54.6 4.4 %all-to-all-start.2 = ((f32[8,96,128]{2,1,0:T(8,128)}), f32[8,96,128]{2,1,0:T(8,128)S(1)}, u32[]{:S(2)}, u32[]{:S(2)}) async-start(f32[8,96,128]{2,1,0:T(8,128)} %get-tuple-element.85), calls=%async_computation.2 | async-start | bytes 786432 | tf_op jit(solution)/shard_map/all_to_all | solution.py:279
  59.0 8.1 %shard_map.92 = (f32[256,4608]{1,0:T(8,128)}, bf16[384,256]{1,0:T(8,128)(2,1)}) custom-call(bf16[128,4608]{1,0:T(8,128)(2,1)} %g_ref.5, bf16[64,4608]{1,0:T(8,128)(2,1)} %collective-permute-done.1.refs_1_, bf16[64,4608]{1,0:T(8,128)(2,1)} %collective-permute-done.3.refs_2_, bf16[64,4608]{1,0:T(8,128)(2,1)} %collective-permute-done.4.refs_3_, ...), custom_call_target="tpu_custom_call" | custom-call | tf_op jit(solution)/shard_map/pallas_call | solution.py:58
  68.7 5.1 %all-to-all-done.2.got_ref = f32[8,96,128]{2,1,0:T(8,128)S(1)} async-done(((f32[8,96,128]{2,1,0:T(8,128)}), f32[8,96,128]{2,1,0:T(8,128)S(1)}, u32[]{:S(2)}, u32[]{:S(2)}) %all-to-all-start.2) | async-done | bytes 393248 | tf_op jit(solution)/shard_map/all_to_all | solution.py:279
  73.8 2.9 %shard_map.94 = (f32[4,4,8,1152]{3,2,1,0:T(8,128)S(1)}, f32[4,4,8,1152]{3,2,1,0:T(8,128)S(1)}, f32[64,64]{1,0:T(8,128)S(1)}) custom-call(s32[1]{0:T(128)} %bitcast.1.core_ref, f32[8,96,128]{2,1,0:T(8,128)S(1)} %all-to-all-done.2.got_ref, f32[64,4608]{1,0:T(8,128)S(1)} %shard_map.93.ep_ref, bf16[128,4608]{1,0:T(8,128)(2,1)} %g_ref.5), custom_call_target="tpu_custom_call" | custom-call | tf_op jit(solution)/shard_map/pallas_call | solution.py:58
  80.4 6.8 %all-to-all-start.3 = ((f32[16,8,1152]{2,1,0:T(8,128)}), f32[16,8,1152]{2,1,0:T(8,128)S(1)}, u32[]{:S(2)}, u32[]{:S(2)}) async-start(f32[16,8,1152]{2,1,0:T(8,128)} %shard_map.95), calls=%async_computation.3 | async-start | bytes 1179648 | tf_op jit(solution)/shard_map/all_to_all | solution.py:278
  87.9 1.9 %collective-permute-start.11 = (bf16[64,4608]{1,0:T(8,128)(2,1)S(1)}, bf16[64,4608]{1,0:T(8,128)(2,1)}, u32[]{:S(2)}, u32[]{:S(2)}) collective-permute-start(bf16[64,4608]{1,0:T(8,128)(2,1)S(1)} %collective-permute-done.6.refs_0_), channel_id=1, source_target_pairs={{0,1},{1,2},{2,3},{3,4},{4,5},{5,6},{6,7},{7,0},{8,9},{9,10},{10,1... | collective-permute-start | bytes 1769480 | tf_op jit(solution)/shard_map/ppermute | solution.py:269
  90.8 5.6 %shard_map.97 = (f32[64,64]{1,0:T(8,128)S(1)}, f32[64,256]{1,0:T(8,128)}) custom-call(f32[64,128]{1,0:T(8,128)S(1)} %shard_map.96.both_ref, f32[64,256]{1,0:T(8,128)S(1)} %get-tuple-element.104.p_ref), custom_call_target="tpu_custom_call" | custom-call | tf_op jit(solution)/shard_map/pallas_call | solution.py:58
  96.4 1.7 %all-to-all-done.3.in_ref = f32[16,8,1152]{2,1,0:T(8,128)S(1)} async-done(((f32[16,8,1152]{2,1,0:T(8,128)}), f32[16,8,1152]{2,1,0:T(8,128)S(1)}, u32[]{:S(2)}, u32[]{:S(2)}) %all-to-all-start.3) | async-done | bytes 589856 | tf_op jit(solution)/shard_map/all_to_all | solution.py:278
  98.8 5.0 %all-to-all-start.4 = ((f32[8,8,1152]{2,1,0:T(8,128)}), f32[8,8,1152]{2,1,0:T(8,128)S(1)}, u32[]{:S(2)}, u32[]{:S(2)}) async-start(f32[8,8,1152]{2,1,0:T(8,128)} %shard_map.98), calls=%async_computation.4 | async-start | bytes 589824 | tf_op jit(solution)/shard_map/all_to_all | solution.py:279
  107.5 2.7 %collective-permute-start.15 = (bf16[64,4608]{1,0:T(8,128)(2,1)}, bf16[64,4608]{1,0:T(8,128)(2,1)S(1)}, u32[]{:S(2)}, u32[]{:S(2)}) collective-permute-start(bf16[64,4608]{1,0:T(8,128)(2,1)} %collective-permute-done.12.refs_3_), channel_id=1, source_target_pairs={{0,7},{1,0},{2,1},{3,2},{4,3},{5,4},{6,5},{7,6},{8,15},{9,8},{10,9... | collective-permute-start | bytes 1769480 | tf_op jit(solution)/shard_map/ppermute | solution.py:269
  110.1 3.8 %all-to-all-done.4.in_ref = f32[8,8,1152]{2,1,0:T(8,128)S(1)} async-done(((f32[8,8,1152]{2,1,0:T(8,128)}), f32[8,8,1152]{2,1,0:T(8,128)S(1)}, u32[]{:S(2)}, u32[]{:S(2)}) %all-to-all-start.4) | async-done | bytes 294944 | tf_op jit(solution)/shard_map/all_to_all | solution.py:279
  114.8 7.1 %all-to-all-start.5 = ((f32[16,8,1152]{2,1,0:T(8,128)}), f32[16,8,1152]{2,1,0:T(8,128)S(1)}, u32[]{:S(2)}, u32[]{:S(2)}) async-start(f32[16,8,1152]{2,1,0:T(8,128)} %shard_map.99), calls=%async_computation.5 | async-start | bytes 1179648 | tf_op jit(solution)/shard_map/all_to_all | solution.py:278
  121.9 8.4 %shard_map.100 = (f32[256,4608]{1,0:T(8,128)}, bf16[384,256]{1,0:T(8,128)(2,1)}) custom-call(bf16[64,4608]{1,0:T(8,128)(2,1)} %copy-done.12, bf16[64,4608]{1,0:T(8,128)(2,1)} %collective-permute-done.9.refs_1_, bf16[64,4608]{1,0:T(8,128)(2,1)} %collective-permute-done.11.refs_2_, bf16[64,4608]{1,0:T(8,128)(2,1)} %collective-permute-done.12.refs_3_, ...), custom_call_target="tpu_custom_call" | custom-call | tf_op jit(solution)/shard_map/pallas_call | solution.py:58
  130.4 7.8 %collective-permute-done.14.refs_1_ = bf16[64,4608]{1,0:T(8,128)(2,1)S(1)} collective-permute-done((bf16[64,4608]{1,0:T(8,128)(2,1)}, bf16[64,4608]{1,0:T(8,128)(2,1)S(1)}, u32[]{:S(2)}, u32[]{:S(2)}) %collective-permute-start.14) | collective-permute-done | bytes 589856 | tf_op jit(solution)/shard_map/ppermute | solution.py:269
  138.2 2.0 %collective-permute-start.17 = (f32[16,8,1152]{2,1,0:T(8,128)S(1)}, f32[16,8,1152]{2,1,0:T(8,128)S(1)}, u32[]{:S(2)}, u32[]{:S(2)}) collective-permute-start(f32[16,8,1152]{2,1,0:T(8,128)S(1)} %all-to-all-done.5), channel_id=1, source_target_pairs={{0,8},{8,0},{1,9},{9,1},{2,10},{10,2},{3,11},{11,3},{4,12},{12,4},... | collective-permute-start | bytes 1769480 | tf_op jit(solution)/shard_map/ppermute | solution.py:269
  141.9 8.5 %shard_map.102 = (bf16[1,256,4608]{2,1,0:T(8,128)(2,1)}, f32[64,4608]{1,0:T(8,128)}, bf16[1024,256]{1,0:T(8,128)(2,1)}) custom-call(s32[1]{0:T(128)} %bitcast.z_ref, s32[1]{0:T(128)} %bitcast.1.core_ref, bf16[64,4608]{1,0:T(8,128)(2,1)} %copy-done.8, bf16[64,4608]{1,0:T(8,128)(2,1)} %copy-done.10, bf16[64,4608]{1,0:T(8,128)(2,1)} %copy-done.11, ...), custom_call_target="tpu_custom_call" | custom-call | tf_op jit(solution)/shard_map/pallas_call | solution.py:58
  (71 shorter events, 27.4 us)
Async XLA Ops:
  4.6 19.5 %all-to-all-start = ((f32[8,64,128]{2,1,0:T(8,128)}), f32[8,64,128]{2,1,0:T(8,128)}, u32[]{:S(2)}, u32[]{:S(2)}) async-start(f32[8,64,128]{2,1,0:T(8,128)} %shard_map.84), calls=%async_computation | async-start | bytes 524288 | tf_op jit(solution)/shard_map/all_to_all | solution.py:279
  17.1 22.6 %collective-permute-start.1 = (bf16[64,4608]{1,0:T(8,128)(2,1)}, bf16[64,4608]{1,0:T(8,128)(2,1)}, u32[]{:S(2)}, u32[]{:S(2)}) collective-permute-start(bf16[64,4608]{1,0:T(8,128)(2,1)} %get-tuple-element.76), channel_id=1, source_target_pairs={{0,1},{1,2},{2,3},{3,4},{4,5},{5,6},{6,7},{7,0},{8,9},{9,10},{10,1... | collective-permute-start | bytes 1769480 | tf_op jit(solution)/shard_map/ppermute | solution.py:269
  18.5 21.1 %collective-permute-start.2 = (bf16[64,4608]{1,0:T(8,128)(2,1)}, bf16[64,4608]{1,0:T(8,128)(2,1)}, u32[]{:S(2)}, u32[]{:S(2)}) collective-permute-start(bf16[64,4608]{1,0:T(8,128)(2,1)} %get-tuple-element.77), channel_id=1, source_target_pairs={{0,7},{1,0},{2,1},{3,2},{4,3},{5,4},{6,5},{7,6},{8,15},{9,8},{10,9... | collective-permute-start | bytes 1769480 | tf_op jit(solution)/shard_map/ppermute | solution.py:269
  19.7 28.8 %collective-permute-start.3 = (bf16[64,4608]{1,0:T(8,128)(2,1)}, bf16[64,4608]{1,0:T(8,128)(2,1)}, u32[]{:S(2)}, u32[]{:S(2)}) collective-permute-start(bf16[64,4608]{1,0:T(8,128)(2,1)} %get-tuple-element.77), channel_id=1, source_target_pairs={{0,1},{1,2},{2,3},{3,4},{4,5},{5,6},{6,7},{7,0},{8,9},{9,10},{10,1... | collective-permute-start | bytes 1769480 | tf_op jit(solution)/shard_map/ppermute | solution.py:269
  20.0 28.5 %collective-permute-start.4 = (bf16[64,4608]{1,0:T(8,128)(2,1)}, bf16[64,4608]{1,0:T(8,128)(2,1)}, u32[]{:S(2)}, u32[]{:S(2)}) collective-permute-start(bf16[64,4608]{1,0:T(8,128)(2,1)} %get-tuple-element.76), channel_id=1, source_target_pairs={{0,7},{1,0},{2,1},{3,2},{4,3},{5,4},{6,5},{7,6},{8,15},{9,8},{10,9... | collective-permute-start | bytes 1769480 | tf_op jit(solution)/shard_map/ppermute | solution.py:269
  25.5 4.1 %collective-permute-start = (f32[32,256]{1,0:T(8,128)S(1)}, f32[32,256]{1,0:T(8,128)S(1)}, u32[]{:S(2)}, u32[]{:S(2)}) collective-permute-start(f32[32,256]{1,0:T(8,128)S(1)} %get-tuple-element.72), channel_id=1, source_target_pairs={{0,8},{8,0},{1,9},{9,1},{2,10},{10,2},{3,11},{11,3},{4,12},{12,4},... | collective-permute-start | bytes 98312 | tf_op jit(solution)/shard_map/ppermute | solution.py:269
  30.5 20.6 %all-to-all-start.1 = ((f32[16,32,256]{2,1,0:T(8,128)}), f32[16,32,256]{2,1,0:T(8,128)S(1)}, u32[]{:S(2)}, u32[]{:S(2)}) async-start(f32[16,32,256]{2,1,0:T(8,128)} %shard_map.87), calls=%async_computation.1 | async-start | bytes 1048576 | tf_op jit(solution)/shard_map/all_to_all | solution.py:278
  48.5 18.6 %collective-permute-start.6 = (bf16[64,4608]{1,0:T(8,128)(2,1)}, bf16[64,4608]{1,0:T(8,128)(2,1)S(1)}, u32[]{:S(2)}, u32[]{:S(2)}) collective-permute-start(bf16[64,4608]{1,0:T(8,128)(2,1)} %collective-permute-done.1.refs_1_), channel_id=1, source_target_pairs={{0,1},{1,2},{2,3},{3,4},{4,5},{5,6},{6,7},{7,0},{8,9},{9,10},{10,1... | collective-permute-start | bytes 1769480 | tf_op jit(solution)/shard_map/ppermute | solution.py:269
  48.5 18.6 %collective-permute-start.7 = (bf16[64,4608]{1,0:T(8,128)(2,1)}, bf16[64,4608]{1,0:T(8,128)(2,1)S(1)}, u32[]{:S(2)}, u32[]{:S(2)}) collective-permute-start(bf16[64,4608]{1,0:T(8,128)(2,1)} %collective-permute-done.2.refs_4_), channel_id=1, source_target_pairs={{0,7},{1,0},{2,1},{3,2},{4,3},{5,4},{6,5},{7,6},{8,15},{9,8},{10,9... | collective-permute-start | bytes 1769480 | tf_op jit(solution)/shard_map/ppermute | solution.py:269
  51.2 2.2 %collective-permute-start.5 = (f32[32,256]{1,0:T(8,128)S(1)}, f32[32,256]{1,0:T(8,128)S(1)}, u32[]{:S(2)}, u32[]{:S(2)}) collective-permute-start(f32[32,256]{1,0:T(8,128)S(1)} %shard_map.90.mine_ref), channel_id=1, source_target_pairs={{0,8},{8,0},{1,9},{9,1},{2,10},{10,2},{3,11},{11,3},{4,12},{12,4},... | collective-permute-start | bytes 98312 | tf_op jit(solution)/shard_map/ppermute | solution.py:269
  54.6 19.2 %all-to-all-start.2 = ((f32[8,96,128]{2,1,0:T(8,128)}), f32[8,96,128]{2,1,0:T(8,128)S(1)}, u32[]{:S(2)}, u32[]{:S(2)}) async-start(f32[8,96,128]{2,1,0:T(8,128)} %get-tuple-element.85), calls=%async_computation.2 | async-start | bytes 786432 | tf_op jit(solution)/shard_map/all_to_all | solution.py:279
  76.7 2.8 %collective-permute-start.8 = (f32[4,4,8,1152]{3,2,1,0:T(8,128)S(1)}, f32[4,4,8,1152]{3,2,1,0:T(8,128)S(1)}, u32[]{:S(2)}, u32[]{:S(2)}) collective-permute-start(f32[4,4,8,1152]{3,2,1,0:T(8,128)S(1)} %get-tuple-element.97), channel_id=1, source_target_pairs={{0,8},{8,0},{1,9},{9,1},{2,10},{10,2},{3,11},{11,3},{4,12},{12,4},... | collective-permute-start | bytes 1769480 | tf_op jit(solution)/shard_map/ppermute | solution.py:269
  77.5 21.3 %collective-permute-start.10 = (bf16[64,4608]{1,0:T(8,128)(2,1)}, bf16[64,4608]{1,0:T(8,128)(2,1)}, u32[]{:S(2)}, u32[]{:S(2)}) collective-permute-start(bf16[64,4608]{1,0:T(8,128)(2,1)} %collective-permute-done.4.refs_3_), channel_id=1, source_target_pairs={{0,7},{1,0},{2,1},{3,2},{4,3},{5,4},{6,5},{7,6},{8,15},{9,8},{10,9... | collective-permute-start | bytes 1769480 | tf_op jit(solution)/shard_map/ppermute | solution.py:269
  78.7 20.1 %collective-permute-start.9 = (bf16[64,4608]{1,0:T(8,128)(2,1)}, bf16[64,4608]{1,0:T(8,128)(2,1)}, u32[]{:S(2)}, u32[]{:S(2)}) collective-permute-start(bf16[64,4608]{1,0:T(8,128)(2,1)} %collective-permute-done.3.refs_2_), channel_id=1, source_target_pairs={{0,1},{1,2},{2,3},{3,4},{4,5},{5,6},{6,7},{7,0},{8,9},{9,10},{10,1... | collective-permute-start | bytes 1769480 | tf_op jit(solution)/shard_map/ppermute | solution.py:269
  80.4 17.7 %all-to-all-start.3 = ((f32[16,8,1152]{2,1,0:T(8,128)}), f32[16,8,1152]{2,1,0:T(8,128)S(1)}, u32[]{:S(2)}, u32[]{:S(2)}) async-start(f32[16,8,1152]{2,1,0:T(8,128)} %shard_map.95), calls=%async_computation.3 | async-start | bytes 1179648 | tf_op jit(solution)/shard_map/all_to_all | solution.py:278
  87.9 19.5 %collective-permute-start.11 = (bf16[64,4608]{1,0:T(8,128)(2,1)S(1)}, bf16[64,4608]{1,0:T(8,128)(2,1)}, u32[]{:S(2)}, u32[]{:S(2)}) collective-permute-start(bf16[64,4608]{1,0:T(8,128)(2,1)S(1)} %collective-permute-done.6.refs_0_), channel_id=1, source_target_pairs={{0,1},{1,2},{2,3},{3,4},{4,5},{5,6},{6,7},{7,0},{8,9},{9,10},{10,1... | collective-permute-start | bytes 1769480 | tf_op jit(solution)/shard_map/ppermute | solution.py:269
  89.8 17.7 %collective-permute-start.12 = (bf16[64,4608]{1,0:T(8,128)(2,1)S(1)}, bf16[64,4608]{1,0:T(8,128)(2,1)}, u32[]{:S(2)}, u32[]{:S(2)}) collective-permute-start(bf16[64,4608]{1,0:T(8,128)(2,1)S(1)} %collective-permute-done.7.refs_5_), channel_id=1, source_target_pairs={{0,7},{1,0},{2,1},{3,2},{4,3},{5,4},{6,5},{7,6},{8,15},{9,8},{10,9... | collective-permute-start | bytes 1769480 | tf_op jit(solution)/shard_map/ppermute | solution.py:269
  98.8 15.1 %all-to-all-start.4 = ((f32[8,8,1152]{2,1,0:T(8,128)}), f32[8,8,1152]{2,1,0:T(8,128)S(1)}, u32[]{:S(2)}, u32[]{:S(2)}) async-start(f32[8,8,1152]{2,1,0:T(8,128)} %shard_map.98), calls=%async_computation.4 | async-start | bytes 589824 | tf_op jit(solution)/shard_map/all_to_all | solution.py:279
  103.8 26.5 %collective-permute-start.13 = (bf16[64,4608]{1,0:T(8,128)(2,1)}, bf16[64,4608]{1,0:T(8,128)(2,1)S(1)}, u32[]{:S(2)}, u32[]{:S(2)}) collective-permute-start(bf16[64,4608]{1,0:T(8,128)(2,1)} %collective-permute-done.9.refs_1_), channel_id=1, source_target_pairs={{0,1},{1,2},{2,3},{3,4},{4,5},{5,6},{6,7},{7,0},{8,9},{9,10},{10,1... | collective-permute-start | bytes 1769480 | tf_op jit(solution)/shard_map/ppermute | solution.py:269
  105.3 25.1 %collective-permute-start.16 = (bf16[64,4608]{1,0:T(8,128)(2,1)}, bf16[64,4608]{1,0:T(8,128)(2,1)S(1)}, u32[]{:S(2)}, u32[]{:S(2)}) collective-permute-start(bf16[64,4608]{1,0:T(8,128)(2,1)} %collective-permute-done.10.refs_4_), channel_id=1, source_target_pairs={{0,7},{1,0},{2,1},{3,2},{4,3},{5,4},{6,5},{7,6},{8,15},{9,8},{10,9... | collective-permute-start | bytes 1769480 | tf_op jit(solution)/shard_map/ppermute | solution.py:269
  107.4 30.7 %collective-permute-start.14 = (bf16[64,4608]{1,0:T(8,128)(2,1)}, bf16[64,4608]{1,0:T(8,128)(2,1)S(1)}, u32[]{:S(2)}, u32[]{:S(2)}) collective-permute-start(bf16[64,4608]{1,0:T(8,128)(2,1)} %collective-permute-done.11.refs_2_), channel_id=1, source_target_pairs={{0,1},{1,2},{2,3},{3,4},{4,5},{5,6},{6,7},{7,0},{8,9},{9,10},{10,1... | collective-permute-start | bytes 1769480 | tf_op jit(solution)/shard_map/ppermute | solution.py:269
  107.5 30.7 %collective-permute-start.15 = (bf16[64,4608]{1,0:T(8,128)(2,1)}, bf16[64,4608]{1,0:T(8,128)(2,1)S(1)}, u32[]{:S(2)}, u32[]{:S(2)}) collective-permute-start(bf16[64,4608]{1,0:T(8,128)(2,1)} %collective-permute-done.12.refs_3_), channel_id=1, source_target_pairs={{0,7},{1,0},{2,1},{3,2},{4,3},{5,4},{6,5},{7,6},{8,15},{9,8},{10,9... | collective-permute-start | bytes 1769480 | tf_op jit(solution)/shard_map/ppermute | solution.py:269
  114.8 23.4 %all-to-all-start.5 = ((f32[16,8,1152]{2,1,0:T(8,128)}), f32[16,8,1152]{2,1,0:T(8,128)S(1)}, u32[]{:S(2)}, u32[]{:S(2)}) async-start(f32[16,8,1152]{2,1,0:T(8,128)} %shard_map.99), calls=%async_computation.5 | async-start | bytes 1179648 | tf_op jit(solution)/shard_map/all_to_all | solution.py:278
  138.2 3.7 %collective-permute-start.17 = (f32[16,8,1152]{2,1,0:T(8,128)S(1)}, f32[16,8,1152]{2,1,0:T(8,128)S(1)}, u32[]{:S(2)}, u32[]{:S(2)}) collective-permute-start(f32[16,8,1152]{2,1,0:T(8,128)S(1)} %all-to-all-done.5), channel_id=1, source_target_pairs={{0,8},{8,0},{1,9},{9,1},{2,10},{10,2},{3,11},{11,3},{4,12},{12,4},... | collective-permute-start | bytes 1769480 | tf_op jit(solution)/shard_map/ppermute | solution.py:269
  (14 other events, 161.0 us)

commit v6 on v5

--- a/solution.py
+++ b/solution.py
@@ -317,9 +317,8 @@
         turn_kernel, [z, shadow],
         [out((256, 384), BF16), out((256, 384), BF16), out((256, 256), BF16)],
     )
-    a_first, u1a, d1b, u1b, d1a = tied(a_first, u1a, d1b, u1b, d1a)
+    a_first, u1a, d1b = tied(a_first, u1a, d1b)
     u2a, d2b = up(u1a), down(d1b)
-    u2b, d2a = up(u1b), down(d1a)
     mine, a_first, a_second, a_far = tied(mine, a_first, a_second, a_far)
     (mine,) = simple(total_kernel, [mine], [out((32, 256))])
 
@@ -329,7 +328,8 @@
     sent, p_t, a_first = tied(sent, p_t, a_first)
     got = column(sent)
     merged, grad_first = near([grad_out, u1a, u1b, d1a, d1b], a_first, error_prev, err_tile)
-    p_then, u2a, d2b = tied(p_t, u2a, d2b)
+    p_then, u2a, d2b, u1b, d1a = tied(p_t, u2a, d2b, u1b, d1a)
+    u2b, d2a = up(u1b), down(d1a)
     (ep,) = call(
         error_terms_kernel, [p_then, error_prev], [whole((K, 256)), err_tile], [out((K, D))],
         [tile(K)], grid=(NT,), flops=3 * 10**9,

time: 152 us -> 154 us (1.013)
  local copies, waits for them, and re-layouts: 2.1 us -> 4.52 us
    ppermute x18, waiting for transfers between devices: 21 us -> 15.4 us  [shift(): return lax.ppermute(v, axis, [(i, (i + by) % size) for i in range(size)])]
    all_to_all x3, waiting for transfers between devices: 1.68 us -> 4.32 us  [on_device(): plane = lambda v: lax.all_to_all(v, ('x', 'y'), 0, 0)]
    all_to_all x3, waiting for transfers between devices: 9.04 us -> 11.6 us  [on_device(): column = lambda v: lax.all_to_all(v, 'z', 0, 0)]
    unnamed x28 -> x36, local copies, waits for them, and re-layouts: 2.1 us -> 4.52 us
    ppermute x18, starting transfers between devices: 25.8 us -> 27.7 us  [shift(): return lax.ppermute(v, axis, [(i, (i + by) % size) for i in range(size)])]
  transfers between devices with their start and end apart: 24 -> 24, of which waited for: 10 -> 11; matrix products, arithmetic and copies ran while one was open for 0% -> 0% of each run, Pallas kernels for 24% -> 23%
where the time goes in v6:
time: 154 us; the launch traced here: 153 us
  starting transfers between devices  64.9 us (42%)
  Pallas kernels  50.7 us (33%)
  waiting for transfers between devices  31.4 us (20%)
  local copies, waits for them, and re-layouts  4.52 us (3%)
    pallas_call x19, Pallas kernels, call(): pl.pallas_call(kernel, grid=grid, in_specs=in_specs, out_specs=out_specs,...  50.7 us
    ppermute x18, starting transfers between devices, shift(): return lax.ppermute(v, axis, [(i, (i + by) % size) for i in range(size)])  27.7 us
    all_to_all x3, starting transfers between devices, on_device(): plane = lambda v: lax.all_to_all(v, ('x', 'y'), 0, 0)  19.1 us
    all_to_all x3, starting transfers between devices, on_device(): column = lambda v: lax.all_to_all(v, 'z', 0, 0)  18.1 us
    ppermute x18, waiting for transfers between devices, shift(): return lax.ppermute(v, axis, [(i, (i + by) % size) for i in range(size)])  15.4 us
    all_to_all x3, waiting for transfers between devices, on_device(): column = lambda v: lax.all_to_all(v, 'z', 0, 0)  11.6 us
    unnamed x36, local copies, waits for them, and re-layouts  4.52 us
    all_to_all x3, waiting for transfers between devices, on_device(): plane = lambda v: lax.all_to_all(v, ('x', 'y'), 0, 0)  4.32 us
  transfers between devices with their start and end apart: 24, of which 11 were waited for; matrix products, arithmetic and copies ran while one was open for 0% of the time, Pallas kernels for 23%

profile of v6, /device:TPU:1, one launch (start us, length us, event | category | flops | bytes accessed | tf_op | source)
XLA Modules:
  0.0 152.6 jit_solution(16298127163944909760)
XLA Ops:
  0.7 4.0 %shard_map.84 = f32[8,64,128]{2,1,0:T(8,128)} custom-call(f32[64,4608]{1,0:T(8,128)} %bitcast.9, bf16[128,4608]{1,0:T(8,128)(2,1)} %g_ref.5), custom_call_target="tpu_custom_call" | custom-call | tf_op jit(solution)/shard_map/pallas_call | solution.py:58
  4.6 9.0 %all-to-all-start = ((f32[8,64,128]{2,1,0:T(8,128)}), f32[8,64,128]{2,1,0:T(8,128)}, u32[]{:S(2)}, u32[]{:S(2)}) async-start(f32[8,64,128]{2,1,0:T(8,128)} %shard_map.84), calls=%async_computation | async-start | bytes 524288 | tf_op jit(solution)/shard_map/all_to_all | solution.py:279
  13.6 3.4 %shard_map.89 = (bf16[64,4608]{1,0:T(8,128)(2,1)}, bf16[64,4608]{1,0:T(8,128)(2,1)}) custom-call(bf16[128,4608]{1,0:T(8,128)(2,1)} %g_ref.5), custom_call_target="tpu_custom_call" | custom-call | tf_op jit(solution)/shard_map/pallas_call | solution.py:58
  21.3 2.8 %all-to-all-done.y_ref = f32[8,64,128]{2,1,0:T(8,128)} async-done(((f32[8,64,128]{2,1,0:T(8,128)}), f32[8,64,128]{2,1,0:T(8,128)}, u32[]{:S(2)}, u32[]{:S(2)}) %all-to-all-start) | async-done | bytes 262176 | tf_op jit(solution)/shard_map/all_to_all | solution.py:279
  25.5 3.3 %collective-permute-start = (f32[32,256]{1,0:T(8,128)S(1)}, f32[32,256]{1,0:T(8,128)S(1)}, u32[]{:S(2)}, u32[]{:S(2)}) collective-permute-start(f32[32,256]{1,0:T(8,128)S(1)} %get-tuple-element.72), channel_id=1, source_target_pairs={{0,8},{8,0},{1,9},{9,1},{2,10},{10,2},{3,11},{11,3},{4,12},{12,4},... | collective-permute-start | bytes 98312 | tf_op jit(solution)/shard_map/ppermute | solution.py:269
  30.5 6.8 %all-to-all-start.1 = ((f32[16,32,256]{2,1,0:T(8,128)}), f32[16,32,256]{2,1,0:T(8,128)S(1)}, u32[]{:S(2)}, u32[]{:S(2)}) async-start(f32[16,32,256]{2,1,0:T(8,128)} %shard_map.87), calls=%async_computation.1 | async-start | bytes 1048576 | tf_op jit(solution)/shard_map/all_to_all | solution.py:278
  37.4 2.7 %collective-permute-start.5 = (bf16[64,4608]{1,0:T(8,128)(2,1)}, bf16[64,4608]{1,0:T(8,128)(2,1)S(1)}, u32[]{:S(2)}, u32[]{:S(2)}) collective-permute-start(bf16[64,4608]{1,0:T(8,128)(2,1)} %get-tuple-element.76), channel_id=1, source_target_pairs={{0,7},{1,0},{2,1},{3,2},{4,3},{5,4},{6,5},{7,6},{8,15},{9,8},{10,9... | collective-permute-start | bytes 1769480 | tf_op jit(solution)/shard_map/ppermute | solution.py:269
  42.4 2.7 %collective-permute-start.7 = (bf16[64,4608]{1,0:T(8,128)(2,1)}, bf16[64,4608]{1,0:T(8,128)(2,1)}, u32[]{:S(2)}, u32[]{:S(2)}) collective-permute-start(bf16[64,4608]{1,0:T(8,128)(2,1)} %collective-permute-done.2.refs_4_), channel_id=1, source_target_pairs={{0,7},{1,0},{2,1},{3,2},{4,3},{5,4},{6,5},{7,6},{8,15},{9,8},{10,9... | collective-permute-start | bytes 1769480 | tf_op jit(solution)/shard_map/ppermute | solution.py:269
  45.0 2.6 %all-to-all-done.1.in_ref = f32[16,32,256]{2,1,0:T(8,128)S(1)} async-done(((f32[16,32,256]{2,1,0:T(8,128)}), f32[16,32,256]{2,1,0:T(8,128)S(1)}, u32[]{:S(2)}, u32[]{:S(2)}) %all-to-all-start.1) | async-done | bytes 524320 | tf_op jit(solution)/shard_map/all_to_all | solution.py:278
  51.9 3.5 %all-to-all-start.2 = ((f32[8,96,128]{2,1,0:T(8,128)}), f32[8,96,128]{2,1,0:T(8,128)S(1)}, u32[]{:S(2)}, u32[]{:S(2)}) async-start(f32[8,96,128]{2,1,0:T(8,128)} %get-tuple-element.85), calls=%async_computation.2 | async-start | bytes 786432 | tf_op jit(solution)/shard_map/all_to_all | solution.py:279
  57.0 8.0 %shard_map.92 = (f32[256,4608]{1,0:T(8,128)}, bf16[384,256]{1,0:T(8,128)(2,1)}) custom-call(bf16[128,4608]{1,0:T(8,128)(2,1)} %g_ref.5, bf16[64,4608]{1,0:T(8,128)(2,1)} %collective-permute-done.1.refs_1_, bf16[64,4608]{1,0:T(8,128)(2,1)} %copy-done.8, bf16[64,4608]{1,0:T(8,128)(2,1)} %copy-done.10, bf16[64,4608]{1,0:T(8,128)(2,1)} %collective-permute-done.2.refs_4_, ...), custom_call_target="tpu_custom_call" | custom-call | tf_op jit(solution)/shard_map/pallas_call | solution.py:58
  65.0 3.0 %collective-permute-done.6.refs_0_ = bf16[64,4608]{1,0:T(8,128)(2,1)S(1)} collective-permute-done((bf16[64,4608]{1,0:T(8,128)(2,1)}, bf16[64,4608]{1,0:T(8,128)(2,1)S(1)}, u32[]{:S(2)}, u32[]{:S(2)}) %collective-permute-start.6) | collective-permute-done | bytes 589856 | tf_op jit(solution)/shard_map/ppermute | solution.py:269
  69.6 4.3 %all-to-all-done.2.got_ref = f32[8,96,128]{2,1,0:T(8,128)S(1)} async-done(((f32[8,96,128]{2,1,0:T(8,128)}), f32[8,96,128]{2,1,0:T(8,128)S(1)}, u32[]{:S(2)}, u32[]{:S(2)}) %all-to-all-start.2) | async-done | bytes 393248 | tf_op jit(solution)/shard_map/all_to_all | solution.py:279
  73.8 2.9 %shard_map.94 = (f32[4,4,8,1152]{3,2,1,0:T(8,128)S(1)}, f32[4,4,8,1152]{3,2,1,0:T(8,128)S(1)}, f32[64,64]{1,0:T(8,128)S(1)}) custom-call(s32[1]{0:T(128)} %bitcast.1.core_ref, f32[8,96,128]{2,1,0:T(8,128)S(1)} %all-to-all-done.2.got_ref, f32[64,4608]{1,0:T(8,128)S(1)} %shard_map.93.ep_ref, bf16[128,4608]{1,0:T(8,128)(2,1)} %g_ref.5), custom_call_target="tpu_custom_call" | custom-call | tf_op jit(solution)/shard_map/pallas_call | solution.py:58
  81.1 6.7 %all-to-all-start.3 = ((f32[16,8,1152]{2,1,0:T(8,128)}), f32[16,8,1152]{2,1,0:T(8,128)S(1)}, u32[]{:S(2)}, u32[]{:S(2)}) async-start(f32[16,8,1152]{2,1,0:T(8,128)} %shard_map.95), calls=%async_computation.3 | async-start | bytes 1179648 | tf_op jit(solution)/shard_map/all_to_all | solution.py:278
  91.5 5.6 %shard_map.97 = (f32[64,64]{1,0:T(8,128)S(1)}, f32[64,256]{1,0:T(8,128)}) custom-call(f32[64,128]{1,0:T(8,128)S(1)} %shard_map.96.both_ref, f32[64,256]{1,0:T(8,128)S(1)} %get-tuple-element.102.p_ref), custom_call_target="tpu_custom_call" | custom-call | tf_op jit(solution)/shard_map/pallas_call | solution.py:58
  100.3 5.7 %all-to-all-start.4 = ((f32[8,8,1152]{2,1,0:T(8,128)}), f32[8,8,1152]{2,1,0:T(8,128)S(1)}, u32[]{:S(2)}, u32[]{:S(2)}) async-start(f32[8,8,1152]{2,1,0:T(8,128)} %shard_map.98), calls=%async_computation.4 | async-start | bytes 589824 | tf_op jit(solution)/shard_map/all_to_all | solution.py:279
  108.9 2.5 %collective-permute-start.15 = (bf16[64,4608]{1,0:T(8,128)(2,1)}, bf16[64,4608]{1,0:T(8,128)(2,1)S(1)}, u32[]{:S(2)}, u32[]{:S(2)}) collective-permute-start(bf16[64,4608]{1,0:T(8,128)(2,1)} %collective-permute-done.12.refs_3_), channel_id=1, source_target_pairs={{0,7},{1,0},{2,1},{3,2},{4,3},{5,4},{6,5},{7,6},{8,15},{9,8},{10,9... | collective-permute-start | bytes 1769480 | tf_op jit(solution)/shard_map/ppermute | solution.py:269
  111.4 4.5 %all-to-all-done.4.in_ref = f32[8,8,1152]{2,1,0:T(8,128)S(1)} async-done(((f32[8,8,1152]{2,1,0:T(8,128)}), f32[8,8,1152]{2,1,0:T(8,128)S(1)}, u32[]{:S(2)}, u32[]{:S(2)}) %all-to-all-start.4) | async-done | bytes 294944 | tf_op jit(solution)/shard_map/all_to_all | solution.py:279
  116.8 5.7 %all-to-all-start.5 = ((f32[16,8,1152]{2,1,0:T(8,128)}), f32[16,8,1152]{2,1,0:T(8,128)S(1)}, u32[]{:S(2)}, u32[]{:S(2)}) async-start(f32[16,8,1152]{2,1,0:T(8,128)} %shard_map.99), calls=%async_computation.5 | async-start | bytes 1179648 | tf_op jit(solution)/shard_map/all_to_all | solution.py:278
  122.5 8.3 %shard_map.100 = (f32[256,4608]{1,0:T(8,128)}, bf16[384,256]{1,0:T(8,128)(2,1)}) custom-call(bf16[64,4608]{1,0:T(8,128)(2,1)} %copy-done.16, bf16[64,4608]{1,0:T(8,128)(2,1)} %collective-permute-done.9.refs_1_, bf16[64,4608]{1,0:T(8,128)(2,1)} %collective-permute-done.11.refs_2_, bf16[64,4608]{1,0:T(8,128)(2,1)} %collective-permute-done.12.refs_3_, ...), custom_call_target="tpu_custom_call" | custom-call | tf_op jit(solution)/shard_map/pallas_call | solution.py:58
  130.9 9.0 %collective-permute-done.14.refs_1_ = bf16[64,4608]{1,0:T(8,128)(2,1)S(1)} collective-permute-done((bf16[64,4608]{1,0:T(8,128)(2,1)}, bf16[64,4608]{1,0:T(8,128)(2,1)S(1)}, u32[]{:S(2)}, u32[]{:S(2)}) %collective-permute-start.14) | collective-permute-done | bytes 589856 | tf_op jit(solution)/shard_map/ppermute | solution.py:269
  140.0 2.2 %collective-permute-start.17 = (f32[16,8,1152]{2,1,0:T(8,128)S(1)}, f32[16,8,1152]{2,1,0:T(8,128)S(1)}, u32[]{:S(2)}, u32[]{:S(2)}) collective-permute-start(f32[16,8,1152]{2,1,0:T(8,128)S(1)} %all-to-all-done.5), channel_id=1, source_target_pairs={{0,8},{8,0},{1,9},{9,1},{2,10},{10,2},{3,11},{11,3},{4,12},{12,4},... | collective-permute-start | bytes 1769480 | tf_op jit(solution)/shard_map/ppermute | solution.py:269
  143.9 8.5 %shard_map.102 = (bf16[1,256,4608]{2,1,0:T(8,128)(2,1)}, f32[64,4608]{1,0:T(8,128)}, bf16[1024,256]{1,0:T(8,128)(2,1)}) custom-call(s32[1]{0:T(128)} %bitcast.z_ref, s32[1]{0:T(128)} %bitcast.1.core_ref, bf16[64,4608]{1,0:T(8,128)(2,1)} %copy-done.12, bf16[64,4608]{1,0:T(8,128)(2,1)} %copy-done.14, bf16[64,4608]{1,0:T(8,128)(2,1)} %copy-done.15, ...), custom_call_target="tpu_custom_call" | custom-call | tf_op jit(solution)/shard_map/pallas_call | solution.py:58
  (79 shorter events, 33.9 us)
Async XLA Ops:
  4.6 19.5 %all-to-all-start = ((f32[8,64,128]{2,1,0:T(8,128)}), f32[8,64,128]{2,1,0:T(8,128)}, u32[]{:S(2)}, u32[]{:S(2)}) async-start(f32[8,64,128]{2,1,0:T(8,128)} %shard_map.84), calls=%async_computation | async-start | bytes 524288 | tf_op jit(solution)/shard_map/all_to_all | solution.py:279
  17.1 25.3 %collective-permute-start.1 = (bf16[64,4608]{1,0:T(8,128)(2,1)}, bf16[64,4608]{1,0:T(8,128)(2,1)}, u32[]{:S(2)}, u32[]{:S(2)}) collective-permute-start(bf16[64,4608]{1,0:T(8,128)(2,1)} %get-tuple-element.76), channel_id=1, source_target_pairs={{0,1},{1,2},{2,3},{3,4},{4,5},{5,6},{6,7},{7,0},{8,9},{9,10},{10,1... | collective-permute-start | bytes 1769480 | tf_op jit(solution)/shard_map/ppermute | solution.py:269
  18.5 23.9 %collective-permute-start.2 = (bf16[64,4608]{1,0:T(8,128)(2,1)}, bf16[64,4608]{1,0:T(8,128)(2,1)}, u32[]{:S(2)}, u32[]{:S(2)}) collective-permute-start(bf16[64,4608]{1,0:T(8,128)(2,1)} %get-tuple-element.77), channel_id=1, source_target_pairs={{0,7},{1,0},{2,1},{3,2},{4,3},{5,4},{6,5},{7,6},{8,15},{9,8},{10,9... | collective-permute-start | bytes 1769480 | tf_op jit(solution)/shard_map/ppermute | solution.py:269
  25.5 4.2 %collective-permute-start = (f32[32,256]{1,0:T(8,128)S(1)}, f32[32,256]{1,0:T(8,128)S(1)}, u32[]{:S(2)}, u32[]{:S(2)}) collective-permute-start(f32[32,256]{1,0:T(8,128)S(1)} %get-tuple-element.72), channel_id=1, source_target_pairs={{0,8},{8,0},{1,9},{9,1},{2,10},{10,2},{3,11},{11,3},{4,12},{12,4},... | collective-permute-start | bytes 98312 | tf_op jit(solution)/shard_map/ppermute | solution.py:269
  30.5 17.1 %all-to-all-start.1 = ((f32[16,32,256]{2,1,0:T(8,128)}), f32[16,32,256]{2,1,0:T(8,128)S(1)}, u32[]{:S(2)}, u32[]{:S(2)}) async-start(f32[16,32,256]{2,1,0:T(8,128)} %shard_map.87), calls=%async_computation.1 | async-start | bytes 1048576 | tf_op jit(solution)/shard_map/all_to_all | solution.py:278
  37.3 18.1 %collective-permute-start.4 = (bf16[64,4608]{1,0:T(8,128)(2,1)}, bf16[64,4608]{1,0:T(8,128)(2,1)S(1)}, u32[]{:S(2)}, u32[]{:S(2)}) collective-permute-start(bf16[64,4608]{1,0:T(8,128)(2,1)} %get-tuple-element.77), channel_id=1, source_target_pairs={{0,1},{1,2},{2,3},{3,4},{4,5},{5,6},{6,7},{7,0},{8,9},{9,10},{10,1... | collective-permute-start | bytes 1769480 | tf_op jit(solution)/shard_map/ppermute | solution.py:269
  37.4 18.0 %collective-permute-start.5 = (bf16[64,4608]{1,0:T(8,128)(2,1)}, bf16[64,4608]{1,0:T(8,128)(2,1)S(1)}, u32[]{:S(2)}, u32[]{:S(2)}) collective-permute-start(bf16[64,4608]{1,0:T(8,128)(2,1)} %get-tuple-element.76), channel_id=1, source_target_pairs={{0,7},{1,0},{2,1},{3,2},{4,3},{5,4},{6,5},{7,6},{8,15},{9,8},{10,9... | collective-permute-start | bytes 1769480 | tf_op jit(solution)/shard_map/ppermute | solution.py:269
  42.4 25.6 %collective-permute-start.6 = (bf16[64,4608]{1,0:T(8,128)(2,1)}, bf16[64,4608]{1,0:T(8,128)(2,1)S(1)}, u32[]{:S(2)}, u32[]{:S(2)}) collective-permute-start(bf16[64,4608]{1,0:T(8,128)(2,1)} %collective-permute-done.1.refs_1_), channel_id=1, source_target_pairs={{0,1},{1,2},{2,3},{3,4},{4,5},{5,6},{6,7},{7,0},{8,9},{9,10},{10,1... | collective-permute-start | bytes 1769480 | tf_op jit(solution)/shard_map/ppermute | solution.py:269
  42.4 25.6 %collective-permute-start.7 = (bf16[64,4608]{1,0:T(8,128)(2,1)}, bf16[64,4608]{1,0:T(8,128)(2,1)}, u32[]{:S(2)}, u32[]{:S(2)}) collective-permute-start(bf16[64,4608]{1,0:T(8,128)(2,1)} %collective-permute-done.2.refs_4_), channel_id=1, source_target_pairs={{0,7},{1,0},{2,1},{3,2},{4,3},{5,4},{6,5},{7,6},{8,15},{9,8},{10,9... | collective-permute-start | bytes 1769480 | tf_op jit(solution)/shard_map/ppermute | solution.py:269
  47.7 3.0 %collective-permute-start.3 = (f32[32,256]{1,0:T(8,128)S(1)}, f32[32,256]{1,0:T(8,128)S(1)}, u32[]{:S(2)}, u32[]{:S(2)}) collective-permute-start(f32[32,256]{1,0:T(8,128)S(1)} %shard_map.90.mine_ref), channel_id=1, source_target_pairs={{0,8},{8,0},{1,9},{9,1},{2,10},{10,2},{3,11},{11,3},{4,12},{12,4},... | collective-permute-start | bytes 98312 | tf_op jit(solution)/shard_map/ppermute | solution.py:269
  51.9 21.9 %all-to-all-start.2 = ((f32[8,96,128]{2,1,0:T(8,128)}), f32[8,96,128]{2,1,0:T(8,128)S(1)}, u32[]{:S(2)}, u32[]{:S(2)}) async-start(f32[8,96,128]{2,1,0:T(8,128)} %get-tuple-element.85), calls=%async_computation.2 | async-start | bytes 786432 | tf_op jit(solution)/shard_map/all_to_all | solution.py:279
  76.7 3.5 %collective-permute-start.8 = (f32[4,4,8,1152]{3,2,1,0:T(8,128)S(1)}, f32[4,4,8,1152]{3,2,1,0:T(8,128)S(1)}, u32[]{:S(2)}, u32[]{:S(2)}) collective-permute-start(f32[4,4,8,1152]{3,2,1,0:T(8,128)S(1)} %get-tuple-element.95), channel_id=1, source_target_pairs={{0,8},{8,0},{1,9},{9,1},{2,10},{10,2},{3,11},{11,3},{4,12},{12,4},... | collective-permute-start | bytes 1769480 | tf_op jit(solution)/shard_map/ppermute | solution.py:269
  78.6 20.9 %collective-permute-start.10 = (bf16[64,4608]{1,0:T(8,128)(2,1)S(1)}, bf16[64,4608]{1,0:T(8,128)(2,1)S(1)}, u32[]{:S(2)}, u32[]{:S(2)}) collective-permute-start(bf16[64,4608]{1,0:T(8,128)(2,1)S(1)} %copy-done.11), channel_id=1, source_target_pairs={{0,7},{1,0},{2,1},{3,2},{4,3},{5,4},{6,5},{7,6},{8,15},{9,8},{10,9... | collective-permute-start | bytes 1769480 | tf_op jit(solution)/shard_map/ppermute | solution.py:269
  80.2 19.3 %collective-permute-start.9 = (bf16[64,4608]{1,0:T(8,128)(2,1)S(1)}, bf16[64,4608]{1,0:T(8,128)(2,1)}, u32[]{:S(2)}, u32[]{:S(2)}) collective-permute-start(bf16[64,4608]{1,0:T(8,128)(2,1)S(1)} %copy-done.9), channel_id=1, source_target_pairs={{0,1},{1,2},{2,3},{3,4},{4,5},{5,6},{6,7},{7,0},{8,9},{9,10},{10,1... | collective-permute-start | bytes 1769480 | tf_op jit(solution)/shard_map/ppermute | solution.py:269
  81.1 17.6 %all-to-all-start.3 = ((f32[16,8,1152]{2,1,0:T(8,128)}), f32[16,8,1152]{2,1,0:T(8,128)S(1)}, u32[]{:S(2)}, u32[]{:S(2)}) async-start(f32[16,8,1152]{2,1,0:T(8,128)} %shard_map.95), calls=%async_computation.3 | async-start | bytes 1179648 | tf_op jit(solution)/shard_map/all_to_all | solution.py:278
  88.5 20.2 %collective-permute-start.11 = (bf16[64,4608]{1,0:T(8,128)(2,1)S(1)}, bf16[64,4608]{1,0:T(8,128)(2,1)}, u32[]{:S(2)}, u32[]{:S(2)}) collective-permute-start(bf16[64,4608]{1,0:T(8,128)(2,1)S(1)} %collective-permute-done.6.refs_0_), channel_id=1, source_target_pairs={{0,1},{1,2},{2,3},{3,4},{4,5},{5,6},{6,7},{7,0},{8,9},{9,10},{10,1... | collective-permute-start | bytes 1769480 | tf_op jit(solution)/shard_map/ppermute | solution.py:269
  90.1 18.8 %collective-permute-start.12 = (bf16[64,4608]{1,0:T(8,128)(2,1)}, bf16[64,4608]{1,0:T(8,128)(2,1)}, u32[]{:S(2)}, u32[]{:S(2)}) collective-permute-start(bf16[64,4608]{1,0:T(8,128)(2,1)} %collective-permute-done.7.refs_5_), channel_id=1, source_target_pairs={{0,7},{1,0},{2,1},{3,2},{4,3},{5,4},{6,5},{7,6},{8,15},{9,8},{10,9... | collective-permute-start | bytes 1769480 | tf_op jit(solution)/shard_map/ppermute | solution.py:269
  100.3 15.7 %all-to-all-start.4 = ((f32[8,8,1152]{2,1,0:T(8,128)}), f32[8,8,1152]{2,1,0:T(8,128)S(1)}, u32[]{:S(2)}, u32[]{:S(2)}) async-start(f32[8,8,1152]{2,1,0:T(8,128)} %shard_map.98), calls=%async_computation.4 | async-start | bytes 589824 | tf_op jit(solution)/shard_map/all_to_all | solution.py:279
  106.0 24.9 %collective-permute-start.13 = (bf16[64,4608]{1,0:T(8,128)(2,1)}, bf16[64,4608]{1,0:T(8,128)(2,1)S(1)}, u32[]{:S(2)}, u32[]{:S(2)}) collective-permute-start(bf16[64,4608]{1,0:T(8,128)(2,1)} %collective-permute-done.9.refs_1_), channel_id=1, source_target_pairs={{0,1},{1,2},{2,3},{3,4},{4,5},{5,6},{6,7},{7,0},{8,9},{9,10},{10,1... | collective-permute-start | bytes 1769480 | tf_op jit(solution)/shard_map/ppermute | solution.py:269
  107.4 23.5 %collective-permute-start.16 = (bf16[64,4608]{1,0:T(8,128)(2,1)}, bf16[64,4608]{1,0:T(8,128)(2,1)S(1)}, u32[]{:S(2)}, u32[]{:S(2)}) collective-permute-start(bf16[64,4608]{1,0:T(8,128)(2,1)} %copy-done.17), channel_id=1, source_target_pairs={{0,7},{1,0},{2,1},{3,2},{4,3},{5,4},{6,5},{7,6},{8,15},{9,8},{10,9... | collective-permute-start | bytes 1769480 | tf_op jit(solution)/shard_map/ppermute | solution.py:269
  108.8 31.2 %collective-permute-start.14 = (bf16[64,4608]{1,0:T(8,128)(2,1)}, bf16[64,4608]{1,0:T(8,128)(2,1)S(1)}, u32[]{:S(2)}, u32[]{:S(2)}) collective-permute-start(bf16[64,4608]{1,0:T(8,128)(2,1)} %collective-permute-done.11.refs_2_), channel_id=1, source_target_pairs={{0,1},{1,2},{2,3},{3,4},{4,5},{5,6},{6,7},{7,0},{8,9},{9,10},{10,1... | collective-permute-start | bytes 1769480 | tf_op jit(solution)/shard_map/ppermute | solution.py:269
  108.9 31.0 %collective-permute-start.15 = (bf16[64,4608]{1,0:T(8,128)(2,1)}, bf16[64,4608]{1,0:T(8,128)(2,1)S(1)}, u32[]{:S(2)}, u32[]{:S(2)}) collective-permute-start(bf16[64,4608]{1,0:T(8,128)(2,1)} %collective-permute-done.12.refs_3_), channel_id=1, source_target_pairs={{0,7},{1,0},{2,1},{3,2},{4,3},{5,4},{6,5},{7,6},{8,15},{9,8},{10,9... | collective-permute-start | bytes 1769480 | tf_op jit(solution)/shard_map/ppermute | solution.py:269
  116.8 23.1 %all-to-all-start.5 = ((f32[16,8,1152]{2,1,0:T(8,128)}), f32[16,8,1152]{2,1,0:T(8,128)S(1)}, u32[]{:S(2)}, u32[]{:S(2)}) async-start(f32[16,8,1152]{2,1,0:T(8,128)} %shard_map.99), calls=%async_computation.5 | async-start | bytes 1179648 | tf_op jit(solution)/shard_map/all_to_all | solution.py:278
  140.0 3.9 %collective-permute-start.17 = (f32[16,8,1152]{2,1,0:T(8,128)S(1)}, f32[16,8,1152]{2,1,0:T(8,128)S(1)}, u32[]{:S(2)}, u32[]{:S(2)}) collective-permute-start(f32[16,8,1152]{2,1,0:T(8,128)S(1)} %all-to-all-done.5), channel_id=1, source_target_pairs={{0,8},{8,0},{1,9},{9,1},{2,10},{10,2},{3,11},{11,3},{4,12},{12,4},... | collective-permute-start | bytes 1769480 | tf_op jit(solution)/shard_map/ppermute | solution.py:269
  (18 other events, 169.4 us)
